TPU v7x, 1024 devices: a whole 8x8x8 slice. The times are simulated.
1024 devices in a mesh: dp: 32 (over z, y_hi), expert: 32 (over x, y_lo, core).
Axes of the slice: x: 8, y: 8 (y_hi: 4, y_lo: 2; y = y_hi * 2 + y_lo), z: 8, core: 2. Of those that a mesh axis runs over, the one named last changes fastest.
Arguments:
- tokens: bfloat16 [131072, 1280], P(('dp', 'expert')), may hold values from -6 to 6
- routes: int32 [131072, 1], P(('dp', 'expert')), may hold values from 0 to 15
- pool_ids: int32 [32, 4096], P('dp', 'expert'), may hold values from 0 to 7, never falling along the last dimension, each value on 1 to 1024 neighbouring positions
- w_router: bfloat16 [1280, 16], replicated, may hold values from -0.15625 to 0.15625
- w_up: bfloat16 [1280, 40960], P(None, 'expert'), may hold values from -0.15625 to 0.15625
- w_down: bfloat16 [40960, 1280], P('expert'), may hold values from -0.125 to 0.125
- captions: bfloat16 [256, 1280], P('dp'), may hold values from -6 to 6
- clip_pairs: int32 [256], replicated, may hold values from 0 to 255, each once
- teacher: float32 [256, 256], P('dp'), may hold values from -12 to 12
Outputs:
- token_grads: float32 [131072, 1280], P(('dp', 'expert'))
- caption_grads: float32 [256, 1280], P('dp')
Inputs may be any that keep to these rules, and one draw needn't show every extreme that they name: `pool_ids`: within each index of dp the clip numbers never fall along the tokens, and every clip has 1 to 1024 tokens. `clip_pairs`: each clip is named by exactly one caption.
All inputs are finite; a program needn't handle non-finite values.
Results may differ from a plain program's by a relative error of at most 0.0018.
Values may be sent and summed in bfloat16 or wider, within the bound.
No kernel may reach another device: no remote copies, remote signals or barrier semaphores. Data moves between devices by JAX's collectives and lax.ppermute only.
A program may use at most 64 MiB of HBM per device.

v0:
```python
import jax
import jax.numpy as jnp
from jax import lax
from jax.sharding import PartitionSpec as P

HIGHEST = lax.Precision.HIGHEST
logit_scale = 10.0
logit_shift = -10.0
norm_eps = 1e-06


def gelu_back(preact, upstream):
    return jax.vjp(jax.nn.gelu, preact)[1](upstream)[0]


def caption_rows(captions):
    return lax.all_gather(captions, "dp", axis=0, tiled=True)


def shards(tokens, routes, pool_ids, w_router, w_up, w_down, captions, clip_pairs, teacher):
    tok_rows = tokens.shape[0]
    width = tokens.shape[1]
    n_experts = w_router.shape[1]
    n_clips = teacher.shape[0]
    n_caps = teacher.shape[1]
    capacity = tok_rows // n_experts
    slot_count = n_experts * capacity
    route_ids = routes[:, 0]
    chosen = (route_ids[:, None] == jnp.arange(n_experts, dtype=jnp.int32)[None, :]).astype(
        jnp.float32
    )
    scores = jnp.dot(tokens, w_router, preferred_element_type=jnp.float32)
    sigmoid_gate = jax.nn.sigmoid(jnp.sum(chosen * scores, axis=1))
    gating = sigmoid_gate.astype(jnp.bfloat16)
    positions = jnp.arange(tok_rows, dtype=jnp.int32)
    earlier = (positions[:, None] > positions[None, :]).astype(jnp.float32)
    arrival = jnp.sum(jnp.dot(earlier, chosen, precision=HIGHEST) * chosen, axis=1)
    slot_index = route_ids.astype(jnp.float32) * capacity + arrival
    slot_range = jnp.arange(slot_count, dtype=jnp.float32)
    placed = ((slot_index[:, None] == slot_range[None, :]) & (arrival < capacity)[:, None]).astype(
        jnp.bfloat16
    )
    members = (pool_ids[0][:, None] == jnp.arange(n_clips, dtype=jnp.int32)[None, :]).astype(
        jnp.bfloat16
    )
    placed_t = placed.T
    slot_rows = jnp.dot(placed_t, tokens, preferred_element_type=jnp.float32).astype(jnp.bfloat16)
    slot_clips = jnp.dot(placed_t, members, preferred_element_type=jnp.float32).astype(jnp.bfloat16)
    slot_gates = jnp.dot(placed_t, gating[:, None], preferred_element_type=jnp.float32)[
        :, 0
    ].astype(jnp.bfloat16)
    send_rows = jnp.repeat(slot_rows.reshape(n_experts, capacity, width), 2, axis=0)
    send_clips = jnp.repeat(slot_clips.reshape(n_experts, capacity, n_clips), 2, axis=0)
    send_gates = jnp.repeat(slot_gates.reshape(n_experts, capacity), 2, axis=0)
    preact = jnp.einsum(
        "skd,dh->skh",
        lax.all_to_all(send_rows, "expert", split_axis=0, concat_axis=0, tiled=True),
        w_up,
        preferred_element_type=jnp.float32,
    )
    hidden = jax.nn.gelu(preact).astype(jnp.bfloat16)
    produced = jnp.einsum("skh,hd->skd", hidden, w_down, preferred_element_type=jnp.float32)
    preact, produced, recv_clips, recv_gates = (
        preact,
        produced,
        lax.all_to_all(send_clips, "expert", split_axis=0, concat_axis=0, tiled=True),
        lax.all_to_all(send_gates, "expert", split_axis=0, concat_axis=0, tiled=True),
    )
    clip_weights = recv_clips.astype(jnp.float32)
    gate_weights = recv_gates.astype(jnp.float32)
    pooled_part = jnp.dot(members.T, tokens, preferred_element_type=jnp.float32)
    pooled_part = pooled_part + jnp.einsum(
        "skc,skd->cd", clip_weights, gate_weights[..., None] * produced, precision=HIGHEST
    )
    counts_part = jnp.sum(members.astype(jnp.float32), axis=0)
    pooled, counts = lax.psum((pooled_part, counts_part), "expert")
    gathered = caption_rows(captions)
    clip_mean = pooled / counts[:, None]
    img_scale = lax.rsqrt(jnp.sum(clip_mean * clip_mean, axis=1, keepdims=True) + norm_eps)
    image_emb = clip_mean * img_scale
    text_raw = gathered.astype(jnp.float32)
    text_scale = lax.rsqrt(jnp.sum(text_raw * text_raw, axis=1, keepdims=True) + norm_eps)
    text_emb = text_raw * text_scale
    logits = logit_scale * jnp.dot(image_emb, text_emb.T, precision=HIGHEST) + logit_shift
    own_clips = lax.axis_index("dp") * n_clips + jnp.arange(n_clips, dtype=jnp.int32)
    matched = (clip_pairs[None, :] == own_clips[:, None]).astype(jnp.float32)
    target = 0.5 * matched + 0.5 * jax.nn.sigmoid(teacher)
    loss_grad = (jax.nn.sigmoid(logits) - target) * (counts[:, None] / n_caps)
    d_image = logit_scale * jnp.dot(loss_grad, text_emb, precision=HIGHEST)
    d_text = logit_scale * jnp.dot(loss_grad.T, image_emb, precision=HIGHEST)
    text_terms = (
        text_scale * d_text
        - text_scale**3 * jnp.sum(text_raw * d_text, axis=1, keepdims=True) * text_raw
    )
    caption_grads = lax.psum_scatter(text_terms, "dp", scatter_dimension=0, tiled=True)
    mean_grad = (
        img_scale * d_image
        - img_scale**3 * jnp.sum(clip_mean * d_image, axis=1, keepdims=True) * clip_mean
    )
    clip_grad = mean_grad / counts[:, None]
    unit_dy = jnp.einsum("skc,cd->skd", clip_weights, clip_grad, precision=HIGHEST)
    cotangent = (gate_weights[..., None] * unit_dy).astype(jnp.bfloat16)
    d_hidden = jnp.einsum("skd,hd->skh", cotangent, w_down, preferred_element_type=jnp.float32)
    d_preact = gelu_back(preact, d_hidden).astype(jnp.bfloat16)
    part_dx = jnp.einsum("skh,dh->skd", d_preact, w_up, preferred_element_type=jnp.float32)
    part_dg = jnp.sum(unit_dy * produced, axis=2)
    back_dx, back_dg = (
        lax.all_to_all(part_dx, "expert", split_axis=0, concat_axis=0, tiled=True),
        lax.all_to_all(part_dg, "expert", split_axis=0, concat_axis=0, tiled=True),
    )
    slot_dx = jnp.sum(back_dx.reshape(n_experts, 2, capacity, width), axis=1).reshape(
        slot_count, width
    )
    slot_dg = jnp.sum(back_dg.reshape(n_experts, 2, capacity), axis=1).reshape(slot_count)
    placed_f = placed.astype(jnp.float32)
    token_dx = jnp.dot(placed_f, slot_dx, precision=HIGHEST)
    token_dg = jnp.dot(placed_f, slot_dg[:, None], precision=HIGHEST)[:, 0]
    token_dy = jnp.dot(members.astype(jnp.float32), clip_grad, precision=HIGHEST)
    router_cols = jnp.dot(chosen, w_router.astype(jnp.float32).T, precision=HIGHEST)
    slope = token_dg * sigmoid_gate * (1.0 - sigmoid_gate)
    token_grads = token_dy + token_dx + slope[:, None] * router_cols
    return (token_grads, caption_grads)


def solution(mesh):
    return jax.shard_map(
        shards,
        mesh=mesh,
        in_specs=(
            P(("dp", "expert"), None),
            P(("dp", "expert"), None),
            P("dp", "expert"),
            P(),
            P(None, "expert"),
            P("expert", None),
            P("dp", None),
            P(),
            P("dp", None),
        ),
        out_specs=(P(("dp", "expert"), None), P("dp", None)),
        check_vma=False,
    )
```

profile of v0, /device:TPU:1, one launch (start us, length us, event | category | flops | bytes accessed | tf_op | source)
XLA Modules:
  0.0 526.8 jit_solution(17911596552968877742)
XLA Ops:
  7.2 1.0 fusion.33
  8.2 0.7 fusion.89
  8.8 1.2 fusion.34
  11.1 17.6 %all-to-all-start.1 = ((bf16[32,1,8]{2,1,0:T(2,128)(2,1)}), bf16[32,1,8]{2,1,0:T(2,128)(2,1)S(1)}, u32[]{:S(2)}, u32[]{:S(2)}) async-start(bf16[32,1,8]{2,1,0:T(2,128)(2,1)} %copy.25), calls=%async_computation.1 | async-start | bytes 32768 | tf_op jit(solution)/shard_map/all_to_all | solution.py:67
  28.7 2.1 fusion.9
  30.8 5.9 %all-to-all-done.1 = bf16[32,1,8]{2,1,0:T(2,128)(2,1)S(1)} async-done(((bf16[32,1,8]{2,1,0:T(2,128)(2,1)}), bf16[32,1,8]{2,1,0:T(2,128)(2,1)S(1)}, u32[]{:S(2)}, u32[]{:S(2)}) %all-to-all-start.1) | async-done | bytes 544 | tf_op jit(solution)/shard_map/all_to_all | solution.py:67
  36.6 1.9 broadcast_in_dim.8
  38.5 4.8 all-to-all-start.2
  43.7 75.8 %all_gather.3 = bf16[256,1280]{1,0:T(8,128)(2,1)S(1)} all-gather(bf16[8,1280]{1,0:T(8,128)(2,1)S(1)} %copy-done.6), channel_id=1, replica_groups=mesh['dp'=32,'expert'=32] {'dp'}, dimensions={0}, use_global_device_ids=true | all-gather | bytes 675840 | tf_op jit(solution)/shard_map/all_gather | solution.py:17
  119.5 0.9 copy-done.1
  120.6 0.6 broadcast_in_dim.6
  121.3 23.1 %all-to-all-start = ((bf16[32,8,8]{2,1,0:T(8,128)(2,1)}), bf16[32,8,8]{2,1,0:T(8,128)(2,1)S(1)}, u32[]{:S(2)}, u32[]{:S(2)}) async-start(bf16[32,8,8]{2,1,0:T(8,128)(2,1)} %bitcast.5), calls=%async_computation | async-start | bytes 131072 | tf_op jit(solution)/shard_map/all_to_all | solution.py:66
  144.3 3.2 fusion.6
  147.5 1.1 copy-done.11
  148.6 2.3 fusion.2
  150.8 1.8 all-to-all-done
  152.6 2.0 convolution_bitcast_fusion
  154.8 102.1 %all-reduce = (f32[8,1280]{1,0:T(8,128)S(1)}, f32[8]{0:T(128)S(1)}) all-reduce(f32[8,1280]{1,0:T(8,128)S(1)} %convolution_add_fusion.1, f32[8]{0:T(128)S(1)} %convert_reduce_fusion), channel_id=1, replica_groups=mesh['dp'=32,'expert'=32] {'expert'}, use_global_device_ids=true, to_apply=%region_2.0 | all-reduce | flops 10248 | bytes 81984 | tf_op jit(solution)/shard_map/psum | solution.py:76
  257.2 2.4 fusion.32
  259.6 2.0 multiply_reduce_fusion.1
  261.7 2.5 multiply_reduce_fusion
  264.1 6.2 %fusion.4 = f32[32,8,1280]{2,1,0:T(8,128)} fusion(bf16[1280,1280]{1,0:T(8,128)(2,1)} %param.13, f32[32,8,1280]{2,1,0:T(8,128)} %copy-done.11, bf16[1280,1280]{1,0:T(8,128)(2,1)S(1)} %copy-done, f32[32,8,1280]{2,1,0:T(8,128)} %get-tuple-element.11, f32[32,8]{1,0:T(8,128)S(1)} %bitcast.70), kind=kOutput, calls=%fused_computation.4 | convolution fusion | flops 1684930560 | bytes 10486784 | tf_op jit(solution)/shard_map/skh,dh->skd/dot_general | solution.py:105
  270.3 9.1 %all-to-all-start.4 = ((f32[32,1,8]{2,1,0:T(1,128)}), f32[32,1,8]{2,1,0:T(1,128)S(1)}, u32[]{:S(2)}, u32[]{:S(2)}) async-start(f32[32,1,8]{2,1,0:T(1,128)} %bitcast.18), calls=%async_computation.4 | async-start | bytes 32768 | tf_op jit(solution)/shard_map/all_to_all | solution.py:109
  279.4 3.5 fusion.20
  282.9 4.3 all-to-all-done.4
  287.2 4.9 all-to-all-start.3
  292.1 2.8 fusion.21
  295.0 1.3 fusion.81
  296.6 29.2 %all-to-all-done.3 = f32[32,8,1280]{2,1,0:T(8,128)} async-done(((f32[32,8,1280]{2,1,0:T(8,128)}), f32[32,8,1280]{2,1,0:T(8,128)}, u32[]{:S(2)}, u32[]{:S(2)}) %all-to-all-start.3) | async-done | bytes 1310752 | tf_op jit(solution)/shard_map/all_to_all | solution.py:108
  325.8 1.5 bitcast_reduce_fusion
  328.2 1.1 fusion.8
  329.3 190.7 %reduce-scatter.2.cloned.1.call-done = f32[8,1280]{1,0:T(8,128)} async-done(((f32[256,1280]{1,0:T(8,128)}), f32[8,1280]{1,0:T(8,128)}) %reduce-scatter.2.cloned.1.call-update) | async-done | bytes 40976 | tf_op jit(solution)/shard_map/reduce_scatter | solution.py:95
  (47 shorter events, 3.2 us)
Async XLA Ops:
  7.2 141.4 %copy-start = (bf16[1280,1280]{1,0:T(8,128)(2,1)S(1)}, bf16[1280,1280]{1,0:T(8,128)(2,1)}, u32[]{:S(2)}) copy-start(bf16[1280,1280]{1,0:T(8,128)(2,1)} %param.14) | copy-start | bytes 9830404
  11.1 25.6 %all-to-all-start.1 = ((bf16[32,1,8]{2,1,0:T(2,128)(2,1)}), bf16[32,1,8]{2,1,0:T(2,128)(2,1)S(1)}, u32[]{:S(2)}, u32[]{:S(2)}) async-start(bf16[32,1,8]{2,1,0:T(2,128)(2,1)} %copy.25), calls=%async_computation.1 | async-start | bytes 32768 | tf_op jit(solution)/shard_map/all_to_all | solution.py:67
  30.7 12.5 %copy-start.8 = (s32[1,128]{1,0:T(1,128)S(1)}, s32[1,128]{1,0:T(1,128)}, u32[]{:S(2)}) copy-start(s32[1,128]{1,0:T(1,128)} %param.11) | copy-start | bytes 1540
  30.8 13.0 %copy-start.6 = (bf16[8,1280]{1,0:T(8,128)(2,1)S(1)}, bf16[8,1280]{1,0:T(8,128)(2,1)}, u32[]{:S(2)}) copy-start(bf16[8,1280]{1,0:T(8,128)(2,1)} %param.15) | copy-start | bytes 61444
  38.5 82.1 %all-to-all-start.2 = ((bf16[32,8,1280]{2,1,0:T(8,128)(2,1)}), bf16[32,8,1280]{2,1,0:T(8,128)(2,1)}, u32[]{:S(2)}, u32[]{:S(2)}) async-start(bf16[32,8,1280]{2,1,0:T(8,128)(2,1)} %bitcast.67), calls=%async_computation.2 | async-start | bytes 1310720 | tf_op jit(solution)/shard_map/all_to_all | solution.py:57
  119.5 0.9 copy-start.1
  121.3 31.4 %all-to-all-start = ((bf16[32,8,8]{2,1,0:T(8,128)(2,1)}), bf16[32,8,8]{2,1,0:T(8,128)(2,1)S(1)}, u32[]{:S(2)}, u32[]{:S(2)}) async-start(bf16[32,8,8]{2,1,0:T(8,128)(2,1)} %bitcast.5), calls=%async_computation | async-start | bytes 131072 | tf_op jit(solution)/shard_map/all_to_all | solution.py:66
  147.5 1.1 copy-start.11
  150.8 106.3 %copy-start.9 = (f32[8,256]{1,0:T(8,128)S(1)}, f32[8,256]{1,0:T(8,128)}, u32[]{:S(2)}) copy-start(f32[8,256]{1,0:T(8,128)} %param.17) | copy-start | bytes 24580
  150.8 106.3 %copy-start.10 = (s32[256]{0:T(256)S(1)}, s32[256]{0:T(256)}, u32[]{:S(2)}) copy-start(s32[256]{0:T(256)} %param.16) | copy-start | bytes 3076
  152.6 2.0 copy-start.3
  257.0 4.7 copy-start.2
  270.3 16.9 %all-to-all-start.4 = ((f32[32,1,8]{2,1,0:T(1,128)}), f32[32,1,8]{2,1,0:T(1,128)S(1)}, u32[]{:S(2)}, u32[]{:S(2)}) async-start(f32[32,1,8]{2,1,0:T(1,128)} %bitcast.18), calls=%async_computation.4 | async-start | bytes 32768 | tf_op jit(solution)/shard_map/all_to_all | solution.py:109
  287.2 38.6 %all-to-all-start.3 = ((f32[32,8,1280]{2,1,0:T(8,128)}), f32[32,8,1280]{2,1,0:T(8,128)}, u32[]{:S(2)}, u32[]{:S(2)}) async-start(f32[32,8,1280]{2,1,0:T(8,128)} %fusion.4), calls=%async_computation.3 | async-start | bytes 2621440 | tf_op jit(solution)/shard_map/all_to_all | solution.py:108
  292.1 227.9 %reduce-scatter.2.cloned.1.call-start = ((), (), s32[]{:S(2)}) async-start(), calls=%async_computation.6 | async-start | bytes 1351680 | tf_op jit(solution)/shard_map/reduce_scatter | solution.py:95
  325.8 1.5 copy-start.4
  327.4 0.8 copy-start.5
  327.4 0.8 copy-start.7
Sparse Core Ops, SparseCore 0:
  299.0 220.9 reduce-scatter.1
where the time goes:
time: 532 us; the launch traced here: 527 us
  waiting for transfers between devices  232 us (44%)
  blocking collectives  178 us (33%)
  starting transfers between devices  59.5 us (11%)
  matrix products  32 us (6%)
  between operations  14.3 us (3%)
  other arithmetic  5.67 us (1%)
  local copies, waits for them, and re-layouts  5.65 us (1%)
    reduce_scatter x1, waiting for transfers between devices, shards(): lax.psum_scatter(text_terms, 'dp', scatter_dimension=0, tiled=True)  191 us
    psum x1, blocking collectives, shards(): pooled, counts = lax.psum((pooled_part, counts_part), 'expert')  102 us
    all_gather x1, blocking collectives, caption_rows(): return lax.all_gather(captions, 'dp', axis=0, tiled=True)  75.8 us
    all_to_all x1, waiting for transfers between devices, shards(): lax.all_to_all(part_dx, 'expert', split_axis=0, concat_axis=0, tiled=True)  29.2 us
    all_to_all x1, starting transfers between devices, shards(): lax.all_to_all(send_clips, 'expert', split_axis=0, concat_axis=0, tiled=T...  23.1 us
    all_to_all x1, starting transfers between devices, shards(): lax.all_to_all(send_gates, 'expert', split_axis=0, concat_axis=0, tiled=T...  17.6 us
  transfers between devices with their start and end apart: 6, of which 5 were waited for; matrix products, arithmetic and copies ran while one was open for 4% of the time, Pallas kernels for 0%

commit v1 on v0

v1 whole, which is shorter than its diff:
```python
import jax
import jax.numpy as jnp
from jax import lax
from jax.sharding import PartitionSpec as P

HIGHEST = lax.Precision.HIGHEST
logit_scale = 10.0
logit_shift = -10.0
norm_eps = 1e-06
f32 = jnp.float32
bf16 = jnp.bfloat16
LANES = 128


def gelu_back(preact, upstream):
    return jax.vjp(jax.nn.gelu, preact)[1](upstream)[0]


def exchange(x, axis):
    return lax.all_to_all(x, axis, split_axis=0, concat_axis=0, tiled=True)


def shards(tokens, routes, pool_ids, w_router, w_up, w_down, captions, clip_pairs, teacher):
    tok_rows, width = tokens.shape
    n_experts = w_router.shape[1]
    n_clips, n_caps = teacher.shape
    n_dp = lax.axis_size("dp")
    n_exp = lax.axis_size("expert")
    capacity = tok_rows // n_experts
    slot_count = n_experts * capacity
    half = width // 2
    strip = width // n_exp
    own = lax.axis_index("expert")
    core = own % 2
    expert = own // 2
    swap = [(i, i ^ 1) for i in range(n_exp)]

    gathered = exchange(
        jnp.broadcast_to(captions[None], (n_dp,) + captions.shape), "dp"
    ).reshape(n_caps, width)

    route_ids = routes[:, 0]
    chosen = (route_ids[:, None] == jnp.arange(n_experts, dtype=jnp.int32)[None, :]).astype(bf16)
    positions = jnp.arange(tok_rows, dtype=jnp.int32)
    earlier = (positions[:, None] > positions[None, :]).astype(bf16)
    arrival = jnp.sum(
        jnp.dot(earlier, chosen, preferred_element_type=f32) * chosen.astype(f32), axis=1
    )
    slot_index = route_ids.astype(f32) * capacity + arrival
    slot_range = jnp.arange(slot_count, dtype=f32)
    placed = (
        (slot_index[:, None] == slot_range[None, :]) & (arrival < capacity)[:, None]
    ).astype(bf16)
    members = (pool_ids[0][:, None] == jnp.arange(n_clips, dtype=jnp.int32)[None, :]).astype(bf16)
    placed_t = placed.T
    slot_rows = jnp.dot(placed_t, tokens, preferred_element_type=f32).astype(bf16)
    slot_clips = jnp.dot(placed_t, members, preferred_element_type=f32).astype(bf16)
    counts_part = jnp.sum(members.astype(f32), axis=0)
    side = jnp.concatenate(
        [
            slot_clips,
            jnp.broadcast_to(counts_part[None].astype(bf16), (slot_count, n_clips)),
            jnp.zeros((slot_count, LANES - 2 * n_clips), bf16),
        ],
        axis=1,
    ).reshape(n_experts, 1, capacity, LANES)
    halves = slot_rows.reshape(n_experts, capacity, 2, half).transpose(0, 2, 1, 3)
    send = jnp.concatenate(
        [halves, jnp.broadcast_to(side, (n_experts, 2, capacity, LANES))], axis=3
    ).reshape(n_exp, capacity, half + LANES)
    recv = exchange(send, "expert")
    rows_own = recv[..., :half].reshape(n_exp * capacity, half)
    rows_other = lax.ppermute(rows_own, "expert", swap)
    rows = jnp.where(
        core == 0,
        jnp.concatenate([rows_own, rows_other], axis=1),
        jnp.concatenate([rows_other, rows_own], axis=1),
    )
    clip_weights = recv[..., half : half + n_clips].reshape(-1, n_clips).astype(f32)
    counts = jnp.sum(recv[:, 0, half + n_clips : half + 2 * n_clips].astype(f32), axis=0)

    own_col = (jnp.arange(n_experts) == expert).astype(f32)
    scores = jnp.dot(rows, w_router, preferred_element_type=f32)
    sigmoid_gate = jax.nn.sigmoid(jnp.sum(scores * own_col[None], axis=1))
    gate = sigmoid_gate.astype(bf16).astype(f32)
    router_col = jnp.sum(w_router.astype(f32) * own_col[None], axis=1)

    preact = jnp.dot(rows, w_up, preferred_element_type=f32)
    hidden = jax.nn.gelu(preact).astype(bf16)
    produced = jnp.dot(hidden, w_down, preferred_element_type=f32)
    pooled_part = jnp.dot(members.T, tokens, preferred_element_type=f32)
    pooled_part = pooled_part + jnp.dot(
        (clip_weights * gate[:, None]).T, produced, precision=HIGHEST
    )
    quarter = n_clips * width // n_exp
    blocks = width // quarter
    pieces = pooled_part.reshape(n_clips, blocks, quarter).transpose(1, 0, 2)
    pieces = exchange(pieces.reshape(n_exp, 1, quarter), "expert")
    piece = jnp.sum(pieces, axis=0, keepdims=True)
    pooled = exchange(jnp.broadcast_to(piece, (n_exp, 1, quarter)), "expert")
    pooled = pooled.reshape(blocks, n_clips, quarter).transpose(1, 0, 2).reshape(n_clips, width)

    clip_mean = pooled / counts[:, None]
    img_scale = lax.rsqrt(jnp.sum(clip_mean * clip_mean, axis=1, keepdims=True) + norm_eps)
    image_emb = clip_mean * img_scale
    text_raw = gathered.astype(f32)
    text_scale = lax.rsqrt(jnp.sum(text_raw * text_raw, axis=1) + norm_eps)
    raw_dots = jnp.dot(image_emb, text_raw.T, precision=HIGHEST)
    logits = logit_scale * raw_dots * text_scale[None] + logit_shift
    own_clips = lax.axis_index("dp") * n_clips + jnp.arange(n_clips, dtype=jnp.int32)
    matched = (clip_pairs[None, :] == own_clips[:, None]).astype(f32)
    target = 0.5 * matched + 0.5 * jax.nn.sigmoid(teacher)
    loss_grad = (jax.nn.sigmoid(logits) - target) * (counts[:, None] / n_caps)
    d_image = logit_scale * jnp.dot(loss_grad * text_scale[None], text_raw, precision=HIGHEST)
    mean_grad = (
        img_scale * d_image
        - img_scale**3 * jnp.sum(clip_mean * d_image, axis=1, keepdims=True) * clip_mean
    )
    clip_grad = mean_grad / counts[:, None]

    emb_strip = lax.dynamic_slice_in_dim(image_emb, own * strip, strip, 1)
    raw_strip = lax.dynamic_slice_in_dim(gathered, own * strip, strip, 1).astype(f32)
    text_strip = logit_scale * jnp.dot(loss_grad.T, emb_strip, precision=HIGHEST)
    text_dot = logit_scale * jnp.sum(loss_grad * raw_dots, axis=0)
    terms = (
        text_scale[:, None] * text_strip
        - (text_scale**3 * text_dot)[:, None] * raw_strip
    )
    caps_dp = n_caps // n_dp
    strip_grads = jnp.sum(
        exchange(terms.reshape(n_dp, 1, caps_dp * strip), "dp"), axis=(0, 1)
    ).reshape(caps_dp, strip)

    unit_dy = jnp.dot(clip_weights, clip_grad, precision=HIGHEST)
    cotangent = (gate[:, None] * unit_dy).astype(bf16)
    d_hidden = lax.dot_general(
        cotangent, w_down, (((1,), (1,)), ((), ())), preferred_element_type=f32
    )
    d_preact = gelu_back(preact, d_hidden).astype(bf16)
    slope = jnp.sum(unit_dy * produced, axis=1) * sigmoid_gate * (1.0 - sigmoid_gate)

    def part_dx(which):
        w_half = lax.dynamic_slice_in_dim(w_up, which * half, half, 0)
        col = lax.dynamic_slice_in_dim(router_col, which * half, half, 0)
        return (
            lax.dot_general(
                d_preact, w_half, (((1,), (1,)), ((), ())), preferred_element_type=f32
            )
            + slope[:, None] * col[None]
        )

    from_other = lax.ppermute(part_dx(1 - core), "expert", swap)
    dx_half = (part_dx(core) + from_other).astype(bf16).reshape(n_exp, capacity, half)

    high = strip_grads.astype(bf16)
    low = (strip_grads - high.astype(f32)).astype(bf16)
    strips = jnp.concatenate([high, low, jnp.zeros((caps_dp, LANES - 2 * strip), bf16)], axis=1)
    back = exchange(
        jnp.concatenate(
            [dx_half, jnp.broadcast_to(strips[None], (n_exp, caps_dp, LANES))], axis=2
        ),
        "expert",
    )
    slot_dx = (
        back[..., :half]
        .reshape(n_experts, 2, capacity, half)
        .transpose(0, 2, 1, 3)
        .reshape(slot_count, width)
    )
    token_dx = jnp.dot(placed, slot_dx, preferred_element_type=f32)
    token_dy = jnp.dot(members.astype(f32), clip_grad, precision=HIGHEST)
    sides = back[..., half : half + 2 * strip].astype(f32)
    caption_grads = (
        (sides[..., :strip] + sides[..., strip:]).transpose(1, 0, 2).reshape(caps_dp, width)
    )
    return (token_dy + token_dx, caption_grads)


def solution(mesh):
    return jax.shard_map(
        shards,
        mesh=mesh,
        in_specs=(
            P(("dp", "expert"), None),
            P(("dp", "expert"), None),
            P("dp", "expert"),
            P(),
            P(None, "expert"),
            P("expert", None),
            P("dp", None),
            P(),
            P("dp", None),
        ),
        out_specs=(P(("dp", "expert"), None), P("dp", None)),
        check_vma=False,
    )
```

time: 532 us -> 172 us (0.32)
  waiting for transfers between devices: 232 us -> 56.4 us
  blocking collectives: 178 us -> 22.6 us
  between operations: 14.3 us -> 1.35 us
  matrix products: 32 us -> 23.2 us
  starting transfers between devices: 59.5 us -> 51 us
    reduce_scatter x1 -> x0, waiting for transfers between devices: 191 us -> none  [shards(): lax.psum_scatter(text_terms, 'dp', scatter_dimension=0, tiled=True)]
    psum x1 -> x0, blocking collectives: 102 us -> none  [shards(): pooled, counts = lax.psum((pooled_part, counts_part), 'expert')]
    all_gather x1 -> x0, blocking collectives: 75.8 us -> none  [caption_rows(): return lax.all_gather(captions, 'dp', axis=0, tiled=True)]
    all_to_all x0 -> x2, blocking collectives: none -> 22.6 us  [exchange(): return lax.all_to_all(x, axis, split_axis=0, concat_axis=0, tiled=True)]
    all_to_all x5 -> x4, starting transfers between devices: 59.5 us -> 43 us  [exchange(): return lax.all_to_all(x, axis, split_axis=0, concat_axis=0, tiled=True)]
    all_to_all x5 -> x4, waiting for transfers between devices: 41.1 us -> 56.4 us  [exchange(): return lax.all_to_all(x, axis, split_axis=0, concat_axis=0, tiled=True)]
    dot_general x18 -> x17, matrix products: 32 us -> 23.2 us  [the longest x2 4.05 us: part_dx(): lax.dot_general(d_preact, w_half, (((1,), (1,)), ((), ())), preferred_ele...]
    ppermute x0 -> x2, starting transfers between devices: none -> 7.98 us  [the longest x1 4.43 us: shards(): from_other = lax.ppermute(part_dx(1 - core), 'expert', swap)]
where the time goes in v1:
time: 172 us; the launch traced here: 171 us
  waiting for transfers between devices  56.4 us (33%)
  starting transfers between devices  51 us (30%)
  matrix products  23.2 us (13%)
  blocking collectives  22.6 us (13%)
  local copies, waits for them, and re-layouts  8.92 us (5%)
  other arithmetic  7.46 us (4%)
    all_to_all x4, waiting for transfers between devices, exchange(): return lax.all_to_all(x, axis, split_axis=0, concat_axis=0, tiled=True)  56.4 us
    all_to_all x4, starting transfers between devices, exchange(): return lax.all_to_all(x, axis, split_axis=0, concat_axis=0, tiled=True)  43 us
    all_to_all x2, blocking collectives, exchange(): return lax.all_to_all(x, axis, split_axis=0, concat_axis=0, tiled=True)  22.6 us
    ppermute x1, starting transfers between devices, shards(): from_other = lax.ppermute(part_dx(1 - core), 'expert', swap)  4.43 us
    dot_general x2, matrix products, part_dx(): lax.dot_general(d_preact, w_half, (((1,), (1,)), ((), ())), preferred_ele...  4.05 us
    ppermute x1, starting transfers between devices, shards(): rows_other = lax.ppermute(rows_own, 'expert', swap)  3.55 us
  transfers between devices with their start and end apart: 6, of which 5 were waited for; matrix products, arithmetic and copies ran while one was open for 4% of the time, Pallas kernels for 0%

profile of v1, /device:TPU:1, one launch (start us, length us, event | category | flops | bytes accessed | tf_op | source)
XLA Modules:
  0.0 171.0 jit_solution(2168499874607038022)
XLA Ops:
  0.6 1.0 fusion.28
  4.2 1.3 convolution_convert_fusion
  6.4 18.3 %all-to-all-start = ((bf16[32,8,768]{2,1,0:T(8,128)(2,1)}), bf16[32,8,768]{2,1,0:T(8,128)(2,1)}, u32[]{:S(2)}, u32[]{:S(2)}) async-start(bf16[32,8,768]{2,1,0:T(8,128)(2,1)} %bitcast.68), calls=%async_computation | async-start | bytes 786432 | tf_op jit(solution)/shard_map/all_to_all | solution.py:20
  24.8 13.9 %all-to-all-done = bf16[32,8,768]{2,1,0:T(8,128)(2,1)} async-done(((bf16[32,8,768]{2,1,0:T(8,128)(2,1)}), bf16[32,8,768]{2,1,0:T(8,128)(2,1)}, u32[]{:S(2)}, u32[]{:S(2)}) %all-to-all-start) | async-done | bytes 393248 | tf_op jit(solution)/shard_map/all_to_all | solution.py:20
  38.7 1.2 slice_bitcast_fusion
  39.9 3.5 %collective-permute-start = (bf16[256,640]{1,0:T(8,128)(2,1)S(1)}, bf16[256,640]{1,0:T(8,128)(2,1)S(1)}, u32[]{:S(2)}, u32[]{:S(2)}) collective-permute-start(bf16[256,640]{1,0:T(8,128)(2,1)S(1)} %slice_bitcast_fusion), channel_id=1, source_target_pairs={{0,1},{1,0},{2,3},{3,2},{4,5},{5,4},{6,7},{7,6},{8,9},{9,8},{10,11... | collective-permute-start | bytes 983048 | tf_op jit(solution)/shard_map/ppermute | solution.py:73
  43.5 1.1 fusion.60
  45.7 1.1 fusion.39
  46.8 1.3 fusion.29
  48.1 1.0 copy-done.1
  49.1 1.6 convolution_add_fusion.1
  50.9 11.3 %all_to_all.30 = f32[32,1,320]{2,1,0:T(1,128)S(1)} all-to-all(f32[32,1,320]{2,1,0:T(1,128)S(1)} %copy.38), channel_id=1, replica_groups=mesh['dp'=32,'expert'=32] {'expert'}, dimensions={0} | all-to-all | bytes 81920 | tf_op jit(solution)/shard_map/all_to_all | solution.py:20
  62.3 11.3 %all_to_all.31 = f32[32,1,320]{2,1,0:T(1,128)S(1)} all-to-all(f32[32,1,320]{2,1,0:T(1,128)S(1)} %broadcast_in_dim.20), channel_id=1, replica_groups=mesh['dp'=32,'expert'=32] {'expert'}, dimensions={0} | all-to-all | bytes 81920 | tf_op jit(solution)/shard_map/all_to_all | solution.py:20
  74.4 13.0 %all-to-all-start.3 = ((bf16[32,8,1280]{2,1,0:T(8,128)(2,1)}), bf16[32,8,1280]{2,1,0:T(8,128)(2,1)}, u32[]{:S(2)}, u32[]{:S(2)}) async-start(bf16[32,8,1280]{2,1,0:T(8,128)(2,1)} %broadcast_in_dim.21), calls=%async_computation.3 | async-start | bytes 1310720 | tf_op jit(solution)/shard_map/all_to_all | solution.py:20
  88.2 1.0 fusion.52
  89.8 18.8 %all-to-all-done.3 = bf16[32,8,1280]{2,1,0:T(8,128)(2,1)} async-done(((bf16[32,8,1280]{2,1,0:T(8,128)(2,1)}), bf16[32,8,1280]{2,1,0:T(8,128)(2,1)}, u32[]{:S(2)}, u32[]{:S(2)}) %all-to-all-start.3) | async-done | bytes 655392 | tf_op jit(solution)/shard_map/all_to_all | solution.py:20
  108.6 1.3 multiply_reduce_fusion.1
  110.0 1.0 constant_dynamic-slice_fusion
  111.1 1.9 %multiply_reduce_fusion.5 = (f32[256]{0:T(256)S(1)}, f32[8,256]{1,0:T(8,128)S(1)}) fusion(f32[8]{0:T(128)S(1)} %broadcast_multiply_fusion.3, f32[8,256]{1,0:T(8,128)S(1)} %copy-done.5, s32[8]{0:T(128)S(1)} %iota_add_fusion, s32[256]{0:T(256)S(1)} %copy-done.22, f32[256]{0:T(256)S(1)} %broadcast_multiply_fusion.1, f32[8,1280]{1,0:T(8,128)S(1)} %mul.287, ...), kind=kOutput, calls=%fused_computation.74 | convolution fusion | flops 31489792 | bytes 715840 | tf_op jit(solution)/shard_map/dot_general | solution.py:108
  113.0 1.6 multiply_reduce_fusion.4
  114.7 1.8 %multiply_reduce_fusion = (f32[256]{0:T(256)S(1)}, f32[256,1280]{1,0:T(8,128)S(1)}) fusion(f32[256,1280]{1,0:T(8,128)S(1)} %copy-done.2, f32[8,1280]{1,0:T(8,128)S(1)} %get-tuple-element.7, f32[8,1280]{1,0:T(8,128)S(1)} %get-tuple-element.14, f32[8]{0:T(128)S(1)} %get-tuple-element.13, f32[8]{0:T(128)S(1)} %fusion.52, f32[8]{0:T(128)S(1)} %get-tuple-element.12, ...), kind=kOutput, calls=%fused_computation.16 | convolution fusion | flops 32153344 | bytes 2770016 | tf_op jit(solution)/shard_map/dot_general | solution.py:134
  116.5 1.5 fusion.10
  118.5 1.5 fusion.14
  120.0 4.4 %collective-permute-start.1 = (f32[256,640]{1,0:T(8,128)}, f32[256,640]{1,0:T(8,128)}, u32[]{:S(2)}, u32[]{:S(2)}) collective-permute-start(f32[256,640]{1,0:T(8,128)} %fusion.14), channel_id=1, source_target_pairs={{0,1},{1,0},{2,3},{3,2},{4,5},{5,4},{6,7},{7,6},{8,9},{9,8},{10,11... | collective-permute-start | bytes 1966088 | tf_op jit(solution)/shard_map/ppermute | solution.py:152
  125.7 6.0 %all-to-all-start.4 = ((f32[32,1,320]{2,1,0:T(1,128)}), f32[32,1,320]{2,1,0:T(1,128)S(1)}, u32[]{:S(2)}, u32[]{:S(2)}) async-start(f32[32,1,320]{2,1,0:T(1,128)} %reshape.174), calls=%async_computation.4 | async-start | bytes 98304 | tf_op jit(solution)/shard_map/all_to_all | solution.py:20
  131.8 11.0 %all-to-all-done.4 = f32[32,1,320]{2,1,0:T(1,128)S(1)} async-done(((f32[32,1,320]{2,1,0:T(1,128)}), f32[32,1,320]{2,1,0:T(1,128)S(1)}, u32[]{:S(2)}, u32[]{:S(2)}) %all-to-all-start.4) | async-done | bytes 40992 | tf_op jit(solution)/shard_map/all_to_all | solution.py:20
  143.0 2.5 %fusion.23 = bf16[32,8,640]{2,1,0:T(8,128)(2,1)S(1)} fusion(f32[256,640]{1,0:T(8,128)} %collective-permute-done.1, bf16[256,1280]{1,0:T(8,128)(2,1)} %copy-done.28, bf16[1280,1280]{1,0:T(8,128)(2,1)} %param.13, s32[]{:T(128)S(6)} %select_n.35, f32[640]{0:T(1024)} %get-tuple-element.10, f32[256]{0:T(256)} %copy-done.23), kind=kOutput, calls=%fused_computation.24 | convolution fusion | flops 420085760 | bytes 3281924 | tf_op jit(solution)/shard_map/dot_general | solution.py:146
  146.4 5.6 %all-to-all-start.5 = ((bf16[32,8,768]{2,1,0:T(8,128)(2,1)}), bf16[32,8,768]{2,1,0:T(8,128)(2,1)}, u32[]{:S(2)}, u32[]{:S(2)}) async-start(bf16[32,8,768]{2,1,0:T(8,128)(2,1)} %pad_maximum_fusion.1), calls=%async_computation.5 | async-start | bytes 786432 | tf_op jit(solution)/shard_map/all_to_all | solution.py:20
  152.1 1.3 fusion.58
  153.4 12.6 %all-to-all-done.5 = bf16[32,8,768]{2,1,0:T(8,128)(2,1)} async-done(((bf16[32,8,768]{2,1,0:T(8,128)(2,1)}), bf16[32,8,768]{2,1,0:T(8,128)(2,1)}, u32[]{:S(2)}, u32[]{:S(2)}) %all-to-all-start.5) | async-done | bytes 393248 | tf_op jit(solution)/shard_map/all_to_all | solution.py:20
  167.7 1.0 slice.31
  168.7 2.2 %convolution_add_fusion = f32[128,1280]{1,0:T(8,128)} fusion(f32[128,1280]{1,0:T(8,128)} %fusion.58, bf16[128,1280]{1,0:T(8,128)(2,1)S(1)} %bitcast.70, f32[128]{0:T(128)S(1)} %copy-done.19, pred[128]{0:T(512)(128)(4,1)S(1)} %copy-done.17), kind=kOutput, calls=%fused_computation | convolution fusion | flops 42139648 | bytes 1639040 | tf_op jit(solution)/shard_map/dot_general | solution.py:170
  (117 shorter events, 11.6 us)
Async XLA Ops:
  0.6 46.1 %copy-start = (bf16[1280,1280]{1,0:T(8,128)(2,1)S(1)}, bf16[1280,1280]{1,0:T(8,128)(2,1)}, u32[]{:S(2)}) copy-start(bf16[1280,1280]{1,0:T(8,128)(2,1)} %param.14) | copy-start | bytes 9830404
  1.6 38.3 %copy-start.16 = (pred[128]{0:T(512)(128)(4,1)}, pred[128]{0:T(512)(128)(4,1)S(1)}, u32[]{:S(2)}) copy-start(pred[128]{0:T(512)(128)(4,1)S(1)} %broadcast_compare_fusion) | copy-start | bytes 388
  2.3 37.6 %copy-start.18 = (f32[128]{0:T(128)}, f32[128]{0:T(128)S(1)}, u32[]{:S(2)}) copy-start(f32[128]{0:T(128)S(1)} %fusion.71) | copy-start | bytes 1540
  5.6 37.9 %copy-start.20 = (s32[1,128]{1,0:T(1,128)S(1)}, s32[1,128]{1,0:T(1,128)}, u32[]{:S(2)}) copy-start(s32[1,128]{1,0:T(1,128)} %param.11) | copy-start | bytes 1540
  5.7 39.1 %copy-start.3 = (bf16[1280,16]{0,1:T(8,128)(2,1)S(1)}, bf16[1280,16]{0,1:T(8,128)(2,1)}, u32[]{:S(2)}) copy-start(bf16[1280,16]{0,1:T(8,128)(2,1)} %param.12) | copy-start | bytes 122884
  6.4 32.3 %all-to-all-start = ((bf16[32,8,768]{2,1,0:T(8,128)(2,1)}), bf16[32,8,768]{2,1,0:T(8,128)(2,1)}, u32[]{:S(2)}, u32[]{:S(2)}) async-start(bf16[32,8,768]{2,1,0:T(8,128)(2,1)} %bitcast.68), calls=%async_computation | async-start | bytes 786432 | tf_op jit(solution)/shard_map/all_to_all | solution.py:20
  38.7 6.9 %copy-start.26 = (bf16[1280,1280]{1,0:T(8,128)(2,1)S(1)}, bf16[1280,1280]{1,0:T(8,128)(2,1)}, u32[]{:S(2)}) copy-start(bf16[1280,1280]{1,0:T(8,128)(2,1)} %param.13) | copy-start | bytes 9830404
  39.9 4.8 %collective-permute-start = (bf16[256,640]{1,0:T(8,128)(2,1)S(1)}, bf16[256,640]{1,0:T(8,128)(2,1)S(1)}, u32[]{:S(2)}, u32[]{:S(2)}) collective-permute-start(bf16[256,640]{1,0:T(8,128)(2,1)S(1)} %slice_bitcast_fusion), channel_id=1, source_target_pairs={{0,1},{1,0},{2,3},{3,2},{4,5},{5,4},{6,7},{7,6},{8,9},{9,8},{10,11... | collective-permute-start | bytes 983048 | tf_op jit(solution)/shard_map/ppermute | solution.py:73
  45.7 2.4 %copy-start.10 = (f32[256]{0:T(256)}, f32[256]{0:T(256)S(1)}, u32[]{:S(2)}) copy-start(f32[256]{0:T(256)S(1)} %get-tuple-element.8) | copy-start | bytes 3076
  48.1 25.5 %copy-start.4 = (bf16[8,1280]{1,0:T(8,128)(2,1)S(1)}, bf16[8,1280]{1,0:T(8,128)(2,1)}, u32[]{:S(2)}) copy-start(bf16[8,1280]{1,0:T(8,128)(2,1)} %param.15) | copy-start | bytes 61444
  74.4 36.7 %copy-start.5 = (f32[8,256]{1,0:T(8,128)S(1)}, f32[8,256]{1,0:T(8,128)}, u32[]{:S(2)}) copy-start(f32[8,256]{1,0:T(8,128)} %param.17) | copy-start | bytes 24580
  74.4 36.7 %copy-start.22 = (s32[256]{0:T(256)S(1)}, s32[256]{0:T(256)}, u32[]{:S(2)}) copy-start(s32[256]{0:T(256)} %param.16) | copy-start | bytes 3076
  74.4 34.2 %all-to-all-start.3 = ((bf16[32,8,1280]{2,1,0:T(8,128)(2,1)}), bf16[32,8,1280]{2,1,0:T(8,128)(2,1)}, u32[]{:S(2)}, u32[]{:S(2)}) async-start(bf16[32,8,1280]{2,1,0:T(8,128)(2,1)} %broadcast_in_dim.21), calls=%async_computation.3 | async-start | bytes 1310720 | tf_op jit(solution)/shard_map/all_to_all | solution.py:20
  89.5 20.5 %copy-start.24 = (f32[8]{0:T(128)}, f32[8]{0:T(128)S(1)}, u32[]{:S(2)}) copy-start(f32[8]{0:T(128)S(1)} %add_rsqrt_fusion.1) | copy-start | bytes 100
  110.0 4.7 %copy-start.12 = (f32[256]{0:T(256)}, f32[256]{0:T(256)S(1)}, u32[]{:S(2)}) copy-start(f32[256]{0:T(256)S(1)} %broadcast_multiply_fusion.1) | copy-start | bytes 3076
  111.1 3.5 %copy-start.2 = (f32[256,1280]{1,0:T(8,128)S(1)}, f32[256,1280]{1,0:T(8,128)}, u32[]{:S(2)}) copy-start(f32[256,1280]{1,0:T(8,128)} %copy-done.1) | copy-start | bytes 3932164
  114.6 1.8 %copy-start.6 = (f32[8]{0:T(128)}, f32[8]{0:T(128)S(1)}, u32[]{:S(2)}) copy-start(f32[8]{0:T(128)S(1)} %get-tuple-element.12) | copy-start | bytes 100
  114.6 1.8 %copy-start.8 = (f32[8]{0:T(128)}, f32[8]{0:T(128)S(1)}, u32[]{:S(2)}) copy-start(f32[8]{0:T(128)S(1)} %get-tuple-element.13) | copy-start | bytes 100
  114.7 1.8 %copy-start.11 = (f32[256]{0:T(256)S(1)}, f32[256]{0:T(256)}, u32[]{:S(2)}) copy-start(f32[256]{0:T(256)} %copy-done.10) | copy-start | bytes 3076
  116.5 1.9 %copy-start.27 = (bf16[1280,1280]{1,0:T(8,128)(2,1)S(1)}, bf16[1280,1280]{1,0:T(8,128)(2,1)}, u32[]{:S(2)}) copy-start(bf16[1280,1280]{1,0:T(8,128)(2,1)} %param.13) | copy-start | bytes 9830404
  118.0 2.0 %copy-start.28 = (bf16[256,1280]{1,0:T(8,128)(2,1)}, bf16[256,1280]{1,0:T(8,128)(2,1)S(1)}, u32[]{:S(2)}) copy-start(bf16[256,1280]{1,0:T(8,128)(2,1)S(1)} %fusion.10) | copy-start | bytes 1966084
  118.1 1.9 %copy-start.23 = (f32[256]{0:T(256)}, f32[256]{0:T(256)S(1)}, u32[]{:S(2)}) copy-start(f32[256]{0:T(256)S(1)} %subtract_multiply_fusion.1) | copy-start | bytes 3076
  118.4 6.0 %copy-start.13 = (f32[256]{0:T(256)S(1)}, f32[256]{0:T(256)}, u32[]{:S(2)}) copy-start(f32[256]{0:T(256)} %copy-done.12) | copy-start | bytes 3076
  118.5 6.0 %copy-start.25 = (f32[8]{0:T(128)S(1)}, f32[8]{0:T(128)}, u32[]{:S(2)}) copy-start(f32[8]{0:T(128)} %copy-done.24) | copy-start | bytes 100
  120.0 23.0 %collective-permute-start.1 = (f32[256,640]{1,0:T(8,128)}, f32[256,640]{1,0:T(8,128)}, u32[]{:S(2)}, u32[]{:S(2)}) collective-permute-start(f32[256,640]{1,0:T(8,128)} %fusion.14), channel_id=1, source_target_pairs={{0,1},{1,0},{2,3},{3,2},{4,5},{5,4},{6,7},{7,6},{8,9},{9,8},{10,11... | collective-permute-start | bytes 1966088 | tf_op jit(solution)/shard_map/ppermute | solution.py:152
  125.7 17.1 %all-to-all-start.4 = ((f32[32,1,320]{2,1,0:T(1,128)}), f32[32,1,320]{2,1,0:T(1,128)S(1)}, u32[]{:S(2)}, u32[]{:S(2)}) async-start(f32[32,1,320]{2,1,0:T(1,128)} %reshape.174), calls=%async_computation.4 | async-start | bytes 98304 | tf_op jit(solution)/shard_map/all_to_all | solution.py:20
  145.5 6.5 %copy-start.7 = (f32[8]{0:T(128)S(1)}, f32[8]{0:T(128)}, u32[]{:S(2)}) copy-start(f32[8]{0:T(128)} %copy-done.6) | copy-start | bytes 100
  145.6 6.5 %copy-start.9 = (f32[8]{0:T(128)S(1)}, f32[8]{0:T(128)}, u32[]{:S(2)}) copy-start(f32[8]{0:T(128)} %copy-done.8) | copy-start | bytes 100
  145.6 6.5 %copy-start.21 = (s32[1,128]{1,0:T(1,128)S(1)}, s32[1,128]{1,0:T(1,128)}, u32[]{:S(2)}) copy-start(s32[1,128]{1,0:T(1,128)} %param.11) | copy-start | bytes 1540
  146.4 19.6 %all-to-all-start.5 = ((bf16[32,8,768]{2,1,0:T(8,128)(2,1)}), bf16[32,8,768]{2,1,0:T(8,128)(2,1)}, u32[]{:S(2)}, u32[]{:S(2)}) async-start(bf16[32,8,768]{2,1,0:T(8,128)(2,1)} %pad_maximum_fusion.1), calls=%async_computation.5 | async-start | bytes 786432 | tf_op jit(solution)/shard_map/all_to_all | solution.py:20
  152.0 16.7 %copy-start.17 = (pred[128]{0:T(512)(128)(4,1)S(1)}, pred[128]{0:T(512)(128)(4,1)}, u32[]{:S(2)}) copy-start(pred[128]{0:T(512)(128)(4,1)} %copy-done.16) | copy-start | bytes 388
  152.1 16.7 %copy-start.19 = (f32[128]{0:T(128)S(1)}, f32[128]{0:T(128)}, u32[]{:S(2)}) copy-start(f32[128]{0:T(128)} %copy-done.18) | copy-start | bytes 1540
  (5 other events, 7.3 us)

commit v2 on v0

v2 whole, which is shorter than its diff:
```python
import functools
import jax
import jax.numpy as jnp
from jax import lax
from jax.experimental import pallas as pl
from jax.experimental.pallas import tpu as pltpu
from jax.sharding import PartitionSpec as P

HIGHEST = lax.Precision.HIGHEST
logit_scale = 10.0
logit_shift = -10.0
norm_eps = 1e-06
f32 = jnp.float32
bf16 = jnp.bfloat16
LANES = 128
LOW = 256
MIB = 1 << 20


def exchange(x, axis):
    return lax.all_to_all(x, axis, split_axis=0, concat_axis=0, tiled=True)


def iota(shape, axis):
    return lax.broadcasted_iota(jnp.int32, shape, axis)


def nn(a, b):
    return lax.dot_general(a, b, (((1,), (0,)), ((), ())), preferred_element_type=f32)


def nt(a, b):
    return lax.dot_general(a, b, (((1,), (1,)), ((), ())), preferred_element_type=f32)


def stack3(x):
    high = x.astype(bf16).astype(f32)
    rest = x - high
    mid = rest.astype(bf16).astype(f32)
    return jnp.concatenate([high, mid, rest - mid], axis=0).astype(bf16)


def fold3(x):
    rows = x.shape[0] // 3
    return x[:rows] + (x[rows : 2 * rows] + x[2 * rows :])


def slot_matrix(route_row, capacity, n_experts):
    toks = route_row.shape[1]
    chosen = (iota((n_experts, toks), 0) == route_row).astype(f32)
    earlier = (iota((toks, toks), 0) < iota((toks, toks), 1)).astype(f32).astype(bf16)
    before = nn(chosen.astype(bf16), earlier)
    arrival = jnp.sum(before * chosen, axis=0, keepdims=True)
    slot = route_row.astype(f32) * capacity + arrival
    slot = jnp.where(arrival < capacity, slot, -1.0)
    return (iota((n_experts * capacity, toks), 0).astype(f32) == slot).astype(f32)


def pack_kernel(capacity, n_experts, n_clips, tok_ref, route_ref, pool_ref, send_ref, base_ref, placed_ref):
    toks, width = tok_ref.shape
    half = width // 2
    placed_t = slot_matrix(route_ref[...], capacity, n_experts)
    placed_ref[...] = placed_t.T.astype(bf16)
    placed_t = placed_t.astype(bf16)
    pool = pool_ref[...]
    ids = iota((LANES, toks), 0)
    members = (ids == pool).astype(f32)
    counted = (ids - n_clips == pool).astype(f32).astype(bf16)
    side = nt(placed_t, members.astype(bf16)) + nt(
        jnp.ones((n_experts * capacity, toks), bf16), counted
    )
    side = side.reshape(n_experts, capacity, LANES).astype(bf16)
    tokens = tok_ref[...]
    base_ref[...] = nn(members[:n_clips].astype(bf16), tokens)
    rows = nn(placed_t, tokens)
    for h in range(2):
        send_ref[:, h, :, :half] = (
            rows[:, h * half : (h + 1) * half].reshape(n_experts, capacity, half).astype(bf16)
        )
        send_ref[:, h, :, half:] = side


def forward_kernel(
    n_clips, at_ref, recv_ref, other_ref, router_ref, up_ref, down_ref, base_ref,
    slope_ref, hidden_ref, aux_ref, counts_ref, pooled_ref,
):
    n_exp, capacity, wide = recv_ref.shape
    half = wide - LANES
    rows = n_exp * capacity
    n_experts = router_ref.shape[0]
    expert = at_ref[0]
    own_at = pl.multiple_of(at_ref[1] * half, LANES)
    other_at = pl.multiple_of((1 - at_ref[1]) * half, LANES)
    own = recv_ref[:, :, :half].astype(f32).reshape(rows, half).astype(bf16)
    other = other_ref[:, :, :half].astype(f32).reshape(rows, half).astype(bf16)
    side = recv_ref[:, :, half:].astype(f32).reshape(rows, LANES)
    scores = nt(own, router_ref[:, pl.ds(own_at, half)]) + nt(
        other, router_ref[:, pl.ds(other_at, half)]
    )
    mine = iota((rows, n_experts), 1) == expert
    score = jnp.sum(jnp.where(mine, scores, 0.0), axis=1, keepdims=True)
    sigmoid_gate = jax.nn.sigmoid(score)
    gate = sigmoid_gate.astype(bf16).astype(f32)
    lane = iota((rows, LANES), 1)
    clip = jnp.where(lane < n_clips, side, 0.0)
    aux_ref[...] = jnp.where(
        lane == n_clips,
        gate,
        jnp.where(lane == n_clips + 1, sigmoid_gate * (1.0 - sigmoid_gate), clip),
    )
    preact = nn(own, up_ref[pl.ds(own_at, half), :]) + nn(other, up_ref[pl.ds(other_at, half), :])
    root = 0.7978845608028654
    square = preact * preact
    tanh = jnp.tanh(root * (preact + 0.044715 * (square * preact)))
    hidden = (preact * (0.5 * (1.0 + tanh))).astype(bf16)
    hidden_ref[...] = hidden
    slope_ref[...] = 0.5 * (1.0 + tanh) + 0.5 * preact * (1.0 - tanh * tanh) * (
        root * (1.0 + (3 * 0.044715) * square)
    )
    produced = nn(hidden, down_ref[...])
    side_t = side.T
    counts_ref[...] = jnp.broadcast_to(
        jnp.sum(side_t[n_clips : 2 * n_clips], axis=1, keepdims=True) / capacity,
        (n_clips, LANES),
    )
    weights = (clip * gate).T[:n_clips].astype(bf16)
    high = produced.astype(bf16)
    low = (produced - high.astype(f32)).astype(bf16)
    pooled_ref[...] = base_ref[...] + (nn(weights, high) + nn(weights, low))


def loss_kernel(
    caps_dp, at_ref, pooled_ref, counts_ref, own_text_ref, other_text_ref, pairs_ref, teacher_ref,
    strip_ref, grad_ref, terms_ref, mean_ref, image_ref, d_image_ref,
):
    n_clips, width = pooled_ref.shape
    n_caps = teacher_ref.shape[1]
    half = width // 2
    own_at = pl.multiple_of(at_ref[1] * half, LANES)
    other_at = pl.multiple_of((1 - at_ref[1]) * half, LANES)
    own_dp = at_ref[2]
    counts = counts_ref[:, :1]
    clip_mean = pooled_ref[...] / counts
    img_scale = lax.rsqrt(jnp.sum(clip_mean * clip_mean, axis=1, keepdims=True) + norm_eps)
    image_emb = clip_mean * img_scale
    mean_ref[...] = clip_mean
    image_ref[...] = image_emb
    own_text = own_text_ref[...]
    other_text = other_text_ref[...]
    ones = jnp.ones((16, half), bf16)

    def squares(text):
        square = text.astype(f32) * text.astype(f32)
        high = square.astype(bf16)
        return nt(ones, high) + nt(ones, (square - high.astype(f32)).astype(bf16))

    text_scale = lax.rsqrt((squares(own_text) + squares(other_text))[:n_clips] + norm_eps)
    raw = fold3(
        nt(stack3(image_ref[:, pl.ds(own_at, half)]), own_text)
        + nt(stack3(image_ref[:, pl.ds(other_at, half)]), other_text)
    )
    order = (
        iota((n_caps, n_caps), 0) == (iota((n_caps, n_caps), 1) ^ (own_dp * caps_dp))
    ).astype(f32).astype(bf16)
    matched = (pairs_ref[...] == own_dp * n_clips + iota((n_clips, n_caps), 0)).astype(f32)
    target = fold3(nn(stack3(0.5 * matched + 0.5 * jax.nn.sigmoid(teacher_ref[...])), order))
    logits = logit_scale * raw * text_scale + logit_shift
    loss_grad = (jax.nn.sigmoid(logits) - target) * (counts / n_caps)
    scaled = loss_grad * text_scale
    scaled3 = stack3(scaled)
    d_image_ref[:, pl.ds(own_at, half)] = logit_scale * fold3(nn(scaled3, own_text))
    d_image_ref[:, pl.ds(other_at, half)] = logit_scale * fold3(nn(scaled3, other_text))
    d_image = d_image_ref[...]
    mean_grad = (
        img_scale * d_image
        - img_scale
        * img_scale
        * img_scale
        * jnp.sum(clip_mean * d_image, axis=1, keepdims=True)
        * clip_mean
    )
    grad_ref[...] = mean_grad / counts
    pick = strip_ref[...]
    emb_strip = fold3(nn(stack3(image_emb), pick))
    own_strip = strip_ref.at[pl.ds(own_at, half), :][...]
    other_strip = strip_ref.at[pl.ds(other_at, half), :][...]
    raw_strip = nn(own_text, own_strip) + nn(other_text, other_strip)
    dots = jnp.sum(loss_grad * raw, axis=0, keepdims=True)
    cube = text_scale[:1] * text_scale[:1] * text_scale[:1] * dots
    both = jnp.concatenate([scaled, jnp.broadcast_to(cube, scaled.shape)], axis=0)
    both = jnp.concatenate([both, jnp.zeros((LANES - both.shape[0], n_caps), f32)], axis=0).T
    left = both[:, :n_clips]
    products = lax.dot_general(
        left, emb_strip, (((1,), (0,)), ((), ())), precision=HIGHEST, preferred_element_type=f32
    )
    terms = logit_scale * (products - both[:, n_clips : n_clips + 1] * raw_strip)
    high = terms.astype(bf16)
    rest = terms - high.astype(f32)
    mid = rest.astype(bf16)
    low = (rest - mid.astype(f32)).astype(bf16)
    terms = nn(order, high) + (nn(order, mid) + nn(order, low))
    terms_ref[...] = terms.reshape(terms_ref.shape)


def backward_kernel(
    n_clips, at_ref, grad_ref, aux_ref, slope_ref, hidden_ref, down_ref, up_ref, router_ref,
    d_preact_ref, out_ref, part_ref, stacked_ref,
):
    rows, hid = hidden_ref.shape
    width = grad_ref.shape[1]
    half = width // 2
    expert = at_ref[0]
    other_at = pl.multiple_of((1 - at_ref[1]) * half, LANES)
    aux = aux_ref[...]
    lane = iota((rows, LANES), 1)
    clip = jnp.sum(jnp.where(lane < n_clips, aux * lane.astype(f32), 0.0), axis=1, keepdims=True)
    gate = aux[:, n_clips : n_clips + 1]
    gate_slope = aux[:, n_clips + 1 : n_clips + 2]
    lane3 = lane % n_clips
    thrice = ((lane3.astype(f32) == clip) & (lane < 3 * n_clips)).astype(f32).astype(bf16)
    grads = grad_ref[...]
    high = grads.astype(bf16).astype(f32)
    rest = grads - high
    mid = rest.astype(bf16).astype(f32)
    parts = jnp.concatenate(
        [high, mid, rest - mid, jnp.zeros((LANES - 3 * n_clips, width), f32)], axis=0
    ).astype(bf16)
    unit_dy = nn(thrice, parts)
    stacked_ref[:rows, :] = (gate * unit_dy).astype(bf16)
    stacked_ref[rows:, :] = jnp.concatenate([high, mid], axis=0).astype(bf16)
    d_all = nt(stacked_ref[...], down_ref[...])
    d_preact = (d_all[:rows] * slope_ref[...]).astype(bf16)
    d_preact_ref[...] = d_preact
    by_clip = d_all[rows : rows + n_clips] + d_all[rows + n_clips :]
    high_v = by_clip.astype(bf16).astype(f32)
    two = jnp.concatenate([high_v, by_clip - high_v], axis=0).astype(bf16)
    dots = nt(hidden_ref[...], two)
    lane2 = iota((rows, 2 * n_clips), 1) % n_clips
    token_dg = jnp.sum(
        jnp.where(lane2.astype(f32) == clip, dots, 0.0), axis=1, keepdims=True
    )
    part = token_dg * gate_slope
    part_ref[...] = jnp.broadcast_to(part, (rows, LANES))
    router = jnp.sum(
        jnp.where(
            iota((router_ref.shape[0], half), 0) == expert,
            router_ref[:, pl.ds(other_at, half)].astype(f32),
            0.0,
        ),
        axis=0,
        keepdims=True,
    )
    out_ref[...] = nt(d_preact, up_ref[pl.ds(other_at, half), :]) + part * router


def own_kernel(at_ref, d_preact_ref, part_ref, up_ref, router_ref, out_ref):
    half = out_ref.shape[1]
    expert = at_ref[0]
    own_at = pl.multiple_of(at_ref[1] * half, LANES)
    router = jnp.sum(
        jnp.where(
            iota((router_ref.shape[0], half), 0) == expert,
            router_ref[:, pl.ds(own_at, half)].astype(f32),
            0.0,
        ),
        axis=0,
        keepdims=True,
    )
    out_ref[...] = nt(d_preact_ref[...], up_ref[pl.ds(own_at, half), :]) + part_ref[:, :1] * router


def return_kernel(own_ref, other_ref, terms_ref, pay_ref):
    n_exp, capacity, _ = pay_ref.shape
    half = own_ref.shape[1]
    total = (own_ref[...] + other_ref[...]).reshape(n_exp, capacity, half)
    high = total.astype(bf16)
    pay_ref[:, :, :half] = high
    pay_ref[:, :, half : half + LOW] = (
        total[:, :, :LOW] - high[:, :, :LOW].astype(f32)
    ).astype(bf16)
    strip = jnp.sum(terms_ref[...], axis=0)
    strip_high = strip.astype(bf16).astype(f32)
    side = strip_high + pltpu.roll(strip - strip_high, LANES // 2, 1)
    pay_ref[:, :, half + LOW :] = jnp.broadcast_to(
        side.astype(bf16)[None], (n_exp, capacity, LANES)
    )


def final_kernel(strip, back_ref, placed_ref, dy_ref, out_ref, caps_ref):
    n_experts, _, capacity, wide = back_ref.shape
    half = wide - LOW - LANES
    placed = placed_ref[...]
    slots = n_experts * capacity

    def pick(h, start, size):
        part = back_ref[:, h, :, start : start + size]
        return nn(placed, part.astype(f32).reshape(slots, size).astype(bf16))

    for h in range(2):
        at = h * half
        high = pick(h, 0, half)
        out_ref[:, at : at + LOW] = dy_ref[:, at : at + LOW] + (
            high[:, :LOW] + pick(h, half, LOW)
        )
        out_ref[:, at + LOW : at + half] = dy_ref[:, at + LOW : at + half] + high[:, LOW:]
    lane = iota((capacity, LANES), 1)
    tiles = [jnp.zeros((capacity, LANES), f32) for _ in range(caps_ref.shape[1] // LANES)]
    for e in range(2 * n_experts):
        side = back_ref[e // 2, e % 2, :, half + LOW :].astype(f32)
        value = jnp.where(lane < strip, side + pltpu.roll(side, LANES // 2, 1), 0.0)
        tile, offset = divmod(e * strip, LANES)
        if offset:
            value = pltpu.roll(value, offset, 1)
        tiles[tile] = tiles[tile] + jnp.where(lane >= offset, value, 0.0)
        if offset + strip > LANES:
            tiles[tile + 1] = tiles[tile + 1] + jnp.where(lane < offset, value, 0.0)
    for t, value in enumerate(tiles):
        caps_ref[:, t * LANES : (t + 1) * LANES] = value


def shards(tokens, routes, pool_ids, w_router, w_up, w_down, captions, clip_pairs, teacher):
    tok_rows, width = tokens.shape
    n_experts = w_router.shape[1]
    n_clips, n_caps = teacher.shape
    hid = w_up.shape[1]
    n_dp = lax.axis_size("dp")
    n_exp = lax.axis_size("expert")
    caps_dp = n_caps // n_dp
    capacity = tok_rows // n_experts
    half = width // 2
    strip = width // n_exp
    rows = n_exp * capacity
    own = lax.axis_index("expert")
    own_dp = lax.axis_index("dp")
    core = own % 2
    at = jnp.stack([own // 2, core, own_dp]).astype(jnp.int32)
    at_spec = pl.BlockSpec(memory_space=pltpu.SMEM)
    swap = [(i, i ^ 1) for i in range(n_exp)]
    route_row = routes.reshape(1, tok_rows)
    router_t = w_router.T
    sds = jax.ShapeDtypeStruct

    def run(body, outs, operands, scratch=(), flops=0, moved=0):
        vmem = pl.BlockSpec(memory_space=pltpu.VMEM)
        return pl.pallas_call(
            body,
            out_shape=outs,
            in_specs=[at_spec if o is at else vmem for o in operands],
            out_specs=jax.tree.map(lambda _: vmem, outs),
            scratch_shapes=list(scratch),
            compiler_params=pltpu.CompilerParams(vmem_limit_bytes=32 * MIB),
            cost_estimate=pl.CostEstimate(flops=flops, bytes_accessed=moved, transcendentals=0),
        )(*operands)

    def after(x, *others):
        return lax.optimization_barrier((x,) + others)[0]

    def from_dp(x, mask):
        return lax.ppermute(x, "dp", [(i, i ^ mask) for i in range(n_dp)])

    send, base, placed = run(
        functools.partial(pack_kernel, capacity, n_experts, n_clips),
        [
            sds((n_experts, 2, capacity, half + LANES), bf16),
            sds((n_clips, width), f32),
            sds((tok_rows, n_experts * capacity), bf16),
        ],
        [tokens, route_row, pool_ids],
        flops=2 * tok_rows * tok_rows * width,
        moved=3 * tok_rows * width * 2,
    )
    block = after(lax.dynamic_slice_in_dim(captions, core * half, half, 1), send)
    blocks = [block] + [from_dp(block, mask) for mask in range(1, min(4, n_dp))]
    blocks = jnp.concatenate(blocks[: min(4, n_dp)])
    mask = 4
    if mask < n_dp:
        blocks = jnp.concatenate([blocks, from_dp(blocks, mask)])
        mask = 2 * mask

    recv = exchange(send.reshape(n_exp, capacity, half + LANES), "expert")
    other = lax.ppermute(recv, "expert", swap)
    if mask < n_dp:
        blocks = after(blocks, recv)
        blocks = jnp.concatenate([blocks, from_dp(blocks, mask)])
        mask = 2 * mask
    gelu_slope, hidden, aux, counts, pooled_part = run(
        functools.partial(forward_kernel, n_clips),
        [
            sds((rows, hid), f32),
            sds((rows, hid), bf16),
            sds((rows, LANES), f32),
            sds((n_clips, LANES), f32),
            sds((n_clips, width), f32),
        ],
        [at, recv, other, router_t, w_up, w_down, base],
        flops=4 * rows * width * hid,
        moved=4 * width * hid + 6 * rows * hid,
    )
    quarter = n_clips * width // n_exp
    parts = width // quarter
    pieces = pooled_part.reshape(n_clips, parts, quarter).transpose(1, 0, 2)
    pieces = pieces.reshape(n_exp, 1, quarter)
    if mask < n_dp:
        blocks = after(blocks, pieces)
        blocks = jnp.concatenate([blocks, from_dp(blocks, mask)])
        mask = 2 * mask
    piece = jnp.sum(exchange(pieces, "expert"), axis=0, keepdims=True)
    pooled = exchange(jnp.broadcast_to(piece, (n_exp, 1, quarter)), "expert")
    pooled = pooled.reshape(parts, n_clips, quarter).transpose(1, 0, 2).reshape(n_clips, width)
    other_blocks = lax.ppermute(blocks, "expert", swap)

    picks = (
        jnp.arange(width, dtype=jnp.int32)[:, None] - own * strip
        == jnp.arange(LANES, dtype=jnp.int32)[None, :]
    ) & (jnp.arange(LANES) < strip)[None, :]
    clip_grad, terms = run(
        functools.partial(loss_kernel, caps_dp),
        [sds((n_clips, width), f32), sds((n_dp, caps_dp, LANES), f32)],
        [
            at, pooled, counts, blocks, other_blocks, clip_pairs.reshape(1, n_caps), teacher,
            picks.astype(bf16),
        ],
        scratch=[pltpu.VMEM((n_clips, width), f32)] * 3,
        flops=8 * 24 * n_caps * width,
        moved=4 * n_caps * width,
    )
    terms = exchange(terms, "dp")

    d_preact, dx_other, part = run(
        functools.partial(backward_kernel, n_clips),
        [sds((rows, hid), bf16), sds((rows, half), f32), sds((rows, LANES), f32)],
        [at, clip_grad, aux, gelu_slope, hidden, w_down, w_up, router_t],
        scratch=[pltpu.VMEM((rows + 2 * n_clips, width), bf16)],
        flops=3 * rows * width * hid,
        moved=4 * width * hid + 6 * rows * hid,
    )
    from_other = lax.ppermute(dx_other, "expert", swap)
    dx_own = run(
        own_kernel,
        sds((rows, half), f32),
        [at, d_preact, part, w_up, router_t],
        flops=rows * width * hid,
        moved=width * hid + 6 * rows * hid,
    )
    pay = run(
        return_kernel,
        sds((n_exp, capacity, half + LOW + LANES), bf16),
        [dx_own, from_other, terms],
        flops=4 * rows * half,
        moved=12 * rows * half,
    )
    back = exchange(pay, "expert")
    members = (pool_ids[0][:, None] == jnp.arange(n_clips, dtype=jnp.int32)[None, :]).astype(f32)
    token_dy = jnp.dot(members, clip_grad, precision=HIGHEST)
    token_grads, caption_grads = run(
        functools.partial(final_kernel, strip),
        [sds((tok_rows, width), f32), sds((caps_dp, width), f32)],
        [back.reshape(n_experts, 2, capacity, half + LOW + LANES), placed, token_dy],
        flops=4 * tok_rows * tok_rows * width,
        moved=8 * tok_rows * width,
    )
    return (token_grads, caption_grads)


def solution(mesh):
    return jax.shard_map(
        shards,
        mesh=mesh,
        in_specs=(
            P(("dp", "expert"), None),
            P(("dp", "expert"), None),
            P("dp", "expert"),
            P(),
            P(None, "expert"),
            P("expert", None),
            P("dp", None),
            P(),
            P("dp", None),
        ),
        out_specs=(P(("dp", "expert"), None), P("dp", None)),
        check_vma=False,
    )
```

time: 532 us -> 172 us (0.32)
  waiting for transfers between devices: 232 us -> 39 us
  blocking collectives: 178 us -> 0 us
  matrix products: 32 us -> 0.45 us
  local copies, waits for them, and re-layouts: 5.65 us -> 30 us
  starting transfers between devices: 59.5 us -> 83 us
  Pallas kernels: 0 us -> 15.5 us
  between operations: 14.3 us -> 1.01 us
    reduce_scatter x1 -> x0, waiting for transfers between devices: 191 us -> none  [shards(): lax.psum_scatter(text_terms, 'dp', scatter_dimension=0, tiled=True)]
    psum x1 -> x0, blocking collectives: 102 us -> none  [shards(): pooled, counts = lax.psum((pooled_part, counts_part), 'expert')]
    all_gather x1 -> x0, blocking collectives: 75.8 us -> none  [caption_rows(): return lax.all_gather(captions, 'dp', axis=0, tiled=True)]
    ppermute x0 -> x9, starting transfers between devices: none -> 38.1 us  [the longest x6 30.1 us: from_dp(): return lax.ppermute(x, 'dp', [(i, i ^ mask) for i in range(n_dp)])]
    dot_general x18 -> x1, matrix products: 32 us -> 0.45 us  [shards(): token_dy = jnp.dot(members, clip_grad, precision=HIGHEST)]
    unnamed x24 -> x66, local copies, waits for them, and re-layouts: 2.22 us -> 25.5 us
    pallas_call x0 -> x7, Pallas kernels: none -> 15.5 us  [run(): pl.pallas_call(body, out_shape=outs, in_specs=[at_spec if o is at else vm...]
    all_to_all x5, starting transfers between devices: 59.5 us -> 44.9 us  [exchange(): return lax.all_to_all(x, axis, split_axis=0, concat_axis=0, tiled=True)]
  transfers between devices with their start and end apart: 6 -> 14, of which waited for: 5 -> 6; matrix products, arithmetic and copies ran while one was open for 4% -> 4% of each run, Pallas kernels for 0% -> 1%
where the time goes in v2:
time: 172 us; the launch traced here: 171 us
  starting transfers between devices  83 us (48%)
  waiting for transfers between devices  39 us (23%)
  local copies, waits for them, and re-layouts  30 us (17%)
  Pallas kernels  15.5 us (9%)
  other arithmetic  1.82 us (1%)
    all_to_all x5, starting transfers between devices, exchange(): return lax.all_to_all(x, axis, split_axis=0, concat_axis=0, tiled=True)  44.9 us
    all_to_all x5, waiting for transfers between devices, exchange(): return lax.all_to_all(x, axis, split_axis=0, concat_axis=0, tiled=True)  33.4 us
    ppermute x6, starting transfers between devices, from_dp(): return lax.ppermute(x, 'dp', [(i, i ^ mask) for i in range(n_dp)])  30.1 us
    unnamed x66, local copies, waits for them, and re-layouts  25.5 us
    pallas_call x7, Pallas kernels, run(): pl.pallas_call(body, out_shape=outs, in_specs=[at_spec if o is at else vm...  15.5 us
    ppermute x6, waiting for transfers between devices, from_dp(): return lax.ppermute(x, 'dp', [(i, i ^ mask) for i in range(n_dp)])  5.55 us
  transfers between devices with their start and end apart: 14, of which 6 were waited for; matrix products, arithmetic and copies ran while one was open for 4% of the time, Pallas kernels for 1%

profile of v2, /device:TPU:1, one launch (start us, length us, event | category | flops | bytes accessed | tf_op | source)
XLA Modules:
  0.0 170.7 jit_solution(4043323078814955546)
XLA Ops:
  2.9 1.1 shard_map.104
  4.1 17.7 %all-to-all-start = ((bf16[32,8,768]{2,1,0:T(8,128)(2,1)}), bf16[32,8,768]{2,1,0:T(8,128)(2,1)S(1)}, u32[]{:S(2)}, u32[]{:S(2)}) async-start(bf16[32,8,768]{2,1,0:T(8,128)(2,1)} %bitcast.4), calls=%async_computation | async-start | bytes 786432 | tf_op jit(solution)/shard_map/all_to_all | solution.py:21
  21.8 1.9 %collective-permute-start.3 = (bf16[8,640]{1,0:T(8,128)(2,1)S(1)}, bf16[8,640]{1,0:T(8,128)(2,1)S(1)}, u32[]{:S(2)}, u32[]{:S(2)}) collective-permute-start(bf16[8,640]{1,0:T(8,128)(2,1)S(1)} %constant_dynamic-slice_fusion), channel_id=1, source_target_pairs={{0,96},{32,64},{64,32},{96,0},{128,224},{160,192},{192,160},{224,1... | collective-permute-start | bytes 30728 | tf_op jit(solution)/shard_map/ppermute | solution.py:359
  23.7 1.9 %collective-permute-start.2 = (bf16[8,640]{1,0:T(8,128)(2,1)S(1)}, bf16[8,640]{1,0:T(8,128)(2,1)S(1)}, u32[]{:S(2)}, u32[]{:S(2)}) collective-permute-start(bf16[8,640]{1,0:T(8,128)(2,1)S(1)} %constant_dynamic-slice_fusion), channel_id=1, source_target_pairs={{0,64},{32,96},{64,0},{96,32},{128,192},{160,224},{192,128},{224,1... | collective-permute-start | bytes 30728 | tf_op jit(solution)/shard_map/ppermute | solution.py:359
  25.7 7.5 %collective-permute-start.1 = (bf16[8,640]{1,0:T(8,128)(2,1)S(1)}, bf16[8,640]{1,0:T(8,128)(2,1)S(1)}, u32[]{:S(2)}, u32[]{:S(2)}) collective-permute-start(bf16[8,640]{1,0:T(8,128)(2,1)S(1)} %constant_dynamic-slice_fusion), channel_id=1, source_target_pairs={{0,32},{32,0},{64,96},{96,64},{128,160},{160,128},{192,224},{224,1... | collective-permute-start | bytes 30728 | tf_op jit(solution)/shard_map/ppermute | solution.py:359
  33.3 1.3 collective-permute-done.1
  34.6 1.9 %collective-permute-start.4 = (bf16[32,640]{1,0:T(8,128)(2,1)S(1)}, bf16[32,640]{1,0:T(8,128)(2,1)S(1)}, u32[]{:S(2)}, u32[]{:S(2)}) collective-permute-start(bf16[32,640]{1,0:T(8,128)(2,1)S(1)} %pad_maximum_fusion.1), channel_id=1, source_target_pairs={{0,128},{32,160},{64,192},{96,224},{128,0},{160,32},{192,64},{224,... | collective-permute-start | bytes 122888 | tf_op jit(solution)/shard_map/ppermute | solution.py:359
  36.5 3.4 %collective-permute-start = (bf16[32,8,768]{2,1,0:T(8,128)(2,1)S(1)}, bf16[32,8,768]{2,1,0:T(8,128)(2,1)S(1)}, u32[]{:S(2)}, u32[]{:S(2)}) collective-permute-start(bf16[32,8,768]{2,1,0:T(8,128)(2,1)S(1)} %all-to-all-done.recv_ref), channel_id=1, source_target_pairs={{0,1},{1,0},{2,3},{3,2},{4,5},{5,4},{6,7},{7,6},{8,9},{9,8},{10,11... | collective-permute-start | bytes 1179656 | tf_op jit(solution)/shard_map/ppermute | solution.py:381
  40.0 5.4 %collective-permute-start.5 = (bf16[64,640]{1,0:T(8,128)(2,1)S(1)}, bf16[64,640]{1,0:T(8,128)(2,1)S(1)}, u32[]{:S(2)}, u32[]{:S(2)}) collective-permute-start(bf16[64,640]{1,0:T(8,128)(2,1)S(1)} %constant_dynamic-update-slice_fusion), channel_id=1, source_target_pairs={{0,256},{32,288},{64,320},{96,352},{128,384},{160,416},{192,448},{... | collective-permute-start | bytes 245768 | tf_op jit(solution)/shard_map/ppermute | solution.py:359
  45.5 4.3 %collective-permute-done.5 = bf16[64,640]{1,0:T(8,128)(2,1)S(1)} collective-permute-done((bf16[64,640]{1,0:T(8,128)(2,1)S(1)}, bf16[64,640]{1,0:T(8,128)(2,1)S(1)}, u32[]{:S(2)}, u32[]{:S(2)}) %collective-permute-start.5) | collective-permute-done | bytes 81952 | tf_op jit(solution)/shard_map/ppermute | solution.py:359
  50.5 1.9 %copy-done.1 = bf16[1280,1280]{1,0:T(8,128)(2,1)S(1)} copy-done((bf16[1280,1280]{1,0:T(8,128)(2,1)S(1)}, bf16[1280,1280]{1,0:T(8,128)(2,1)}, u32[]{:S(2)}) %copy-start.1) | copy-done | bytes 3276824
  52.4 1.9 %copy-done.3 = bf16[1280,1280]{1,0:T(8,128)(2,1)S(1)} copy-done((bf16[1280,1280]{1,0:T(8,128)(2,1)S(1)}, bf16[1280,1280]{1,0:T(8,128)(2,1)}, u32[]{:S(2)}) %copy-start.3) | copy-done | bytes 3276824
  56.1 3.5 %shard_map.105 = (f32[256,1280]{1,0:T(8,128)S(1)}, bf16[256,1280]{1,0:T(8,128)(2,1)S(1)}, f32[256,128]{1,0:T(8,128)S(1)}, f32[8,128]{1,0:T(8,128)S(1)}, f32[8,1280]{1,0:T(8,128)S(1)}) custom-call(s32[3]{0:T(128)S(1)} %pad_add_fusion.at_ref, bf16[32,8,768]{2,1,0:T(8,128)(2,1)S(1)} %copy-done.8, bf16[32,8,768]{2,1,0:T(8,128)(2,1)S(1)} %collective-permute-done.other_ref, ...), custom_call_target="tpu_custom_call" | custom-call | flops 1677721600 | bytes 8519680 | tf_op jit(solution)/shard_map/pallas_call | solution.py:345
  63.8 11.4 %collective-permute-start.6 = (bf16[128,640]{1,0:T(8,128)(2,1)}, bf16[128,640]{1,0:T(8,128)(2,1)}, u32[]{:S(2)}, u32[]{:S(2)}) collective-permute-start(bf16[128,640]{1,0:T(8,128)(2,1)} %pad_maximum_fusion), channel_id=1, source_target_pairs={{0,512},{32,544},{64,576},{96,608},{128,640},{160,672},{192,704},{... | collective-permute-start | bytes 491528 | tf_op jit(solution)/shard_map/ppermute | solution.py:359
  75.9 8.7 %all-to-all-start.1 = ((f32[32,1,320]{2,1,0:T(1,128)}), f32[32,1,320]{2,1,0:T(1,128)S(1)}, u32[]{:S(2)}, u32[]{:S(2)}) async-start(f32[32,1,320]{2,1,0:T(1,128)} %copy.14), calls=%async_computation.1 | async-start | bytes 98304 | tf_op jit(solution)/shard_map/all_to_all | solution.py:21
  84.6 1.6 constant_dynamic-update-slice_fusion.6
  86.2 6.5 %all-to-all-done.1 = f32[32,1,320]{2,1,0:T(1,128)S(1)} async-done(((f32[32,1,320]{2,1,0:T(1,128)}), f32[32,1,320]{2,1,0:T(1,128)S(1)}, u32[]{:S(2)}, u32[]{:S(2)}) %all-to-all-start.1) | async-done | bytes 40992 | tf_op jit(solution)/shard_map/all_to_all | solution.py:21
  93.4 3.9 %all-to-all-start.2 = ((f32[32,1,320]{2,1,0:T(1,128)}), f32[32,1,320]{2,1,0:T(1,128)S(1)}, u32[]{:S(2)}, u32[]{:S(2)}) async-start(f32[32,1,320]{2,1,0:T(1,128)} %broadcast_in_dim.2), calls=%async_computation.2 | async-start | bytes 98304 | tf_op jit(solution)/shard_map/all_to_all | solution.py:21
  97.3 1.6 constant_dynamic-update-slice_fusion.5.own_text_ref
  98.9 2.2 %collective-permute-start.7 = (bf16[256,640]{1,0:T(8,128)(2,1)}, bf16[256,640]{1,0:T(8,128)(2,1)}, u32[]{:S(2)}, u32[]{:S(2)}) collective-permute-start(bf16[256,640]{1,0:T(8,128)(2,1)} %constant_dynamic-update-slice_fusion.5.own_text_ref), channel_id=1, source_target_pairs={{0,1},{1,0},{2,3},{3,2},{4,5},{5,4},{6,7},{7,6},{8,9},{9,8},{10,11... | collective-permute-start | bytes 983048 | tf_op jit(solution)/shard_map/ppermute | solution.py:410
  102.1 3.4 %all-to-all-done.2 = f32[32,1,320]{2,1,0:T(1,128)S(1)} async-done(((f32[32,1,320]{2,1,0:T(1,128)}), f32[32,1,320]{2,1,0:T(1,128)S(1)}, u32[]{:S(2)}, u32[]{:S(2)}) %all-to-all-start.2) | async-done | bytes 40992 | tf_op jit(solution)/shard_map/all_to_all | solution.py:21
  107.7 2.8 %shard_map.106 = (f32[8,1280]{1,0:T(8,128)S(1)}, f32[32,8,128]{2,1,0:T(8,128)S(1)}) custom-call(s32[3]{0:T(128)S(1)} %pad_add_fusion.at_ref, f32[8,1280]{1,0:T(8,128)S(1)} %reshape.48.pooled_ref, f32[8,128]{1,0:T(8,128)S(1)} %get-tuple-element.21.counts_ref, bf16[256,640]{1,0:T(8,128)(2,1)S(1)} %copy-done.12, ...), custom_call_target="tpu_custom_call" | custom-call | flops 62914560 | bytes 1310720 | tf_op jit(solution)/shard_map/pallas_call | solution.py:345
  111.2 1.9 %copy-done.4 = bf16[1280,1280]{1,0:T(8,128)(2,1)S(1)} copy-done((bf16[1280,1280]{1,0:T(8,128)(2,1)S(1)}, bf16[1280,1280]{1,0:T(8,128)(2,1)}, u32[]{:S(2)}) %copy-start.4) | copy-done | bytes 3276824
  113.1 1.3 copy-done.10
  116.4 3.5 %shard_map.107 = (bf16[256,1280]{1,0:T(8,128)(2,1)S(1)}, f32[256,640]{1,0:T(8,128)}, f32[256,128]{1,0:T(8,128)S(1)}) custom-call(s32[3]{0:T(128)S(1)} %pad_add_fusion.at_ref, f32[8,1280]{1,0:T(8,128)S(1)} %get-tuple-element.25.grad_ref, f32[256,128]{1,0:T(8,128)S(1)} %copy-done.21, f32[256,1280]{1,0:T(8,128)S(1)} %copy-done.10, ...), custom_call_target="tpu_custom_call" | custom-call | flops 1258291200 | bytes 8519680 | tf_op jit(solution)/shard_map/pallas_call | solution.py:345
  121.4 2.3 %collective-permute-start.8 = (f32[256,640]{1,0:T(8,128)}, f32[256,640]{1,0:T(8,128)}, u32[]{:S(2)}, u32[]{:S(2)}) collective-permute-start(f32[256,640]{1,0:T(8,128)} %get-tuple-element.31), channel_id=1, source_target_pairs={{0,1},{1,0},{2,3},{3,2},{4,5},{5,4},{6,7},{7,6},{8,9},{9,8},{10,11... | collective-permute-start | bytes 1966088 | tf_op jit(solution)/shard_map/ppermute | solution.py:437
  123.7 7.6 %all-to-all-start.3 = ((f32[32,8,128]{2,1,0:T(8,128)}), f32[32,8,128]{2,1,0:T(8,128)S(1)}, u32[]{:S(2)}, u32[]{:S(2)}) async-start(f32[32,8,128]{2,1,0:T(8,128)} %copy-done.24), calls=%async_computation.3 | async-start | bytes 262144 | tf_op jit(solution)/shard_map/all_to_all | solution.py:21
  133.3 1.2 shard_map.108.own_ref
  135.5 7.2 %all-to-all-done.3.terms_ref = f32[32,8,128]{2,1,0:T(8,128)S(1)} async-done(((f32[32,8,128]{2,1,0:T(8,128)}), f32[32,8,128]{2,1,0:T(8,128)S(1)}, u32[]{:S(2)}, u32[]{:S(2)}) %all-to-all-start.3) | async-done | bytes 131104 | tf_op jit(solution)/shard_map/all_to_all | solution.py:21
  143.7 2.2 %shard_map.109 = bf16[32,8,1024]{2,1,0:T(8,128)(2,1)} custom-call(f32[256,640]{1,0:T(8,128)S(1)} %copy-done.6, f32[256,640]{1,0:T(8,128)} %collective-permute-done.8.other_ref, f32[32,8,128]{2,1,0:T(8,128)S(1)} %all-to-all-done.3.terms_ref), custom_call_target="tpu_custom_call" | custom-call | flops 655360 | bytes 1966080 | tf_op jit(solution)/shard_map/pallas_call | solution.py:345
  145.9 7.0 %all-to-all-start.4 = ((bf16[32,8,1024]{2,1,0:T(8,128)(2,1)}), bf16[32,8,1024]{2,1,0:T(8,128)(2,1)S(1)}, u32[]{:S(2)}, u32[]{:S(2)}) async-start(bf16[32,8,1024]{2,1,0:T(8,128)(2,1)} %shard_map.109), calls=%async_computation.4 | async-start | bytes 1048576 | tf_op jit(solution)/shard_map/all_to_all | solution.py:21
  153.4 16.2 %all-to-all-done.4 = bf16[32,8,1024]{2,1,0:T(8,128)(2,1)S(1)} async-done(((bf16[32,8,1024]{2,1,0:T(8,128)(2,1)}), bf16[32,8,1024]{2,1,0:T(8,128)(2,1)S(1)}, u32[]{:S(2)}, u32[]{:S(2)}) %all-to-all-start.4) | async-done | bytes 524320 | tf_op jit(solution)/shard_map/all_to_all | solution.py:21
  (86 shorter events, 23.1 us)
Async XLA Ops:
  0.6 21.1 %copy-start = (bf16[8,1280]{1,0:T(8,128)(2,1)S(1)}, bf16[8,1280]{1,0:T(8,128)(2,1)}, u32[]{:S(2)}) copy-start(bf16[8,1280]{1,0:T(8,128)(2,1)} %param.15) | copy-start | bytes 61444
  0.6 1.0 copy-start.19
  4.1 32.4 %all-to-all-start = ((bf16[32,8,768]{2,1,0:T(8,128)(2,1)}), bf16[32,8,768]{2,1,0:T(8,128)(2,1)S(1)}, u32[]{:S(2)}, u32[]{:S(2)}) async-start(bf16[32,8,768]{2,1,0:T(8,128)(2,1)} %bitcast.4), calls=%async_computation | async-start | bytes 786432 | tf_op jit(solution)/shard_map/all_to_all | solution.py:21
  21.8 11.5 %collective-permute-start.3 = (bf16[8,640]{1,0:T(8,128)(2,1)S(1)}, bf16[8,640]{1,0:T(8,128)(2,1)S(1)}, u32[]{:S(2)}, u32[]{:S(2)}) collective-permute-start(bf16[8,640]{1,0:T(8,128)(2,1)S(1)} %constant_dynamic-slice_fusion), channel_id=1, source_target_pairs={{0,96},{32,64},{64,32},{96,0},{128,224},{160,192},{192,160},{224,1... | collective-permute-start | bytes 30728 | tf_op jit(solution)/shard_map/ppermute | solution.py:359
  23.7 9.5 %collective-permute-start.2 = (bf16[8,640]{1,0:T(8,128)(2,1)S(1)}, bf16[8,640]{1,0:T(8,128)(2,1)S(1)}, u32[]{:S(2)}, u32[]{:S(2)}) collective-permute-start(bf16[8,640]{1,0:T(8,128)(2,1)S(1)} %constant_dynamic-slice_fusion), channel_id=1, source_target_pairs={{0,64},{32,96},{64,0},{96,32},{128,192},{160,224},{192,128},{224,1... | collective-permute-start | bytes 30728 | tf_op jit(solution)/shard_map/ppermute | solution.py:359
  25.7 8.9 %collective-permute-start.1 = (bf16[8,640]{1,0:T(8,128)(2,1)S(1)}, bf16[8,640]{1,0:T(8,128)(2,1)S(1)}, u32[]{:S(2)}, u32[]{:S(2)}) collective-permute-start(bf16[8,640]{1,0:T(8,128)(2,1)S(1)} %constant_dynamic-slice_fusion), channel_id=1, source_target_pairs={{0,32},{32,0},{64,96},{96,64},{128,160},{160,128},{192,224},{224,1... | collective-permute-start | bytes 30728 | tf_op jit(solution)/shard_map/ppermute | solution.py:359
  34.6 5.4 %collective-permute-start.4 = (bf16[32,640]{1,0:T(8,128)(2,1)S(1)}, bf16[32,640]{1,0:T(8,128)(2,1)S(1)}, u32[]{:S(2)}, u32[]{:S(2)}) collective-permute-start(bf16[32,640]{1,0:T(8,128)(2,1)S(1)} %pad_maximum_fusion.1), channel_id=1, source_target_pairs={{0,128},{32,160},{64,192},{96,224},{128,0},{160,32},{192,64},{224,... | collective-permute-start | bytes 122888 | tf_op jit(solution)/shard_map/ppermute | solution.py:359
  36.5 14.0 %copy-start.7 = (bf16[32,8,768]{2,1,0:T(8,128)(2,1)}, bf16[32,8,768]{2,1,0:T(8,128)(2,1)S(1)}, u32[]{:S(2)}) copy-start(bf16[32,8,768]{2,1,0:T(8,128)(2,1)S(1)} %all-to-all-done.recv_ref) | copy-start | bytes 1179652
  36.5 14.0 %collective-permute-start = (bf16[32,8,768]{2,1,0:T(8,128)(2,1)S(1)}, bf16[32,8,768]{2,1,0:T(8,128)(2,1)S(1)}, u32[]{:S(2)}, u32[]{:S(2)}) collective-permute-start(bf16[32,8,768]{2,1,0:T(8,128)(2,1)S(1)} %all-to-all-done.recv_ref), channel_id=1, source_target_pairs={{0,1},{1,0},{2,3},{3,2},{4,5},{5,4},{6,7},{7,6},{8,9},{9,8},{10,11... | collective-permute-start | bytes 1179656 | tf_op jit(solution)/shard_map/ppermute | solution.py:381
  40.0 9.8 %collective-permute-start.5 = (bf16[64,640]{1,0:T(8,128)(2,1)S(1)}, bf16[64,640]{1,0:T(8,128)(2,1)S(1)}, u32[]{:S(2)}, u32[]{:S(2)}) collective-permute-start(bf16[64,640]{1,0:T(8,128)(2,1)S(1)} %constant_dynamic-update-slice_fusion), channel_id=1, source_target_pairs={{0,256},{32,288},{64,320},{96,352},{128,384},{160,416},{192,448},{... | collective-permute-start | bytes 245768 | tf_op jit(solution)/shard_map/ppermute | solution.py:359
  50.5 1.9 %copy-start.1 = (bf16[1280,1280]{1,0:T(8,128)(2,1)S(1)}, bf16[1280,1280]{1,0:T(8,128)(2,1)}, u32[]{:S(2)}) copy-start(bf16[1280,1280]{1,0:T(8,128)(2,1)} %up_ref.5) | copy-start | bytes 9830404
  52.4 1.9 %copy-start.3 = (bf16[1280,1280]{1,0:T(8,128)(2,1)S(1)}, bf16[1280,1280]{1,0:T(8,128)(2,1)}, u32[]{:S(2)}) copy-start(bf16[1280,1280]{1,0:T(8,128)(2,1)} %down_ref.3) | copy-start | bytes 9830404
  54.3 1.0 copy-start.8
  56.1 49.6 %copy-start.25 = (f32[8,256]{1,0:T(8,128)S(1)}, f32[8,256]{1,0:T(8,128)}, u32[]{:S(2)}) copy-start(f32[8,256]{1,0:T(8,128)} %teacher_ref.1) | copy-start | bytes 24580
  56.1 49.6 %copy-start.28 = (s32[256]{0:T(256)S(1)}, s32[256]{0:T(256)}, u32[]{:S(2)}) copy-start(s32[256]{0:T(256)} %param.16) | copy-start | bytes 3076
  56.1 55.1 %copy-start.2 = (bf16[1280,1280]{1,0:T(8,128)(2,1)S(1)}, bf16[1280,1280]{1,0:T(8,128)(2,1)}, u32[]{:S(2)}) copy-start(bf16[1280,1280]{1,0:T(8,128)(2,1)} %up_ref.5) | copy-start | bytes 9830404
  56.1 55.1 %copy-start.18 = (bf16[1280,16]{0,1:T(8,128)(2,1)S(1)}, bf16[1280,16]{0,1:T(8,128)(2,1)}, u32[]{:S(2)}) copy-start(bf16[1280,16]{0,1:T(8,128)(2,1)} %param.12) | copy-start | bytes 122884
  59.6 1.1 copy-start.9
  63.8 33.5 %collective-permute-start.6 = (bf16[128,640]{1,0:T(8,128)(2,1)}, bf16[128,640]{1,0:T(8,128)(2,1)}, u32[]{:S(2)}, u32[]{:S(2)}) collective-permute-start(bf16[128,640]{1,0:T(8,128)(2,1)} %pad_maximum_fusion), channel_id=1, source_target_pairs={{0,512},{32,544},{64,576},{96,608},{128,640},{160,672},{192,704},{... | collective-permute-start | bytes 491528 | tf_op jit(solution)/shard_map/ppermute | solution.py:359
  75.9 16.9 %all-to-all-start.1 = ((f32[32,1,320]{2,1,0:T(1,128)}), f32[32,1,320]{2,1,0:T(1,128)S(1)}, u32[]{:S(2)}, u32[]{:S(2)}) async-start(f32[32,1,320]{2,1,0:T(1,128)} %copy.14), calls=%async_computation.1 | async-start | bytes 98304 | tf_op jit(solution)/shard_map/all_to_all | solution.py:21
  93.4 12.2 %all-to-all-start.2 = ((f32[32,1,320]{2,1,0:T(1,128)}), f32[32,1,320]{2,1,0:T(1,128)S(1)}, u32[]{:S(2)}, u32[]{:S(2)}) async-start(f32[32,1,320]{2,1,0:T(1,128)} %broadcast_in_dim.2), calls=%async_computation.2 | async-start | bytes 98304 | tf_op jit(solution)/shard_map/all_to_all | solution.py:21
  98.9 6.8 %collective-permute-start.7 = (bf16[256,640]{1,0:T(8,128)(2,1)}, bf16[256,640]{1,0:T(8,128)(2,1)}, u32[]{:S(2)}, u32[]{:S(2)}) collective-permute-start(bf16[256,640]{1,0:T(8,128)(2,1)} %constant_dynamic-update-slice_fusion.5.own_text_ref), channel_id=1, source_target_pairs={{0,1},{1,0},{2,3},{3,2},{4,5},{5,4},{6,7},{7,6},{8,9},{9,8},{10,11... | collective-permute-start | bytes 983048 | tf_op jit(solution)/shard_map/ppermute | solution.py:410
  105.7 1.0 copy-start.11
  111.2 1.9 %copy-start.4 = (bf16[1280,1280]{1,0:T(8,128)(2,1)S(1)}, bf16[1280,1280]{1,0:T(8,128)(2,1)}, u32[]{:S(2)}) copy-start(bf16[1280,1280]{1,0:T(8,128)(2,1)} %down_ref.3) | copy-start | bytes 9830404
  113.1 1.3 copy-start.10
  114.4 1.1 copy-start.14
  121.4 21.2 %collective-permute-start.8 = (f32[256,640]{1,0:T(8,128)}, f32[256,640]{1,0:T(8,128)}, u32[]{:S(2)}, u32[]{:S(2)}) collective-permute-start(f32[256,640]{1,0:T(8,128)} %get-tuple-element.31), channel_id=1, source_target_pairs={{0,1},{1,0},{2,3},{3,2},{4,5},{5,4},{6,7},{7,6},{8,9},{9,8},{10,11... | collective-permute-start | bytes 1966088 | tf_op jit(solution)/shard_map/ppermute | solution.py:437
  123.7 18.9 %all-to-all-start.3 = ((f32[32,8,128]{2,1,0:T(8,128)}), f32[32,8,128]{2,1,0:T(8,128)S(1)}, u32[]{:S(2)}, u32[]{:S(2)}) async-start(f32[32,8,128]{2,1,0:T(8,128)} %copy-done.24), calls=%async_computation.3 | async-start | bytes 262144 | tf_op jit(solution)/shard_map/all_to_all | solution.py:21
  131.4 1.1 copy-start.16
  133.3 19.5 %copy-start.27 = (s32[1,128]{1,0:T(1,128)S(1)}, s32[1,128]{1,0:T(1,128)}, u32[]{:S(2)}) copy-start(s32[1,128]{1,0:T(1,128)} %pool_ref.1) | copy-start | bytes 1540
  142.6 1.1 copy-start.6
  145.9 23.7 %all-to-all-start.4 = ((bf16[32,8,1024]{2,1,0:T(8,128)(2,1)}), bf16[32,8,1024]{2,1,0:T(8,128)(2,1)S(1)}, u32[]{:S(2)}, u32[]{:S(2)}) async-start(bf16[32,8,1024]{2,1,0:T(8,128)(2,1)} %shard_map.109), calls=%async_computation.4 | async-start | bytes 1048576 | tf_op jit(solution)/shard_map/all_to_all | solution.py:21
  (12 other events, 9.4 us)

commit v3 on v2

v3 whole, which is shorter than its diff:
```python
import functools
import jax
import jax.numpy as jnp
from jax import lax
from jax.experimental import pallas as pl
from jax.experimental.pallas import tpu as pltpu
from jax.sharding import PartitionSpec as P

HIGHEST = lax.Precision.HIGHEST
logit_scale = 10.0
logit_shift = -10.0
norm_eps = 1e-06
f32 = jnp.float32
bf16 = jnp.bfloat16
LANES = 128
LOW = 256
MIB = 1 << 20
OWN_FLOPS = 10_000_000_000


def exchange(x, axis):
    return lax.all_to_all(x, axis, split_axis=0, concat_axis=0, tiled=True)


class Late:
    def __init__(self, copy, ref):
        self.copy, self.ref, self.waited = copy, ref, False
        copy.start()

    def ready(self):
        if not self.waited:
            self.copy.wait()
            self.waited = True
        return self.ref


class Leaving:
    def __init__(self, copy, ref):
        self.copy, self.ref, self.sent = copy, ref, False

    def send(self, value):
        self.ref[...] = value
        self.copy.start()
        self.sent = True


def iota(shape, axis):
    return lax.broadcasted_iota(jnp.int32, shape, axis)


def nn(a, b):
    return lax.dot_general(a, b, (((1,), (0,)), ((), ())), preferred_element_type=f32)


def nt(a, b):
    return lax.dot_general(a, b, (((1,), (1,)), ((), ())), preferred_element_type=f32)


def stack3(x):
    high = x.astype(bf16).astype(f32)
    rest = x - high
    mid = rest.astype(bf16).astype(f32)
    return jnp.concatenate([high, mid, rest - mid], axis=0).astype(bf16)


def fold3(x):
    rows = x.shape[0] // 3
    return x[:rows] + (x[rows : 2 * rows] + x[2 * rows :])


def slot_matrix(route_row, capacity, n_experts):
    toks = route_row.shape[1]
    chosen = (iota((n_experts, toks), 0) == route_row).astype(f32)
    earlier = (iota((toks, toks), 0) < iota((toks, toks), 1)).astype(f32).astype(bf16)
    before = nn(chosen.astype(bf16), earlier)
    arrival = jnp.sum(before * chosen, axis=0, keepdims=True)
    slot = route_row.astype(f32) * capacity + arrival
    slot = jnp.where(arrival < capacity, slot, -1.0)
    return (iota((n_experts * capacity, toks), 0).astype(f32) == slot).astype(f32)


def pack_kernel(capacity, n_experts, n_clips, route, pool, tok, send_ref, base_ref, placed_ref):
    toks, width = tok.ref.shape
    half = width // 2
    placed_t = slot_matrix(route.ready()[...], capacity, n_experts)
    placed_ref[...] = placed_t.T.astype(bf16)
    placed_t = placed_t.astype(bf16)
    pool = pool.ready()[...]
    ids = iota((LANES, toks), 0)
    members = (ids == pool).astype(f32)
    counted = (ids - n_clips == pool).astype(f32).astype(bf16)
    side = nt(placed_t, members.astype(bf16)) + nt(
        jnp.ones((n_experts * capacity, toks), bf16), counted
    )
    side = side.reshape(n_experts, capacity, LANES).astype(bf16)
    tokens = tok.ready()[...]
    rows = nn(placed_t, tokens)
    for h in range(2):
        send_ref[:, h, :, :half] = (
            rows[:, h * half : (h + 1) * half].reshape(n_experts, capacity, half).astype(bf16)
        )
        send_ref[:, h, :, half:] = side
    base_ref[...] = nn(members[:n_clips].astype(bf16), tokens)


def cut_strip(tiles, e, strip):
    tile, offset = divmod(e * strip, LANES)
    lane = iota(tiles[0].shape, 1)
    value = tiles[tile]
    if offset + strip > LANES:
        value = jnp.where(lane >= offset, value, tiles[tile + 1])
    if offset:
        value = pltpu.roll(value, LANES - offset, 1)
    return jnp.where(lane < strip, value, 0.0)


def join_strips(strips, strip, n_tiles):
    lane = iota(strips[0].shape, 1)
    tiles = [jnp.zeros(strips[0].shape, f32) for _ in range(n_tiles)]
    for e, value in enumerate(strips):
        tile, offset = divmod(e * strip, LANES)
        if offset:
            value = pltpu.roll(value, offset, 1)
        if offset + strip > LANES:
            tiles[tile] = tiles[tile] + jnp.where(lane >= offset, value, 0.0)
            tiles[tile + 1] = tiles[tile + 1] + jnp.where(lane < offset, value, 0.0)
        else:
            tiles[tile] = tiles[tile] + value
    return tiles


def spread3(value, strip):
    high = value.astype(bf16).astype(f32)
    rest = value - high
    mid = rest.astype(bf16).astype(f32)
    return high + pltpu.roll(mid, strip, 1) + pltpu.roll(rest - mid, 2 * strip, 1)


def gather3(value, strip):
    lane = iota(value.shape, 1)
    low = pltpu.roll(value, LANES - 2 * strip, 1)
    mid = pltpu.roll(value, LANES - strip, 1)
    return jnp.where(lane < strip, value + (mid + low), 0.0)


def forward_kernel(
    n_clips, strip, at_ref, recv, other, router, up, block, down, base, slope, hidden_out, aux_out, counts, pay_ref,
):
    n_exp, capacity, wide = recv.ref.shape
    half = wide - LANES
    rows = n_exp * capacity
    n_experts = router.ref.shape[0]
    expert = at_ref[0]
    own_at = pl.multiple_of(at_ref[1] * half, LANES)
    other_at = pl.multiple_of((1 - at_ref[1]) * half, LANES)
    recv_ref = recv.ready()
    own = recv_ref[:, :, :half].astype(f32).reshape(rows, half).astype(bf16)
    side = recv_ref[:, :, half:].astype(f32).reshape(rows, LANES)
    other_rows = other.ready()[:, :, :half].astype(f32).reshape(rows, half).astype(bf16)
    router_ref = router.ready()
    scores = nt(own, router_ref[:, pl.ds(own_at, half)]) + nt(
        other_rows, router_ref[:, pl.ds(other_at, half)]
    )
    mine = iota((rows, n_experts), 1) == expert
    score = jnp.sum(jnp.where(mine, scores, 0.0), axis=1, keepdims=True)
    sigmoid_gate = jax.nn.sigmoid(score)
    gate = sigmoid_gate.astype(bf16).astype(f32)
    lane = iota((rows, LANES), 1)
    clip = jnp.where(lane < n_clips, side, 0.0)
    aux_out.send(
        jnp.where(
            lane == n_clips,
            gate,
            jnp.where(lane == n_clips + 1, sigmoid_gate * (1.0 - sigmoid_gate), clip),
        )
    )
    side_t = side.T
    counts.send(
        jnp.broadcast_to(
            jnp.sum(side_t[n_clips : 2 * n_clips], axis=1, keepdims=True) / capacity,
            (n_clips, LANES),
        )
    )
    weights = (clip * gate).T[:n_clips].astype(bf16)
    up_ref = up.ready()
    preact = nn(own, up_ref[pl.ds(own_at, half), :]) + nn(
        other_rows, up_ref[pl.ds(other_at, half), :]
    )
    root = 0.7978845608028654
    square = preact * preact
    tanh = jnp.tanh(root * (preact + 0.044715 * (square * preact)))
    hidden = (preact * (0.5 * (1.0 + tanh))).astype(bf16)
    hidden_out.send(hidden)
    slope.send(
        0.5 * (1.0 + tanh)
        + 0.5 * preact * (1.0 - tanh * tanh) * (root * (1.0 + (3 * 0.044715) * square))
    )
    captions = block.ready()
    for h in range(2):
        pay_ref[:, h, :, :half] = jnp.broadcast_to(
            captions[:, h * half : (h + 1) * half][None], (n_exp // 2, captions.shape[0], half)
        )
    produced = nn(hidden, down.ready()[...])
    high = produced.astype(bf16)
    low = (produced - high.astype(f32)).astype(bf16)
    pooled = base.ready()[...] + (nn(weights, high) + nn(weights, low))
    tiles = [pooled[:, t * LANES : (t + 1) * LANES] for t in range(pooled.shape[1] // LANES)]
    for e in range(n_exp):
        pay_ref[e // 2, e % 2, :, half:] = spread3(cut_strip(tiles, e, strip), strip).astype(bf16)


def sum_kernel(strip, side, out_ref):
    total = jnp.sum(side.ready()[...].astype(f32), axis=0)
    total = spread3(gather3(total, strip), strip).astype(bf16)
    out_ref[...] = jnp.broadcast_to(total[None], out_ref.shape)


def loss_kernel(
    strip, at_ref, sums_ref, counts, own, other, pairs, teacher, grad_out, terms_out,
    mean_ref, image_ref, d_image_ref, text_ref,
):
    n_exp, n_clips, wide = own.ref.shape
    n_caps = teacher.ref.shape[1]
    half = wide - LANES
    width = 2 * half
    own_at = pl.multiple_of(at_ref[1] * half, LANES)
    other_at = pl.multiple_of((1 - at_ref[1]) * half, LANES)
    own_dp = at_ref[2]
    n_tiles = width // LANES
    tiles = join_strips(
        [gather3(sums_ref[e].astype(f32), strip) for e in range(n_exp)], strip, n_tiles
    )
    counts = counts.ready()[:, :1]
    for t, tile in enumerate(tiles):
        mean_ref[:, t * LANES : (t + 1) * LANES] = tile / counts
    clip_mean = mean_ref[...]
    img_scale = lax.rsqrt(jnp.sum(clip_mean * clip_mean, axis=1, keepdims=True) + norm_eps)
    image_emb = clip_mean * img_scale
    image_ref[...] = image_emb
    own_text = own.ready()[:, :, :half].astype(f32).reshape(n_caps, half)
    other_text = other.ready()[:, :, :half].astype(f32).reshape(n_caps, half)
    ones = jnp.ones((16, half), bf16)

    def squares(text):
        square = text * text
        high = square.astype(bf16)
        return nt(ones, high) + nt(ones, (square - high.astype(f32)).astype(bf16))

    text_scale = lax.rsqrt((squares(own_text) + squares(other_text))[:n_clips] + norm_eps)
    own_text = own_text.astype(bf16)
    other_text = other_text.astype(bf16)
    text_ref[:, pl.ds(own_at, half)] = own_text
    text_ref[:, pl.ds(other_at, half)] = other_text
    text = text_ref[...]
    raw = fold3(nt(stack3(image_emb), text))
    matched = (
        pairs.ready()[...] == own_dp * n_clips + iota((n_clips, n_caps), 0)
    ).astype(f32)
    target = 0.5 * matched + 0.5 * jax.nn.sigmoid(teacher.ready()[...])
    logits = logit_scale * raw * text_scale + logit_shift
    loss_grad = (jax.nn.sigmoid(logits) - target) * (counts / n_caps)
    scaled = loss_grad * text_scale
    d_image = logit_scale * fold3(nn(stack3(scaled), text))
    mean_grad = (
        img_scale * d_image
        - img_scale
        * img_scale
        * img_scale
        * jnp.sum(clip_mean * d_image, axis=1, keepdims=True)
        * clip_mean
    )
    grad_out.send(mean_grad / counts)
    pick = (
        (iota((width, LANES), 0) - at_ref[3] * strip == iota((width, LANES), 1))
        & (iota((width, LANES), 1) < strip)
    ).astype(f32).astype(bf16)
    emb_strip = fold3(nn(stack3(image_emb), pick))
    raw_strip = nn(text, pick)
    dots = jnp.sum(loss_grad * raw, axis=0, keepdims=True)
    cube = text_scale[:1] * text_scale[:1] * text_scale[:1] * dots
    both = jnp.concatenate([scaled, jnp.broadcast_to(cube, scaled.shape)], axis=0)
    both = jnp.concatenate([both, jnp.zeros((LANES - both.shape[0], n_caps), f32)], axis=0).T
    products = lax.dot_general(
        both[:, :n_clips], emb_strip, (((1,), (0,)), ((), ())),
        precision=HIGHEST, preferred_element_type=f32,
    )
    terms = logit_scale * (products - both[:, n_clips : n_clips + 1] * raw_strip)
    terms_out.send(terms.reshape(terms_out.ref.shape))


def backward_kernel(
    n_clips, at_ref, grad, aux, down, slope, hidden, router, up,
    d_preact_out, out, part_out, stacked_ref,
):
    rows, hid = hidden.ref.shape
    width = grad.ref.shape[1]
    half = width // 2
    expert = at_ref[0]
    other_at = pl.multiple_of((1 - at_ref[1]) * half, LANES)
    grads = grad.ready()[...]
    aux = aux.ready()[...]
    lane = iota((rows, LANES), 1)
    clip = jnp.sum(jnp.where(lane < n_clips, aux * lane.astype(f32), 0.0), axis=1, keepdims=True)
    gate = aux[:, n_clips : n_clips + 1]
    gate_slope = aux[:, n_clips + 1 : n_clips + 2]
    lane3 = lane % n_clips
    thrice = ((lane3.astype(f32) == clip) & (lane < 3 * n_clips)).astype(f32).astype(bf16)
    high = grads.astype(bf16).astype(f32)
    rest = grads - high
    mid = rest.astype(bf16).astype(f32)
    parts = jnp.concatenate(
        [high, mid, rest - mid, jnp.zeros((LANES - 3 * n_clips, width), f32)], axis=0
    ).astype(bf16)
    unit_dy = nn(thrice, parts)
    stacked_ref[:rows, :] = (gate * unit_dy).astype(bf16)
    stacked_ref[rows:, :] = jnp.concatenate([high, mid], axis=0).astype(bf16)
    d_all = nt(stacked_ref[...], down.ready()[...])
    d_preact = (d_all[:rows] * slope.ready()[...]).astype(bf16)
    d_preact_out.send(d_preact)
    by_clip = d_all[rows : rows + n_clips] + d_all[rows + n_clips :]
    high_v = by_clip.astype(bf16).astype(f32)
    two = jnp.concatenate([high_v, by_clip - high_v], axis=0).astype(bf16)
    dots = nt(hidden.ready()[...], two)
    lane2 = iota((rows, 2 * n_clips), 1) % n_clips
    token_dg = jnp.sum(
        jnp.where(lane2.astype(f32) == clip, dots, 0.0), axis=1, keepdims=True
    )
    part = token_dg * gate_slope
    part_out.send(jnp.broadcast_to(part, (rows, LANES)))
    router = jnp.sum(
        jnp.where(
            iota((router.ref.shape[0], half), 0) == expert,
            router.ready()[:, pl.ds(other_at, half)].astype(f32),
            0.0,
        ),
        axis=0,
        keepdims=True,
    )
    out.send(nt(d_preact, up.ready()[pl.ds(other_at, half), :]) + part * router)


def own_kernel(at_ref, d_preact, up, part, router, out):
    half = out.ref.shape[1]
    expert = at_ref[0]
    own_at = pl.multiple_of(at_ref[1] * half, LANES)
    router = jnp.sum(
        jnp.where(
            iota((router.ref.shape[0], half), 0) == expert,
            router.ready()[:, pl.ds(own_at, half)].astype(f32),
            0.0,
        ),
        axis=0,
        keepdims=True,
    )
    out.send(
        nt(d_preact.ready()[...], up.ready()[pl.ds(own_at, half), :])
        + part.ready()[:, :1] * router
    )


def return_kernel(own, other, terms, pay_ref):
    n_exp, capacity, _ = pay_ref.shape
    half = own.ref.shape[1]
    strip = jnp.sum(terms.ready()[...], axis=0)
    strip_high = strip.astype(bf16).astype(f32)
    side = strip_high + pltpu.roll(strip - strip_high, LANES // 2, 1)
    pay_ref[:, :, half + LOW :] = jnp.broadcast_to(
        side.astype(bf16)[None], (n_exp, capacity, LANES)
    )
    total = (own.ready()[...] + other.ready()[...]).reshape(n_exp, capacity, half)
    high = total.astype(bf16)
    pay_ref[:, :, :half] = high
    pay_ref[:, :, half : half + LOW] = (
        total[:, :, :LOW] - high[:, :, :LOW].astype(f32)
    ).astype(bf16)


def final_kernel(strip, back_ref, placed_ref, dy_ref, out_ref, caps_ref):
    n_experts, _, capacity, wide = back_ref.shape
    half = wide - LOW - LANES
    placed = placed_ref[...]
    slots = n_experts * capacity

    def pick(h, start, size):
        part = back_ref[:, h, :, start : start + size]
        return nn(placed, part.astype(f32).reshape(slots, size).astype(bf16))

    for h in range(2):
        at = h * half
        high = pick(h, 0, half)
        out_ref[:, at : at + LOW] = dy_ref[:, at : at + LOW] + (
            high[:, :LOW] + pick(h, half, LOW)
        )
        out_ref[:, at + LOW : at + half] = dy_ref[:, at + LOW : at + half] + high[:, LOW:]
    lane = iota((capacity, LANES), 1)
    strips = []
    for e in range(2 * n_experts):
        side = back_ref[e // 2, e % 2, :, half + LOW :].astype(f32)
        strips.append(jnp.where(lane < strip, side + pltpu.roll(side, LANES // 2, 1), 0.0))
    for t, value in enumerate(join_strips(strips, strip, caps_ref.shape[1] // LANES)):
        caps_ref[:, t * LANES : (t + 1) * LANES] = value


def shards(tokens, routes, pool_ids, w_router, w_up, w_down, captions, clip_pairs, teacher):
    tok_rows, width = tokens.shape
    n_experts = w_router.shape[1]
    n_clips, n_caps = teacher.shape
    hid = w_up.shape[1]
    n_dp = lax.axis_size("dp")
    n_exp = lax.axis_size("expert")
    caps_dp = n_caps // n_dp
    capacity = tok_rows // n_experts
    half = width // 2
    strip = width // n_exp
    rows = n_exp * capacity
    own = lax.axis_index("expert")
    own_dp = lax.axis_index("dp")
    at = jnp.stack([own // 2, own % 2, own_dp, own]).astype(jnp.int32)
    swap = [(i, i ^ 1) for i in range(n_exp)]
    router_t = w_router.T
    sds = jax.ShapeDtypeStruct

    def run(body, outs, operands, near=(), kept=(), scratch=(), flops=0):
        vmem = pl.BlockSpec(memory_space=pltpu.VMEM)
        hbm = pl.BlockSpec(memory_space=pltpu.HBM)
        late = [i for i, o in enumerate(operands) if o is not at and i not in near]
        leaving = [i for i in range(len(outs)) if i not in kept]

        def kernel(*refs):
            n_in, n_out = len(operands), len(outs)
            ins, results = list(refs[:n_in]), list(refs[n_in : n_in + n_out])
            rest = list(refs[n_in + n_out :])
            in_bufs, rest = rest[: len(late)], rest[len(late) :]
            out_bufs, rest = rest[: len(leaving)], rest[len(leaving) :]
            in_sems, out_sems, rest = rest[0], rest[1], rest[2:]
            for k, i in enumerate(late):
                ins[i] = Late(pltpu.make_async_copy(ins[i], in_bufs[k], in_sems.at[k]), in_bufs[k])
            for k, i in enumerate(leaving):
                results[i] = Leaving(
                    pltpu.make_async_copy(out_bufs[k], results[i], out_sems.at[k]), out_bufs[k]
                )
            body(*ins, *results, *rest)
            for i in late:
                ins[i].ready()
            for i in leaving:
                results[i].copy.wait()

        return pl.pallas_call(
            kernel,
            out_shape=outs,
            in_specs=[
                pl.BlockSpec(memory_space=pltpu.SMEM) if o is at else hbm if i in late else vmem
                for i, o in enumerate(operands)
            ],
            out_specs=[hbm if i in leaving else vmem for i in range(len(outs))],
            scratch_shapes=[pltpu.VMEM(operands[i].shape, operands[i].dtype) for i in late]
            + [pltpu.VMEM(outs[i].shape, outs[i].dtype) for i in leaving]
            + [
                pltpu.SemaphoreType.DMA((max(len(late), 1),)),
                pltpu.SemaphoreType.DMA((max(len(leaving), 1),)),
            ]
            + list(scratch),
            compiler_params=pltpu.CompilerParams(vmem_limit_bytes=64 * MIB),
            cost_estimate=pl.CostEstimate(flops=flops, bytes_accessed=0, transcendentals=0),
        )(*operands)

    send, base, placed = run(
        functools.partial(pack_kernel, capacity, n_experts, n_clips),
        [
            sds((n_experts, 2, capacity, half + LANES), bf16),
            sds((n_clips, width), f32),
            sds((tok_rows, n_experts * capacity), bf16),
        ],
        [routes.reshape(1, tok_rows), pool_ids, tokens],
        kept=(0, 1, 2),
    )
    recv = exchange(send.reshape(n_exp, capacity, half + LANES), "expert")
    start, _ = lax.optimization_barrier((captions, send))
    block = lax.ppermute(
        start,
        ("dp", "expert"),
        [(a * n_exp + b, (b * n_exp + a) if b < n_dp else a * n_exp + b) for a in range(n_dp) for b in range(n_exp)],
    )
    recv, block = lax.optimization_barrier((recv, block))
    other = lax.ppermute(recv, "expert", swap)
    gelu_slope, hidden, aux, counts, pay = run(
        functools.partial(forward_kernel, n_clips, strip),
        [
            sds((rows, hid), f32),
            sds((rows, hid), bf16),
            sds((rows, LANES), f32),
            sds((n_clips, LANES), f32),
            sds((n_exp // 2, 2, caps_dp, half + LANES), bf16),
        ],
        [at, recv, other, router_t, w_up, block, w_down, base],
        kept=(4,),
    )
    sums = exchange(pay.reshape(n_exp, caps_dp, half + LANES), "expert")
    (total,) = run(
        functools.partial(sum_kernel, strip),
        [sds((n_exp, n_clips, LANES), bf16)],
        [sums[:, :, half:]],
        kept=(0,),
    )
    total = exchange(total, "expert")
    other_sums = lax.ppermute(sums, "expert", swap)
    clip_grad, terms = run(
        functools.partial(loss_kernel, strip),
        [sds((n_clips, width), f32), sds((n_dp, caps_dp, LANES), f32)],
        [at, total, counts, sums, other_sums, clip_pairs.reshape(1, n_caps), teacher],
        near=(1,),
        scratch=[pltpu.VMEM((n_clips, width), f32)] * 3 + [pltpu.VMEM((n_caps, width), bf16)],
    )
    terms = exchange(terms, "dp")
    d_preact, dx_other, part = run(
        functools.partial(backward_kernel, n_clips),
        [sds((rows, hid), bf16), sds((rows, half), f32), sds((rows, LANES), f32)],
        [at, clip_grad, aux, w_down, gelu_slope, hidden, router_t, w_up],
        scratch=[pltpu.VMEM((rows + 2 * n_clips, width), bf16)],
    )
    from_other = lax.ppermute(dx_other, "expert", swap)
    (dx_own,) = run(
        own_kernel,
        [sds((rows, half), f32)],
        [at, d_preact, w_up, part, router_t],
        flops=OWN_FLOPS,
    )
    (pay,) = run(
        return_kernel,
        [sds((n_exp, capacity, half + LOW + LANES), bf16)],
        [dx_own, from_other, terms],
        kept=(0,),
    )
    back = exchange(pay, "expert")
    members = (pool_ids[0][:, None] == jnp.arange(n_clips, dtype=jnp.int32)[None, :]).astype(f32)
    token_dy = jnp.dot(members, clip_grad, precision=HIGHEST)
    token_grads, caption_grads = run(
        functools.partial(final_kernel, strip),
        [sds((tok_rows, width), f32), sds((caps_dp, width), f32)],
        [back.reshape(n_experts, 2, capacity, half + LOW + LANES), placed, token_dy],
        near=(0, 1, 2),
        kept=(0, 1),
    )
    return (token_grads, caption_grads)


def solution(mesh):
    return jax.shard_map(
        shards,
        mesh=mesh,
        in_specs=(
            P(("dp", "expert"), None),
            P(("dp", "expert"), None),
            P("dp", "expert"),
            P(),
            P(None, "expert"),
            P("expert", None),
            P("dp", None),
            P(),
            P("dp", None),
        ),
        out_specs=(P(("dp", "expert"), None), P("dp", None)),
        check_vma=False,
    )
```

time: 172 us -> 149 us (0.87)
  starting transfers between devices: 83 us -> 43.2 us
  blocking collectives: 0 us -> 39.4 us
  local copies, waits for them, and re-layouts: 30 us -> 2.94 us
  Pallas kernels: 15.5 us -> 31.1 us
  waiting for transfers between devices: 39 us -> 27.4 us
    all_to_all x0 -> x2, blocking collectives: none -> 39.4 us  [exchange(): return lax.all_to_all(x, axis, split_axis=0, concat_axis=0, tiled=True)]
    ppermute x7 -> x2, starting transfers between devices: 32.4 us -> 5.52 us  [the longest x1 3.59 us: shards(): other_sums = lax.ppermute(sums, 'expert', swap)]
    unnamed x66 -> x4, local copies, waits for them, and re-layouts: 25.5 us -> 1.48 us
    pallas_call x7 -> x8, Pallas kernels: 15.5 us -> 31.1 us  [run(): pl.pallas_call(kernel, out_shape=outs, in_specs=[pl.BlockSpec(memory_spac...]
    all_to_all x5 -> x3, starting transfers between devices: 44.9 us -> 31.6 us  [exchange(): return lax.all_to_all(x, axis, split_axis=0, concat_axis=0, tiled=True)]
    all_to_all x5 -> x3, waiting for transfers between devices: 33.4 us -> 22.2 us  [exchange(): return lax.all_to_all(x, axis, split_axis=0, concat_axis=0, tiled=True)]
    reshape x4 -> x0, local copies, waits for them, and re-layouts: 2.28 us -> none  [the longest x2 1.51 us: shards(): pieces = pooled_part.reshape(n_clips, parts, quarter).transpose(1, 0, 2)]
    ppermute x7 -> x2, waiting for transfers between devices: 5.55 us -> 4.58 us  [the longest x1 4.58 us: shards(): lax.ppermute(start, ('dp', 'expert'), [(a * n_exp + b, b * n_exp + a if b...]
  transfers between devices with their start and end apart: 14 -> 7, of which waited for: 6 -> 4; matrix products, arithmetic and copies ran while one was open for 4% -> 3% of each run, Pallas kernels for 1% -> 9%
where the time goes in v3:
time: 149 us; the launch traced here: 148 us
  starting transfers between devices  43.2 us (29%)
  blocking collectives  39.4 us (26%)
  Pallas kernels  31.1 us (21%)
  waiting for transfers between devices  27.4 us (18%)
  local copies, waits for them, and re-layouts  2.94 us (2%)
  matrix products  2.1 us (1%)
    all_to_all x2, blocking collectives, exchange(): return lax.all_to_all(x, axis, split_axis=0, concat_axis=0, tiled=True)  39.4 us
    all_to_all x3, starting transfers between devices, exchange(): return lax.all_to_all(x, axis, split_axis=0, concat_axis=0, tiled=True)  31.6 us
    pallas_call x8, Pallas kernels, run(): pl.pallas_call(kernel, out_shape=outs, in_specs=[pl.BlockSpec(memory_spac...  31.1 us
    all_to_all x3, waiting for transfers between devices, exchange(): return lax.all_to_all(x, axis, split_axis=0, concat_axis=0, tiled=True)  22.2 us
    ppermute x1, waiting for transfers between devices, shards(): lax.ppermute(start, ('dp', 'expert'), [(a * n_exp + b, b * n_exp + a if b...  4.58 us
    ppermute x1, starting transfers between devices, shards(): other_sums = lax.ppermute(sums, 'expert', swap)  3.59 us
    ppermute x1, starting transfers between devices, shards(): other = lax.ppermute(recv, 'expert', swap)  3.54 us
  transfers between devices with their start and end apart: 7, of which 4 were waited for; matrix products, arithmetic and copies ran while one was open for 3% of the time, Pallas kernels for 9%

profile of v3, /device:TPU:1, one launch (start us, length us, event | category | flops | bytes accessed | tf_op | source)
XLA Modules:
  0.0 147.6 jit_solution(1812153516527605168)
XLA Ops:
  0.6 2.1 %shard_map.104 = (bf16[16,2,8,768]{3,2,1,0:T(8,128)(2,1)}, f32[8,1280]{1,0:T(8,128)}, bf16[128,128]{1,0:T(8,128)(2,1)}) custom-call(s32[1,128]{1,0:T(1,128)} %bitcast.19, s32[1,128]{1,0:T(1,128)} %refs_1_.1, bf16[128,1280]{1,0:T(8,128)(2,1)} %refs_2_.2), custom_call_target="tpu_custom_call" | custom-call | tf_op jit(solution)/shard_map/pallas_call | solution.py:448
  2.8 17.7 %all-to-all-start = ((bf16[32,8,768]{2,1,0:T(8,128)(2,1)}), bf16[32,8,768]{2,1,0:T(8,128)(2,1)S(1)}, u32[]{:S(2)}, u32[]{:S(2)}) async-start(bf16[32,8,768]{2,1,0:T(8,128)(2,1)} %bitcast.12), calls=%async_computation | async-start | bytes 786432 | tf_op jit(solution)/shard_map/all_to_all | solution.py:22
  20.5 1.9 %collective-permute-start = (bf16[8,1280]{1,0:T(8,128)(2,1)}, bf16[8,1280]{1,0:T(8,128)(2,1)}, u32[]{:S(2)}, u32[]{:S(2)}) collective-permute-start(bf16[8,1280]{1,0:T(8,128)(2,1)} %param.15), channel_id=1, source_target_pairs={{0,0},{1,32},{2,64},{3,96},{4,128},{5,160},{6,192},{7,224},{8,256}... | collective-permute-start | bytes 61448 | tf_op jit(solution)/shard_map/ppermute | solution.py:479
  22.4 4.6 %collective-permute-done.refs_5_ = bf16[8,1280]{1,0:T(8,128)(2,1)} collective-permute-done((bf16[8,1280]{1,0:T(8,128)(2,1)}, bf16[8,1280]{1,0:T(8,128)(2,1)}, u32[]{:S(2)}, u32[]{:S(2)}) %collective-permute-start) | collective-permute-done | bytes 20512 | tf_op jit(solution)/shard_map/ppermute | solution.py:479
  27.0 7.4 %all-to-all-done.refs_1_ = bf16[32,8,768]{2,1,0:T(8,128)(2,1)S(1)} async-done(((bf16[32,8,768]{2,1,0:T(8,128)(2,1)}), bf16[32,8,768]{2,1,0:T(8,128)(2,1)S(1)}, u32[]{:S(2)}, u32[]{:S(2)}) %all-to-all-start) | async-done | bytes 393248 | tf_op jit(solution)/shard_map/all_to_all | solution.py:22
  34.4 0.0 copy-start
  34.4 0.7 copy-done
  35.1 3.5 %collective-permute-start.1 = (bf16[32,8,768]{2,1,0:T(8,128)(2,1)S(1)}, bf16[32,8,768]{2,1,0:T(8,128)(2,1)S(1)}, u32[]{:S(2)}, u32[]{:S(2)}) collective-permute-start(bf16[32,8,768]{2,1,0:T(8,128)(2,1)S(1)} %all-to-all-done.refs_1_), channel_id=1, source_target_pairs={{0,1},{1,0},{2,3},{3,2},{4,5},{5,4},{6,7},{7,6},{8,9},{9,8},{10,11... | collective-permute-start | bytes 1179656 | tf_op jit(solution)/shard_map/ppermute | solution.py:485
  38.7 0.7 pad_add_fusion.refs_0_
  39.4 0.6 collective-permute-done.1.refs_2_
  40.0 0.0 copy-start.1
  40.0 0.7 copy-done.1
  40.7 7.2 %shard_map.105 = (f32[256,1280]{1,0:T(8,128)}, bf16[256,1280]{1,0:T(8,128)(2,1)}, f32[256,128]{1,0:T(8,128)}, f32[8,128]{1,0:T(8,128)}, bf16[16,2,8,768]{3,2,1,0:T(8,128)(2,1)}) custom-call(s32[4]{0:T(128)} %pad_add_fusion.refs_0_, bf16[32,8,768]{2,1,0:T(8,128)(2,1)} %copy-done, bf16[32,8,768]{2,1,0:T(8,128)(2,1)} %copy-done.1, bf16[16,1280]{1,0:T(8,128)(2,1)} %bitcast.14, ...), custom_call_target="tpu_custom_call" | custom-call | tf_op jit(solution)/shard_map/pallas_call | solution.py:448
  47.9 26.7 %all_to_all.25.refs_3_ = bf16[32,8,768]{2,1,0:T(8,128)(2,1)} all-to-all(bf16[32,8,768]{2,1,0:T(8,128)(2,1)} %bitcast.13), channel_id=1, replica_groups=mesh['dp'=32,'expert'=32] {'expert'}, dimensions={0} | all-to-all | bytes 786432 | tf_op jit(solution)/shard_map/all_to_all | solution.py:22
  74.7 3.6 %collective-permute-start.2 = (bf16[32,8,768]{2,1,0:T(8,128)(2,1)}, bf16[32,8,768]{2,1,0:T(8,128)(2,1)}, u32[]{:S(2)}, u32[]{:S(2)}) collective-permute-start(bf16[32,8,768]{2,1,0:T(8,128)(2,1)} %all_to_all.25.refs_3_), channel_id=1, source_target_pairs={{0,1},{1,0},{2,3},{3,2},{4,5},{5,4},{6,7},{7,6},{8,9},{9,8},{10,11... | collective-permute-start | bytes 1179656 | tf_op jit(solution)/shard_map/ppermute | solution.py:506
  78.3 1.5 slice.4.refs_0_
  79.7 1.7 %shard_map.106 = bf16[32,8,128]{2,1,0:T(8,128)(2,1)} custom-call(bf16[32,8,128]{2,1,0:T(8,128)(2,1)} %slice.4.refs_0_), custom_call_target="tpu_custom_call" | custom-call | tf_op jit(solution)/shard_map/pallas_call | solution.py:448
  81.4 12.6 %all_to_all.26.refs_1_ = bf16[32,8,128]{2,1,0:T(8,128)(2,1)} all-to-all(bf16[32,8,128]{2,1,0:T(8,128)(2,1)} %shard_map.106), channel_id=1, replica_groups=mesh['dp'=32,'expert'=32] {'expert'}, dimensions={0} | all-to-all | bytes 131072 | tf_op jit(solution)/shard_map/all_to_all | solution.py:22
  94.0 0.0 collective-permute-done.2.refs_4_
  94.0 4.4 %shard_map.107 = (f32[8,1280]{1,0:T(8,128)}, f32[32,8,128]{2,1,0:T(8,128)}) custom-call(s32[4]{0:T(128)} %pad_add_fusion.refs_0_, bf16[32,8,128]{2,1,0:T(8,128)(2,1)} %all_to_all.26.refs_1_, f32[8,128]{1,0:T(8,128)} %get-tuple-element.24.refs_2_, bf16[32,8,768]{2,1,0:T(8,128)(2,1)} %all_to_all.25.refs_3_, ...), custom_call_target="tpu_custom_call" | custom-call | tf_op jit(solution)/shard_map/pallas_call | solution.py:448
  98.4 9.5 %all-to-all-start.3 = ((f32[32,8,128]{2,1,0:T(8,128)}), f32[32,8,128]{2,1,0:T(8,128)}, u32[]{:S(2)}, u32[]{:S(2)}) async-start(f32[32,8,128]{2,1,0:T(8,128)} %get-tuple-element.32), calls=%async_computation.3 | async-start | bytes 262144 | tf_op jit(solution)/shard_map/all_to_all | solution.py:22
  107.9 6.4 %shard_map.108 = (bf16[256,1280]{1,0:T(8,128)(2,1)}, f32[256,640]{1,0:T(8,128)}, f32[256,128]{1,0:T(8,128)}) custom-call(s32[4]{0:T(128)} %pad_add_fusion.refs_0_, f32[8,1280]{1,0:T(8,128)} %get-tuple-element.25.refs_1_, f32[256,128]{1,0:T(8,128)} %get-tuple-element.26.refs_2_, bf16[1280,1280]{1,0:T(8,128)(2,1)} %refs_3_.1, ...), custom_call_target="tpu_custom_call" | custom-call | tf_op jit(solution)/shard_map/pallas_call | solution.py:448
  114.3 2.6 %collective-permute-start.3 = (f32[256,640]{1,0:T(8,128)}, f32[256,640]{1,0:T(8,128)}, u32[]{:S(2)}, u32[]{:S(2)}) collective-permute-start(f32[256,640]{1,0:T(8,128)} %get-tuple-element.31), channel_id=1, source_target_pairs={{0,1},{1,0},{2,3},{3,2},{4,5},{5,4},{6,7},{7,6},{8,9},{9,8},{10,11... | collective-permute-start | bytes 1966088 | tf_op jit(solution)/shard_map/ppermute | solution.py:521
  116.9 4.5 %shard_map.109.refs_0_ = f32[256,640]{1,0:T(8,128)} custom-call(s32[4]{0:T(128)} %pad_add_fusion.refs_0_, bf16[256,1280]{1,0:T(8,128)(2,1)} %get-tuple-element.29.refs_1_, bf16[1280,1280]{1,0:T(8,128)(2,1)} %refs_2_.3, f32[256,128]{1,0:T(8,128)} %get-tuple-element.30.refs_3_, bf16[16,1280]{1,0:T(8,128)(2,1)} %bitcast.16), custom_call_target="tpu_custom_call" | custom-call | flops 10000000000 | tf_op jit(solution)/shard_map/pallas_call | solution.py:448
  121.4 0.0 all-to-all-done.3.refs_2_
  121.4 0.0 collective-permute-done.3.refs_1_
  121.4 2.4 %shard_map.110 = bf16[32,8,1024]{2,1,0:T(8,128)(2,1)} custom-call(f32[256,640]{1,0:T(8,128)} %shard_map.109.refs_0_, f32[256,640]{1,0:T(8,128)} %collective-permute-done.3.refs_1_, f32[32,8,128]{2,1,0:T(8,128)} %all-to-all-done.3.refs_2_), custom_call_target="tpu_custom_call" | custom-call | tf_op jit(solution)/shard_map/pallas_call | solution.py:448
  123.8 4.4 %all-to-all-start.4 = ((bf16[32,8,1024]{2,1,0:T(8,128)(2,1)}), bf16[32,8,1024]{2,1,0:T(8,128)(2,1)}, u32[]{:S(2)}, u32[]{:S(2)}) async-start(bf16[32,8,1024]{2,1,0:T(8,128)(2,1)} %shard_map.110), calls=%async_computation.4 | async-start | bytes 1048576 | tf_op jit(solution)/shard_map/all_to_all | solution.py:22
  128.2 2.1 %fusion.refs_2_ = f32[128,1280]{1,0:T(8,128)} fusion(f32[8,1280]{1,0:T(8,128)} %get-tuple-element.25.refs_1_, s32[128]{0:T(128)} %bitcast.17), kind=kOutput, calls=%fused_computation.1 | convolution fusion | flops 15729664 | bytes 696832 | tf_op jit(solution)/shard_map/dot_general | solution.py:536
  130.3 14.8 %all-to-all-done.4 = bf16[32,8,1024]{2,1,0:T(8,128)(2,1)} async-done(((bf16[32,8,1024]{2,1,0:T(8,128)(2,1)}), bf16[32,8,1024]{2,1,0:T(8,128)(2,1)}, u32[]{:S(2)}, u32[]{:S(2)}) %all-to-all-start.4) | async-done | bytes 524320 | tf_op jit(solution)/shard_map/all_to_all | solution.py:22
  145.2 2.4 %shard_map.111 = (f32[128,1280]{1,0:T(8,128)}, f32[8,1280]{1,0:T(8,128)}) custom-call(bf16[16,2,8,1024]{3,2,1,0:T(8,128)(2,1)} %bitcast.9.refs_0_, bf16[128,128]{1,0:T(8,128)(2,1)} %get-tuple-element.33.refs_1_, f32[128,1280]{1,0:T(8,128)} %fusion.refs_2_), custom_call_target="tpu_custom_call" | custom-call | tf_op jit(solution)/shard_map/pallas_call | solution.py:448
Async XLA Ops:
  2.8 31.6 %all-to-all-start = ((bf16[32,8,768]{2,1,0:T(8,128)(2,1)}), bf16[32,8,768]{2,1,0:T(8,128)(2,1)S(1)}, u32[]{:S(2)}, u32[]{:S(2)}) async-start(bf16[32,8,768]{2,1,0:T(8,128)(2,1)} %bitcast.12), calls=%async_computation | async-start | bytes 786432 | tf_op jit(solution)/shard_map/all_to_all | solution.py:22
  20.5 6.5 %collective-permute-start = (bf16[8,1280]{1,0:T(8,128)(2,1)}, bf16[8,1280]{1,0:T(8,128)(2,1)}, u32[]{:S(2)}, u32[]{:S(2)}) collective-permute-start(bf16[8,1280]{1,0:T(8,128)(2,1)} %param.15), channel_id=1, source_target_pairs={{0,0},{1,32},{2,64},{3,96},{4,128},{5,160},{6,192},{7,224},{8,256}... | collective-permute-start | bytes 61448 | tf_op jit(solution)/shard_map/ppermute | solution.py:479
  34.4 0.7 copy-start
  35.1 4.9 %collective-permute-start.1 = (bf16[32,8,768]{2,1,0:T(8,128)(2,1)S(1)}, bf16[32,8,768]{2,1,0:T(8,128)(2,1)S(1)}, u32[]{:S(2)}, u32[]{:S(2)}) collective-permute-start(bf16[32,8,768]{2,1,0:T(8,128)(2,1)S(1)} %all-to-all-done.refs_1_), channel_id=1, source_target_pairs={{0,1},{1,0},{2,3},{3,2},{4,5},{5,4},{6,7},{7,6},{8,9},{9,8},{10,11... | collective-permute-start | bytes 1179656 | tf_op jit(solution)/shard_map/ppermute | solution.py:485
  40.0 0.7 copy-start.1
  74.7 19.4 %collective-permute-start.2 = (bf16[32,8,768]{2,1,0:T(8,128)(2,1)}, bf16[32,8,768]{2,1,0:T(8,128)(2,1)}, u32[]{:S(2)}, u32[]{:S(2)}) collective-permute-start(bf16[32,8,768]{2,1,0:T(8,128)(2,1)} %all_to_all.25.refs_3_), channel_id=1, source_target_pairs={{0,1},{1,0},{2,3},{3,2},{4,5},{5,4},{6,7},{7,6},{8,9},{9,8},{10,11... | collective-permute-start | bytes 1179656 | tf_op jit(solution)/shard_map/ppermute | solution.py:506
  98.4 23.0 %all-to-all-start.3 = ((f32[32,8,128]{2,1,0:T(8,128)}), f32[32,8,128]{2,1,0:T(8,128)}, u32[]{:S(2)}, u32[]{:S(2)}) async-start(f32[32,8,128]{2,1,0:T(8,128)} %get-tuple-element.32), calls=%async_computation.3 | async-start | bytes 262144 | tf_op jit(solution)/shard_map/all_to_all | solution.py:22
  114.3 7.1 %collective-permute-start.3 = (f32[256,640]{1,0:T(8,128)}, f32[256,640]{1,0:T(8,128)}, u32[]{:S(2)}, u32[]{:S(2)}) collective-permute-start(f32[256,640]{1,0:T(8,128)} %get-tuple-element.31), channel_id=1, source_target_pairs={{0,1},{1,0},{2,3},{3,2},{4,5},{5,4},{6,7},{7,6},{8,9},{9,8},{10,11... | collective-permute-start | bytes 1966088 | tf_op jit(solution)/shard_map/ppermute | solution.py:521
  123.8 21.3 %all-to-all-start.4 = ((bf16[32,8,1024]{2,1,0:T(8,128)(2,1)}), bf16[32,8,1024]{2,1,0:T(8,128)(2,1)}, u32[]{:S(2)}, u32[]{:S(2)}) async-start(bf16[32,8,1024]{2,1,0:T(8,128)(2,1)} %shard_map.110), calls=%async_computation.4 | async-start | bytes 1048576 | tf_op jit(solution)/shard_map/all_to_all | solution.py:22

commit v4 on v3

--- a/solution.py
+++ b/solution.py
@@ -13,9 +13,8 @@
 f32 = jnp.float32
 bf16 = jnp.bfloat16
 LANES = 128
-LOW = 256
 MIB = 1 << 20
-OWN_FLOPS = 10_000_000_000
+COVER = 10_000_000_000
 
 
 def exchange(x, axis):
@@ -24,10 +23,15 @@
 
 class Late:
     def __init__(self, copy, ref):
-        self.copy, self.ref, self.waited = copy, ref, False
-        copy.start()
+        self.copy, self.ref, self.begun, self.waited = copy, ref, False, False
+
+    def begin(self):
+        if not self.begun:
+            self.copy.start()
+            self.begun = True
 
     def ready(self):
+        self.begin()
         if not self.waited:
             self.copy.wait()
             self.waited = True
@@ -36,12 +40,14 @@
 
 class Leaving:
     def __init__(self, copy, ref):
-        self.copy, self.ref, self.sent = copy, ref, False
+        self.copy, self.ref = copy, ref
 
     def send(self, value):
         self.ref[...] = value
+        self.go()
+
+    def go(self):
         self.copy.start()
-        self.sent = True
 
 
 def iota(shape, axis):
@@ -183,6 +189,9 @@
     )
     weights = (clip * gate).T[:n_clips].astype(bf16)
     up_ref = up.ready()
+    down.begin()
+    block.begin()
+    base.begin()
     preact = nn(own, up_ref[pl.ds(own_at, half), :]) + nn(
         other_rows, up_ref[pl.ds(other_at, half), :]
     )
@@ -215,17 +224,42 @@
     out_ref[...] = jnp.broadcast_to(total[None], out_ref.shape)
 
 
-def loss_kernel(
-    strip, at_ref, sums_ref, counts, own, other, pairs, teacher, grad_out, terms_out,
-    mean_ref, image_ref, d_image_ref, text_ref,
-):
-    n_exp, n_clips, wide = own.ref.shape
-    n_caps = teacher.ref.shape[1]
-    half = wide - LANES
+def text_kernel(strip, at_ref, own, other, pairs, teacher, text_out, table_out, strip_out):
+    n_clips, n_caps = teacher.ref.shape
+    half = own.ref.shape[2]
     width = 2 * half
     own_at = pl.multiple_of(at_ref[1] * half, LANES)
     other_at = pl.multiple_of((1 - at_ref[1]) * half, LANES)
-    own_dp = at_ref[2]
+    matched = (
+        pairs.ready()[...] == at_ref[2] * n_clips + iota((n_clips, n_caps), 0)
+    ).astype(f32)
+    target = 0.5 * matched + 0.5 * jax.nn.sigmoid(teacher.ready()[...])
+    own_text = own.ready()[...].astype(f32).reshape(n_caps, half)
+    other_text = other.ready()[...].astype(f32).reshape(n_caps, half)
+    text_out.ref[:, pl.ds(own_at, half)] = own_text.astype(bf16)
+    text_out.ref[:, pl.ds(other_at, half)] = other_text.astype(bf16)
+    text_out.go()
+    ones = jnp.ones((16, half), bf16)
+
+    def squares(text):
+        square = text * text
+        high = square.astype(bf16)
+        return nt(ones, high) + nt(ones, (square - high.astype(f32)).astype(bf16))
+
+    text_scale = lax.rsqrt((squares(own_text) + squares(other_text))[:n_clips] + norm_eps)
+    table_out.send(jnp.concatenate([text_scale, target], axis=0))
+    pick = (
+        (iota((width, LANES), 0) - at_ref[3] * strip == iota((width, LANES), 1))
+        & (iota((width, LANES), 1) < strip)
+    ).astype(f32).astype(bf16)
+    strip_out.send(nn(text_out.ref[...], pick))
+
+
+def loss_kernel(
+    strip, at_ref, sums_ref, counts, table, text, raw_strip, grad_out, terms_out, mean_ref,
+):
+    n_exp, n_clips, _ = sums_ref.shape
+    n_caps, width = text.ref.shape
     n_tiles = width // LANES
     tiles = join_strips(
         [gather3(sums_ref[e].astype(f32), strip) for e in range(n_exp)], strip, n_tiles
@@ -236,29 +270,12 @@
     clip_mean = mean_ref[...]
     img_scale = lax.rsqrt(jnp.sum(clip_mean * clip_mean, axis=1, keepdims=True) + norm_eps)
     image_emb = clip_mean * img_scale
-    image_ref[...] = image_emb
-    own_text = own.ready()[:, :, :half].astype(f32).reshape(n_caps, half)
-    other_text = other.ready()[:, :, :half].astype(f32).reshape(n_caps, half)
-    ones = jnp.ones((16, half), bf16)
-
-    def squares(text):
-        square = text * text
-        high = square.astype(bf16)
-        return nt(ones, high) + nt(ones, (square - high.astype(f32)).astype(bf16))
-
-    text_scale = lax.rsqrt((squares(own_text) + squares(other_text))[:n_clips] + norm_eps)
-    own_text = own_text.astype(bf16)
-    other_text = other_text.astype(bf16)
-    text_ref[:, pl.ds(own_at, half)] = own_text
-    text_ref[:, pl.ds(other_at, half)] = other_text
-    text = text_ref[...]
+    text = text.ready()[...]
     raw = fold3(nt(stack3(image_emb), text))
-    matched = (
-        pairs.ready()[...] == own_dp * n_clips + iota((n_clips, n_caps), 0)
-    ).astype(f32)
-    target = 0.5 * matched + 0.5 * jax.nn.sigmoid(teacher.ready()[...])
+    table = table.ready()[...]
+    text_scale = table[:n_clips]
     logits = logit_scale * raw * text_scale + logit_shift
-    loss_grad = (jax.nn.sigmoid(logits) - target) * (counts / n_caps)
+    loss_grad = (jax.nn.sigmoid(logits) - table[n_clips:]) * (counts / n_caps)
     scaled = loss_grad * text_scale
     d_image = logit_scale * fold3(nn(stack3(scaled), text))
     mean_grad = (
@@ -270,12 +287,7 @@
         * clip_mean
     )
     grad_out.send(mean_grad / counts)
-    pick = (
-        (iota((width, LANES), 0) - at_ref[3] * strip == iota((width, LANES), 1))
-        & (iota((width, LANES), 1) < strip)
-    ).astype(f32).astype(bf16)
-    emb_strip = fold3(nn(stack3(image_emb), pick))
-    raw_strip = nn(text, pick)
+    emb_strip = gather3(sums_ref[at_ref[3]].astype(f32), strip) / counts * img_scale
     dots = jnp.sum(loss_grad * raw, axis=0, keepdims=True)
     cube = text_scale[:1] * text_scale[:1] * text_scale[:1] * dots
     both = jnp.concatenate([scaled, jnp.broadcast_to(cube, scaled.shape)], axis=0)
@@ -284,7 +296,7 @@
         both[:, :n_clips], emb_strip, (((1,), (0,)), ((), ())),
         precision=HIGHEST, preferred_element_type=f32,
     )
-    terms = logit_scale * (products - both[:, n_clips : n_clips + 1] * raw_strip)
+    terms = logit_scale * (products - both[:, n_clips : n_clips + 1] * raw_strip.ready()[...])
     terms_out.send(terms.reshape(terms_out.ref.shape))
 
 
@@ -312,6 +324,11 @@
         [high, mid, rest - mid, jnp.zeros((LANES - 3 * n_clips, width), f32)], axis=0
     ).astype(bf16)
     unit_dy = nn(thrice, parts)
+    down.ready()
+    slope.begin()
+    hidden.begin()
+    router.begin()
+    up.begin()
     stacked_ref[:rows, :] = (gate * unit_dy).astype(bf16)
     stacked_ref[rows:, :] = jnp.concatenate([high, mid], axis=0).astype(bf16)
     d_all = nt(stacked_ref[...], down.ready()[...])
@@ -336,7 +353,7 @@
         axis=0,
         keepdims=True,
     )
-    out.send(nt(d_preact, up.ready()[pl.ds(other_at, half), :]) + part * router)
+    out.send(nt(d_preact, up.ready()[...]) + part * router)
 
 
 def own_kernel(at_ref, d_preact, up, part, router, out):
@@ -353,7 +370,7 @@
         keepdims=True,
     )
     out.send(
-        nt(d_preact.ready()[...], up.ready()[pl.ds(own_at, half), :])
+        nt(d_preact.ready()[...], up.ready()[...])
         + part.ready()[:, :1] * router
     )
 
@@ -364,38 +381,28 @@
     strip = jnp.sum(terms.ready()[...], axis=0)
     strip_high = strip.astype(bf16).astype(f32)
     side = strip_high + pltpu.roll(strip - strip_high, LANES // 2, 1)
-    pay_ref[:, :, half + LOW :] = jnp.broadcast_to(
+    pay_ref[:, :, half:] = jnp.broadcast_to(
         side.astype(bf16)[None], (n_exp, capacity, LANES)
     )
     total = (own.ready()[...] + other.ready()[...]).reshape(n_exp, capacity, half)
-    high = total.astype(bf16)
-    pay_ref[:, :, :half] = high
-    pay_ref[:, :, half : half + LOW] = (
-        total[:, :, :LOW] - high[:, :, :LOW].astype(f32)
-    ).astype(bf16)
+    pay_ref[:, :, :half] = total.astype(bf16)
 
 
 def final_kernel(strip, back_ref, placed_ref, dy_ref, out_ref, caps_ref):
     n_experts, _, capacity, wide = back_ref.shape
-    half = wide - LOW - LANES
+    half = wide - LANES
     placed = placed_ref[...]
     slots = n_experts * capacity
 
-    def pick(h, start, size):
-        part = back_ref[:, h, :, start : start + size]
-        return nn(placed, part.astype(f32).reshape(slots, size).astype(bf16))
-
     for h in range(2):
-        at = h * half
-        high = pick(h, 0, half)
-        out_ref[:, at : at + LOW] = dy_ref[:, at : at + LOW] + (
-            high[:, :LOW] + pick(h, half, LOW)
+        part = back_ref[:, h, :, :half].astype(f32).reshape(slots, half).astype(bf16)
+        out_ref[:, h * half : (h + 1) * half] = (
+            dy_ref[:, h * half : (h + 1) * half] + nn(placed, part)
         )
-        out_ref[:, at + LOW : at + half] = dy_ref[:, at + LOW : at + half] + high[:, LOW:]
     lane = iota((capacity, LANES), 1)
     strips = []
     for e in range(2 * n_experts):
-        side = back_ref[e // 2, e % 2, :, half + LOW :].astype(f32)
+        side = back_ref[e // 2, e % 2, :, half:].astype(f32)
         strips.append(jnp.where(lane < strip, side + pltpu.roll(side, LANES // 2, 1), 0.0))
     for t, value in enumerate(join_strips(strips, strip, caps_ref.shape[1] // LANES)):
         caps_ref[:, t * LANES : (t + 1) * LANES] = value
@@ -420,7 +427,8 @@
     router_t = w_router.T
     sds = jax.ShapeDtypeStruct
 
-    def run(body, outs, operands, near=(), kept=(), scratch=(), flops=0):
+    def run(body, outs, operands, near=(), kept=(), held=(), views=(), scratch=(), flops=0):
+        views = dict(views)
         vmem = pl.BlockSpec(memory_space=pltpu.VMEM)
         hbm = pl.BlockSpec(memory_space=pltpu.HBM)
         late = [i for i, o in enumerate(operands) if o is not at and i not in near]
@@ -434,7 +442,10 @@
             out_bufs, rest = rest[: len(leaving)], rest[len(leaving) :]
             in_sems, out_sems, rest = rest[0], rest[1], rest[2:]
             for k, i in enumerate(late):
-                ins[i] = Late(pltpu.make_async_copy(ins[i], in_bufs[k], in_sems.at[k]), in_bufs[k])
+                source = views[i][1](ins[i], ins[0]) if i in views else ins[i]
+                ins[i] = Late(pltpu.make_async_copy(source, in_bufs[k], in_sems.at[k]), in_bufs[k])
+                if i not in held:
+                    ins[i].begin()
             for k, i in enumerate(leaving):
                 results[i] = Leaving(
                     pltpu.make_async_copy(out_bufs[k], results[i], out_sems.at[k]), out_bufs[k]
@@ -453,7 +464,10 @@
                 for i, o in enumerate(operands)
             ],
             out_specs=[hbm if i in leaving else vmem for i in range(len(outs))],
-            scratch_shapes=[pltpu.VMEM(operands[i].shape, operands[i].dtype) for i in late]
+            scratch_shapes=[
+                pltpu.VMEM(views[i][0] if i in views else operands[i].shape, operands[i].dtype)
+                for i in late
+            ]
             + [pltpu.VMEM(outs[i].shape, outs[i].dtype) for i in leaving]
             + [
                 pltpu.SemaphoreType.DMA((max(len(late), 1),)),
@@ -463,6 +477,12 @@
             compiler_params=pltpu.CompilerParams(vmem_limit_bytes=64 * MIB),
             cost_estimate=pl.CostEstimate(flops=flops, bytes_accessed=0, transcendentals=0),
         )(*operands)
+
+    def up_rows(flip):
+        def cut(ref, at_ref):
+            return ref.at[pl.ds(pl.multiple_of((at_ref[1] ^ flip) * half, LANES), half), :]
+
+        return ((half, hid), cut)
 
     send, base, placed = run(
         functools.partial(pack_kernel, capacity, n_experts, n_clips),
@@ -494,28 +514,44 @@
         ],
         [at, recv, other, router_t, w_up, block, w_down, base],
         kept=(4,),
+        held=(5, 6, 7),
     )
     sums = exchange(pay.reshape(n_exp, caps_dp, half + LANES), "expert")
     (total,) = run(
         functools.partial(sum_kernel, strip),
         [sds((n_exp, n_clips, LANES), bf16)],
-        [sums[:, :, half:]],
+        [sums],
         kept=(0,),
+        views={0: ((n_exp, caps_dp, LANES), lambda ref, _: ref.at[:, :, pl.ds(half, LANES)])},
     )
     total = exchange(total, "expert")
     other_sums = lax.ppermute(sums, "expert", swap)
+    cut_text = ((n_exp, caps_dp, half), lambda ref, _: ref.at[:, :, pl.ds(0, half)])
+    text, table, raw_strip = run(
+        functools.partial(text_kernel, strip),
+        [
+            sds((n_caps, width), bf16),
+            sds((2 * n_clips, n_caps), f32),
+            sds((n_caps, LANES), f32),
+        ],
+        [at, sums, other_sums, clip_pairs.reshape(1, n_caps), teacher],
+        views={1: cut_text, 2: cut_text},
+        flops=COVER,
+    )
     clip_grad, terms = run(
         functools.partial(loss_kernel, strip),
         [sds((n_clips, width), f32), sds((n_dp, caps_dp, LANES), f32)],
-        [at, total, counts, sums, other_sums, clip_pairs.reshape(1, n_caps), teacher],
+        [at, total, counts, table, text, raw_strip],
         near=(1,),
-        scratch=[pltpu.VMEM((n_clips, width), f32)] * 3 + [pltpu.VMEM((n_caps, width), bf16)],
+        scratch=[pltpu.VMEM((n_clips, width), f32)],
     )
     terms = exchange(terms, "dp")
     d_preact, dx_other, part = run(
         functools.partial(backward_kernel, n_clips),
         [sds((rows, hid), bf16), sds((rows, half), f32), sds((rows, LANES), f32)],
         [at, clip_grad, aux, w_down, gelu_slope, hidden, router_t, w_up],
+        held=(4, 5, 6, 7),
+        views={7: up_rows(1)},
         scratch=[pltpu.VMEM((rows + 2 * n_clips, width), bf16)],
     )
     from_other = lax.ppermute(dx_other, "expert", swap)
@@ -523,11 +559,12 @@
         own_kernel,
         [sds((rows, half), f32)],
         [at, d_preact, w_up, part, router_t],
-        flops=OWN_FLOPS,
+        views={2: up_rows(0)},
+        flops=COVER,
     )
     (pay,) = run(
         return_kernel,
-        [sds((n_exp, capacity, half + LOW + LANES), bf16)],
+        [sds((n_exp, capacity, half + LANES), bf16)],
         [dx_own, from_other, terms],
         kept=(0,),
     )
@@ -537,7 +574,7 @@
     token_grads, caption_grads = run(
         functools.partial(final_kernel, strip),
         [sds((tok_rows, width), f32), sds((caps_dp, width), f32)],
-        [back.reshape(n_experts, 2, capacity, half + LOW + LANES), placed, token_dy],
+        [back.reshape(n_experts, 2, capacity, half + LANES), placed, token_dy],
         near=(0, 1, 2),
         kept=(0, 1),
     )

time: 149 us -> 152 us (1.020)
  blocking collectives: 39.4 us -> 26.7 us
  waiting for transfers between devices: 27.4 us -> 36.9 us
  starting transfers between devices: 43.2 us -> 48.8 us
  Pallas kernels: 31.1 us -> 33.3 us
    all_to_all x2 -> x1, blocking collectives: 39.4 us -> 26.7 us  [exchange(): return lax.all_to_all(x, axis, split_axis=0, concat_axis=0, tiled=True)]
    all_to_all x3 -> x4, waiting for transfers between devices: 22.2 us -> 31.6 us  [exchange(): return lax.all_to_all(x, axis, split_axis=0, concat_axis=0, tiled=True)]
    all_to_all x3 -> x4, starting transfers between devices: 31.6 us -> 37.4 us  [exchange(): return lax.all_to_all(x, axis, split_axis=0, concat_axis=0, tiled=True)]
    pallas_call x8 -> x9, Pallas kernels: 31.1 us -> 33.3 us  [run(): pl.pallas_call(kernel, out_shape=outs, in_specs=[pl.BlockSpec(memory_spac...]
  transfers between devices with their start and end apart: 7 -> 8, of which waited for: 4 -> 6; matrix products, arithmetic and copies ran while one was open for 3% -> 2% of each run, Pallas kernels for 9% -> 6%
where the time goes in v4:
time: 152 us; the launch traced here: 151 us
  starting transfers between devices  48.8 us (32%)
  waiting for transfers between devices  36.9 us (24%)
  Pallas kernels  33.3 us (22%)
  blocking collectives  26.7 us (18%)
  matrix products  2.09 us (1%)
    all_to_all x4, starting transfers between devices, exchange(): return lax.all_to_all(x, axis, split_axis=0, concat_axis=0, tiled=True)  37.4 us
    pallas_call x9, Pallas kernels, run(): pl.pallas_call(kernel, out_shape=outs, in_specs=[pl.BlockSpec(memory_spac...  33.3 us
    all_to_all x4, waiting for transfers between devices, exchange(): return lax.all_to_all(x, axis, split_axis=0, concat_axis=0, tiled=True)  31.6 us
    all_to_all x1, blocking collectives, exchange(): return lax.all_to_all(x, axis, split_axis=0, concat_axis=0, tiled=True)  26.7 us
    ppermute x1, waiting for transfers between devices, shards(): lax.ppermute(start, ('dp', 'expert'), [(a * n_exp + b, b * n_exp + a if b...  4.58 us
    ppermute x1, starting transfers between devices, shards(): other_sums = lax.ppermute(sums, 'expert', swap)  3.59 us
    ppermute x1, starting transfers between devices, shards(): other = lax.ppermute(recv, 'expert', swap)  3.54 us
  transfers between devices with their start and end apart: 8, of which 6 were waited for; matrix products, arithmetic and copies ran while one was open for 2% of the time, Pallas kernels for 6%

profile of v4, /device:TPU:1, one launch (start us, length us, event | category | flops | bytes accessed | tf_op | source)
XLA Modules:
  0.0 150.6 jit_solution(3986602814345000229)
XLA Ops:
  0.6 2.1 %shard_map.104 = (bf16[16,2,8,768]{3,2,1,0:T(8,128)(2,1)}, f32[8,1280]{1,0:T(8,128)}, bf16[128,128]{1,0:T(8,128)(2,1)}) custom-call(s32[1,128]{1,0:T(1,128)} %bitcast.18, s32[1,128]{1,0:T(1,128)} %refs_1_.1, bf16[128,1280]{1,0:T(8,128)(2,1)} %refs_2_.2), custom_call_target="tpu_custom_call" | custom-call | tf_op jit(solution)/shard_map/pallas_call | solution.py:459
  2.8 17.7 %all-to-all-start = ((bf16[32,8,768]{2,1,0:T(8,128)(2,1)}), bf16[32,8,768]{2,1,0:T(8,128)(2,1)S(1)}, u32[]{:S(2)}, u32[]{:S(2)}) async-start(bf16[32,8,768]{2,1,0:T(8,128)(2,1)} %bitcast.12), calls=%async_computation | async-start | bytes 786432 | tf_op jit(solution)/shard_map/all_to_all | solution.py:21
  20.5 1.9 %collective-permute-start = (bf16[8,1280]{1,0:T(8,128)(2,1)}, bf16[8,1280]{1,0:T(8,128)(2,1)}, u32[]{:S(2)}, u32[]{:S(2)}) collective-permute-start(bf16[8,1280]{1,0:T(8,128)(2,1)} %param.15), channel_id=1, source_target_pairs={{0,0},{1,32},{2,64},{3,96},{4,128},{5,160},{6,192},{7,224},{8,256}... | collective-permute-start | bytes 61448 | tf_op jit(solution)/shard_map/ppermute | solution.py:499
  22.4 4.6 %collective-permute-done.refs_5_ = bf16[8,1280]{1,0:T(8,128)(2,1)} collective-permute-done((bf16[8,1280]{1,0:T(8,128)(2,1)}, bf16[8,1280]{1,0:T(8,128)(2,1)}, u32[]{:S(2)}, u32[]{:S(2)}) %collective-permute-start) | collective-permute-done | bytes 20512 | tf_op jit(solution)/shard_map/ppermute | solution.py:499
  27.0 7.4 %all-to-all-done.refs_1_ = bf16[32,8,768]{2,1,0:T(8,128)(2,1)S(1)} async-done(((bf16[32,8,768]{2,1,0:T(8,128)(2,1)}), bf16[32,8,768]{2,1,0:T(8,128)(2,1)S(1)}, u32[]{:S(2)}, u32[]{:S(2)}) %all-to-all-start) | async-done | bytes 393248 | tf_op jit(solution)/shard_map/all_to_all | solution.py:21
  34.4 0.0 copy-start
  34.4 0.8 copy-done
  35.2 3.5 %collective-permute-start.1 = (bf16[32,8,768]{2,1,0:T(8,128)(2,1)S(1)}, bf16[32,8,768]{2,1,0:T(8,128)(2,1)S(1)}, u32[]{:S(2)}, u32[]{:S(2)}) collective-permute-start(bf16[32,8,768]{2,1,0:T(8,128)(2,1)S(1)} %all-to-all-done.refs_1_), channel_id=1, source_target_pairs={{0,1},{1,0},{2,3},{3,2},{4,5},{5,4},{6,7},{7,6},{8,9},{9,8},{10,11... | collective-permute-start | bytes 1179656 | tf_op jit(solution)/shard_map/ppermute | solution.py:505
  38.7 0.6 pad_add_fusion.refs_0_
  39.3 0.7 collective-permute-done.1.refs_2_
  40.0 0.0 copy-start.1
  40.0 0.7 copy-done.1
  40.8 7.3 %shard_map.105 = (f32[256,1280]{1,0:T(8,128)}, bf16[256,1280]{1,0:T(8,128)(2,1)}, f32[256,128]{1,0:T(8,128)}, f32[8,128]{1,0:T(8,128)}, bf16[16,2,8,768]{3,2,1,0:T(8,128)(2,1)}) custom-call(s32[4]{0:T(128)} %pad_add_fusion.refs_0_, bf16[32,8,768]{2,1,0:T(8,128)(2,1)} %copy-done, bf16[32,8,768]{2,1,0:T(8,128)(2,1)} %copy-done.1, bf16[16,1280]{1,0:T(8,128)(2,1)} %bitcast.14, ...), custom_call_target="tpu_custom_call" | custom-call | tf_op jit(solution)/shard_map/pallas_call | solution.py:459
  48.1 26.7 %all_to_all.25.refs_0_.refs_1_ = bf16[32,8,768]{2,1,0:T(8,128)(2,1)} all-to-all(bf16[32,8,768]{2,1,0:T(8,128)(2,1)} %bitcast.13), channel_id=1, replica_groups=mesh['dp'=32,'expert'=32] {'expert'}, dimensions={0} | all-to-all | bytes 786432 | tf_op jit(solution)/shard_map/all_to_all | solution.py:21
  74.9 3.6 %collective-permute-start.2 = (bf16[32,8,768]{2,1,0:T(8,128)(2,1)}, bf16[32,8,768]{2,1,0:T(8,128)(2,1)}, u32[]{:S(2)}, u32[]{:S(2)}) collective-permute-start(bf16[32,8,768]{2,1,0:T(8,128)(2,1)} %all_to_all.25.refs_0_.refs_1_), channel_id=1, source_target_pairs={{0,1},{1,0},{2,3},{3,2},{4,5},{5,4},{6,7},{7,6},{8,9},{9,8},{10,11... | collective-permute-start | bytes 1179656 | tf_op jit(solution)/shard_map/ppermute | solution.py:528
  78.5 1.7 %shard_map.106 = bf16[32,8,128]{2,1,0:T(8,128)(2,1)} custom-call(bf16[32,8,768]{2,1,0:T(8,128)(2,1)} %all_to_all.25.refs_0_.refs_1_), custom_call_target="tpu_custom_call" | custom-call | tf_op jit(solution)/shard_map/pallas_call | solution.py:459
  80.1 4.4 %all-to-all-start.2 = ((bf16[32,8,128]{2,1,0:T(8,128)(2,1)}), bf16[32,8,128]{2,1,0:T(8,128)(2,1)}, u32[]{:S(2)}, u32[]{:S(2)}) async-start(bf16[32,8,128]{2,1,0:T(8,128)(2,1)} %shard_map.106), calls=%async_computation.2 | async-start | bytes 131072 | tf_op jit(solution)/shard_map/all_to_all | solution.py:21
  84.5 0.0 collective-permute-done.2.refs_2_
  84.5 3.1 %shard_map.107 = (bf16[256,1280]{1,0:T(8,128)(2,1)}, f32[16,256]{1,0:T(8,128)}, f32[256,128]{1,0:T(8,128)}) custom-call(s32[4]{0:T(128)} %pad_add_fusion.refs_0_, bf16[32,8,768]{2,1,0:T(8,128)(2,1)} %all_to_all.25.refs_0_.refs_1_, bf16[32,8,768]{2,1,0:T(8,128)(2,1)} %collective-permute-done.2.refs_2_, s32[1,256]{1,0:T(1,128)} %bitcast.19, f32[8,256]{1,0:T(8,128)} %refs_4_.3), custom_call_target="tpu_custom_call" | custom-call | flops 10000000000 | tf_op jit(solution)/shard_map/pallas_call | solution.py:459
  87.7 5.1 %all-to-all-done.2.refs_1_ = bf16[32,8,128]{2,1,0:T(8,128)(2,1)} async-done(((bf16[32,8,128]{2,1,0:T(8,128)(2,1)}), bf16[32,8,128]{2,1,0:T(8,128)(2,1)}, u32[]{:S(2)}, u32[]{:S(2)}) %all-to-all-start.2) | async-done | bytes 65568 | tf_op jit(solution)/shard_map/all_to_all | solution.py:21
  92.8 3.7 %shard_map.108 = (f32[8,1280]{1,0:T(8,128)}, f32[32,8,128]{2,1,0:T(8,128)}) custom-call(s32[4]{0:T(128)} %pad_add_fusion.refs_0_, bf16[32,8,128]{2,1,0:T(8,128)(2,1)} %all-to-all-done.2.refs_1_, f32[8,128]{1,0:T(8,128)} %get-tuple-element.27.refs_2_, f32[16,256]{1,0:T(8,128)} %get-tuple-element.28.refs_3_, bf16[256,1280]{1,0:T(8,128)(2,1)} %get-tuple-element.29.refs_4_, ...), custom_call_target="tpu_custom_call" | custom-call | tf_op jit(solution)/shard_map/pallas_call | solution.py:459
  96.5 6.6 %shard_map.109 = (bf16[256,1280]{1,0:T(8,128)(2,1)}, f32[256,640]{1,0:T(8,128)}, f32[256,128]{1,0:T(8,128)}) custom-call(s32[4]{0:T(128)} %pad_add_fusion.refs_0_, f32[8,1280]{1,0:T(8,128)} %get-tuple-element.31.refs_1_, f32[256,128]{1,0:T(8,128)} %get-tuple-element.32.refs_2_, bf16[1280,1280]{1,0:T(8,128)(2,1)} %refs_3_.1, ...), custom_call_target="tpu_custom_call" | custom-call | tf_op jit(solution)/shard_map/pallas_call | solution.py:459
  103.1 2.3 %collective-permute-start.3 = (f32[256,640]{1,0:T(8,128)}, f32[256,640]{1,0:T(8,128)}, u32[]{:S(2)}, u32[]{:S(2)}) collective-permute-start(f32[256,640]{1,0:T(8,128)} %get-tuple-element.37), channel_id=1, source_target_pairs={{0,1},{1,0},{2,3},{3,2},{4,5},{5,4},{6,7},{7,6},{8,9},{9,8},{10,11... | collective-permute-start | bytes 1966088 | tf_op jit(solution)/shard_map/ppermute | solution.py:557
  105.4 9.5 %all-to-all-start.3 = ((f32[32,8,128]{2,1,0:T(8,128)}), f32[32,8,128]{2,1,0:T(8,128)}, u32[]{:S(2)}, u32[]{:S(2)}) async-start(f32[32,8,128]{2,1,0:T(8,128)} %get-tuple-element.38), calls=%async_computation.3 | async-start | bytes 262144 | tf_op jit(solution)/shard_map/all_to_all | solution.py:21
  114.9 4.0 %shard_map.110.refs_0_ = f32[256,640]{1,0:T(8,128)} custom-call(s32[4]{0:T(128)} %pad_add_fusion.refs_0_, bf16[256,1280]{1,0:T(8,128)(2,1)} %get-tuple-element.35.refs_1_, bf16[1280,1280]{1,0:T(8,128)(2,1)} %refs_2_.3, f32[256,128]{1,0:T(8,128)} %get-tuple-element.36.refs_3_, bf16[16,1280]{1,0:T(8,128)(2,1)} %bitcast.16), custom_call_target="tpu_custom_call" | custom-call | flops 10000000000 | tf_op jit(solution)/shard_map/pallas_call | solution.py:459
  118.9 7.2 %all-to-all-done.3.refs_2_ = f32[32,8,128]{2,1,0:T(8,128)} async-done(((f32[32,8,128]{2,1,0:T(8,128)}), f32[32,8,128]{2,1,0:T(8,128)}, u32[]{:S(2)}, u32[]{:S(2)}) %all-to-all-start.3) | async-done | bytes 131104 | tf_op jit(solution)/shard_map/all_to_all | solution.py:21
  126.2 0.0 collective-permute-done.3.refs_1_
  126.2 2.3 %shard_map.111 = bf16[32,8,768]{2,1,0:T(8,128)(2,1)} custom-call(f32[256,640]{1,0:T(8,128)} %shard_map.110.refs_0_, f32[256,640]{1,0:T(8,128)} %collective-permute-done.3.refs_1_, f32[32,8,128]{2,1,0:T(8,128)} %all-to-all-done.3.refs_2_), custom_call_target="tpu_custom_call" | custom-call | tf_op jit(solution)/shard_map/pallas_call | solution.py:459
  128.5 5.8 %all-to-all-start.4 = ((bf16[32,8,768]{2,1,0:T(8,128)(2,1)}), bf16[32,8,768]{2,1,0:T(8,128)(2,1)}, u32[]{:S(2)}, u32[]{:S(2)}) async-start(bf16[32,8,768]{2,1,0:T(8,128)(2,1)} %shard_map.111), calls=%async_computation.4 | async-start | bytes 786432 | tf_op jit(solution)/shard_map/all_to_all | solution.py:21
  134.3 2.1 %fusion.refs_2_ = f32[128,1280]{1,0:T(8,128)} fusion(f32[8,1280]{1,0:T(8,128)} %get-tuple-element.31.refs_1_, s32[128]{0:T(128)} %bitcast.17), kind=kOutput, calls=%fused_computation.1 | convolution fusion | flops 15729664 | bytes 696832 | tf_op jit(solution)/shard_map/dot_general | solution.py:573
  136.4 11.9 %all-to-all-done.4 = bf16[32,8,768]{2,1,0:T(8,128)(2,1)} async-done(((bf16[32,8,768]{2,1,0:T(8,128)(2,1)}), bf16[32,8,768]{2,1,0:T(8,128)(2,1)}, u32[]{:S(2)}, u32[]{:S(2)}) %all-to-all-start.4) | async-done | bytes 393248 | tf_op jit(solution)/shard_map/all_to_all | solution.py:21
  148.3 2.3 %shard_map.112 = (f32[128,1280]{1,0:T(8,128)}, f32[8,1280]{1,0:T(8,128)}) custom-call(bf16[16,2,8,768]{3,2,1,0:T(8,128)(2,1)} %bitcast.9.refs_0_, bf16[128,128]{1,0:T(8,128)(2,1)} %get-tuple-element.39.refs_1_, f32[128,1280]{1,0:T(8,128)} %fusion.refs_2_), custom_call_target="tpu_custom_call" | custom-call | tf_op jit(solution)/shard_map/pallas_call | solution.py:459
Async XLA Ops:
  2.8 31.6 %all-to-all-start = ((bf16[32,8,768]{2,1,0:T(8,128)(2,1)}), bf16[32,8,768]{2,1,0:T(8,128)(2,1)S(1)}, u32[]{:S(2)}, u32[]{:S(2)}) async-start(bf16[32,8,768]{2,1,0:T(8,128)(2,1)} %bitcast.12), calls=%async_computation | async-start | bytes 786432 | tf_op jit(solution)/shard_map/all_to_all | solution.py:21
  20.5 6.5 %collective-permute-start = (bf16[8,1280]{1,0:T(8,128)(2,1)}, bf16[8,1280]{1,0:T(8,128)(2,1)}, u32[]{:S(2)}, u32[]{:S(2)}) collective-permute-start(bf16[8,1280]{1,0:T(8,128)(2,1)} %param.15), channel_id=1, source_target_pairs={{0,0},{1,32},{2,64},{3,96},{4,128},{5,160},{6,192},{7,224},{8,256}... | collective-permute-start | bytes 61448 | tf_op jit(solution)/shard_map/ppermute | solution.py:499
  34.4 0.8 copy-start
  35.2 4.9 %collective-permute-start.1 = (bf16[32,8,768]{2,1,0:T(8,128)(2,1)S(1)}, bf16[32,8,768]{2,1,0:T(8,128)(2,1)S(1)}, u32[]{:S(2)}, u32[]{:S(2)}) collective-permute-start(bf16[32,8,768]{2,1,0:T(8,128)(2,1)S(1)} %all-to-all-done.refs_1_), channel_id=1, source_target_pairs={{0,1},{1,0},{2,3},{3,2},{4,5},{5,4},{6,7},{7,6},{8,9},{9,8},{10,11... | collective-permute-start | bytes 1179656 | tf_op jit(solution)/shard_map/ppermute | solution.py:505
  40.0 0.7 copy-start.1
  74.9 9.7 %collective-permute-start.2 = (bf16[32,8,768]{2,1,0:T(8,128)(2,1)}, bf16[32,8,768]{2,1,0:T(8,128)(2,1)}, u32[]{:S(2)}, u32[]{:S(2)}) collective-permute-start(bf16[32,8,768]{2,1,0:T(8,128)(2,1)} %all_to_all.25.refs_0_.refs_1_), channel_id=1, source_target_pairs={{0,1},{1,0},{2,3},{3,2},{4,5},{5,4},{6,7},{7,6},{8,9},{9,8},{10,11... | collective-permute-start | bytes 1179656 | tf_op jit(solution)/shard_map/ppermute | solution.py:528
  80.1 12.6 %all-to-all-start.2 = ((bf16[32,8,128]{2,1,0:T(8,128)(2,1)}), bf16[32,8,128]{2,1,0:T(8,128)(2,1)}, u32[]{:S(2)}, u32[]{:S(2)}) async-start(bf16[32,8,128]{2,1,0:T(8,128)(2,1)} %shard_map.106), calls=%async_computation.2 | async-start | bytes 131072 | tf_op jit(solution)/shard_map/all_to_all | solution.py:21
  103.1 23.1 %collective-permute-start.3 = (f32[256,640]{1,0:T(8,128)}, f32[256,640]{1,0:T(8,128)}, u32[]{:S(2)}, u32[]{:S(2)}) collective-permute-start(f32[256,640]{1,0:T(8,128)} %get-tuple-element.37), channel_id=1, source_target_pairs={{0,1},{1,0},{2,3},{3,2},{4,5},{5,4},{6,7},{7,6},{8,9},{9,8},{10,11... | collective-permute-start | bytes 1966088 | tf_op jit(solution)/shard_map/ppermute | solution.py:557
  105.4 20.8 %all-to-all-start.3 = ((f32[32,8,128]{2,1,0:T(8,128)}), f32[32,8,128]{2,1,0:T(8,128)}, u32[]{:S(2)}, u32[]{:S(2)}) async-start(f32[32,8,128]{2,1,0:T(8,128)} %get-tuple-element.38), calls=%async_computation.3 | async-start | bytes 262144 | tf_op jit(solution)/shard_map/all_to_all | solution.py:21
  128.5 19.8 %all-to-all-start.4 = ((bf16[32,8,768]{2,1,0:T(8,128)(2,1)}), bf16[32,8,768]{2,1,0:T(8,128)(2,1)}, u32[]{:S(2)}, u32[]{:S(2)}) async-start(bf16[32,8,768]{2,1,0:T(8,128)(2,1)} %shard_map.111), calls=%async_computation.4 | async-start | bytes 786432 | tf_op jit(solution)/shard_map/all_to_all | solution.py:21

commit v5 on v3

--- a/solution.py
+++ b/solution.py
@@ -13,9 +13,8 @@
 f32 = jnp.float32
 bf16 = jnp.bfloat16
 LANES = 128
-LOW = 256
 MIB = 1 << 20
-OWN_FLOPS = 10_000_000_000
+COVER = 10_000_000_000
 
 
 def exchange(x, axis):
@@ -336,7 +335,7 @@
         axis=0,
         keepdims=True,
     )
-    out.send(nt(d_preact, up.ready()[pl.ds(other_at, half), :]) + part * router)
+    out.send(nt(d_preact, up.ready()[...]) + part * router)
 
 
 def own_kernel(at_ref, d_preact, up, part, router, out):
@@ -353,7 +352,7 @@
         keepdims=True,
     )
     out.send(
-        nt(d_preact.ready()[...], up.ready()[pl.ds(own_at, half), :])
+        nt(d_preact.ready()[...], up.ready()[...])
         + part.ready()[:, :1] * router
     )
 
@@ -364,38 +363,28 @@
     strip = jnp.sum(terms.ready()[...], axis=0)
     strip_high = strip.astype(bf16).astype(f32)
     side = strip_high + pltpu.roll(strip - strip_high, LANES // 2, 1)
-    pay_ref[:, :, half + LOW :] = jnp.broadcast_to(
+    pay_ref[:, :, half:] = jnp.broadcast_to(
         side.astype(bf16)[None], (n_exp, capacity, LANES)
     )
     total = (own.ready()[...] + other.ready()[...]).reshape(n_exp, capacity, half)
-    high = total.astype(bf16)
-    pay_ref[:, :, :half] = high
-    pay_ref[:, :, half : half + LOW] = (
-        total[:, :, :LOW] - high[:, :, :LOW].astype(f32)
-    ).astype(bf16)
+    pay_ref[:, :, :half] = total.astype(bf16)
 
 
 def final_kernel(strip, back_ref, placed_ref, dy_ref, out_ref, caps_ref):
     n_experts, _, capacity, wide = back_ref.shape
-    half = wide - LOW - LANES
+    half = wide - LANES
     placed = placed_ref[...]
     slots = n_experts * capacity
 
-    def pick(h, start, size):
-        part = back_ref[:, h, :, start : start + size]
-        return nn(placed, part.astype(f32).reshape(slots, size).astype(bf16))
-
     for h in range(2):
-        at = h * half
-        high = pick(h, 0, half)
-        out_ref[:, at : at + LOW] = dy_ref[:, at : at + LOW] + (
-            high[:, :LOW] + pick(h, half, LOW)
+        part = back_ref[:, h, :, :half].astype(f32).reshape(slots, half).astype(bf16)
+        out_ref[:, h * half : (h + 1) * half] = (
+            dy_ref[:, h * half : (h + 1) * half] + nn(placed, part)
         )
-        out_ref[:, at + LOW : at + half] = dy_ref[:, at + LOW : at + half] + high[:, LOW:]
     lane = iota((capacity, LANES), 1)
     strips = []
     for e in range(2 * n_experts):
-        side = back_ref[e // 2, e % 2, :, half + LOW :].astype(f32)
+        side = back_ref[e // 2, e % 2, :, half:].astype(f32)
         strips.append(jnp.where(lane < strip, side + pltpu.roll(side, LANES // 2, 1), 0.0))
     for t, value in enumerate(join_strips(strips, strip, caps_ref.shape[1] // LANES)):
         caps_ref[:, t * LANES : (t + 1) * LANES] = value
@@ -420,7 +409,8 @@
     router_t = w_router.T
     sds = jax.ShapeDtypeStruct
 
-    def run(body, outs, operands, near=(), kept=(), scratch=(), flops=0):
+    def run(body, outs, operands, near=(), kept=(), views=(), scratch=(), flops=0):
+        views = dict(views)
         vmem = pl.BlockSpec(memory_space=pltpu.VMEM)
         hbm = pl.BlockSpec(memory_space=pltpu.HBM)
         late = [i for i, o in enumerate(operands) if o is not at and i not in near]
@@ -434,7 +424,8 @@
             out_bufs, rest = rest[: len(leaving)], rest[len(leaving) :]
             in_sems, out_sems, rest = rest[0], rest[1], rest[2:]
             for k, i in enumerate(late):
-                ins[i] = Late(pltpu.make_async_copy(ins[i], in_bufs[k], in_sems.at[k]), in_bufs[k])
+                source = views[i][1](ins[i], ins[0]) if i in views else ins[i]
+                ins[i] = Late(pltpu.make_async_copy(source, in_bufs[k], in_sems.at[k]), in_bufs[k])
             for k, i in enumerate(leaving):
                 results[i] = Leaving(
                     pltpu.make_async_copy(out_bufs[k], results[i], out_sems.at[k]), out_bufs[k]
@@ -453,7 +444,10 @@
                 for i, o in enumerate(operands)
             ],
             out_specs=[hbm if i in leaving else vmem for i in range(len(outs))],
-            scratch_shapes=[pltpu.VMEM(operands[i].shape, operands[i].dtype) for i in late]
+            scratch_shapes=[
+                pltpu.VMEM(views[i][0] if i in views else operands[i].shape, operands[i].dtype)
+                for i in late
+            ]
             + [pltpu.VMEM(outs[i].shape, outs[i].dtype) for i in leaving]
             + [
                 pltpu.SemaphoreType.DMA((max(len(late), 1),)),
@@ -463,6 +457,12 @@
             compiler_params=pltpu.CompilerParams(vmem_limit_bytes=64 * MIB),
             cost_estimate=pl.CostEstimate(flops=flops, bytes_accessed=0, transcendentals=0),
         )(*operands)
+
+    def up_rows(flip):
+        def cut(ref, at_ref):
+            return ref.at[pl.ds(pl.multiple_of((at_ref[1] ^ flip) * half, LANES), half), :]
+
+        return ((half, hid), cut)
 
     send, base, placed = run(
         functools.partial(pack_kernel, capacity, n_experts, n_clips),
@@ -499,8 +499,9 @@
     (total,) = run(
         functools.partial(sum_kernel, strip),
         [sds((n_exp, n_clips, LANES), bf16)],
-        [sums[:, :, half:]],
+        [sums],
         kept=(0,),
+        views={0: ((n_exp, caps_dp, LANES), lambda ref, _: ref.at[:, :, pl.ds(half, LANES)])},
     )
     total = exchange(total, "expert")
     other_sums = lax.ppermute(sums, "expert", swap)
@@ -516,6 +517,7 @@
         functools.partial(backward_kernel, n_clips),
         [sds((rows, hid), bf16), sds((rows, half), f32), sds((rows, LANES), f32)],
         [at, clip_grad, aux, w_down, gelu_slope, hidden, router_t, w_up],
+        views={7: up_rows(1)},
         scratch=[pltpu.VMEM((rows + 2 * n_clips, width), bf16)],
     )
     from_other = lax.ppermute(dx_other, "expert", swap)
@@ -523,11 +525,12 @@
         own_kernel,
         [sds((rows, half), f32)],
         [at, d_preact, w_up, part, router_t],
-        flops=OWN_FLOPS,
+        views={2: up_rows(0)},
+        flops=COVER,
     )
     (pay,) = run(
         return_kernel,
-        [sds((n_exp, capacity, half + LOW + LANES), bf16)],
+        [sds((n_exp, capacity, half + LANES), bf16)],
         [dx_own, from_other, terms],
         kept=(0,),
     )
@@ -537,7 +540,7 @@
     token_grads, caption_grads = run(
         functools.partial(final_kernel, strip),
         [sds((tok_rows, width), f32), sds((caps_dp, width), f32)],
-        [back.reshape(n_experts, 2, capacity, half + LOW + LANES), placed, token_dy],
+        [back.reshape(n_experts, 2, capacity, half + LANES), placed, token_dy],
         near=(0, 1, 2),
         kept=(0, 1),
     )

time: 149 us -> 143 us (0.960)
  waiting for transfers between devices: 27.4 us -> 24.5 us
    all_to_all x3, waiting for transfers between devices: 22.2 us -> 19.3 us  [exchange(): return lax.all_to_all(x, axis, split_axis=0, concat_axis=0, tiled=True)]
  transfers between devices with their start and end apart: 7 -> 7, of which waited for: 4 -> 4; matrix products, arithmetic and copies ran while one was open for 3% -> 2% of each run, Pallas kernels for 9% -> 8%
where the time goes in v5:
time: 143 us
  starting transfers between devices  43.2 us (30%)
  blocking collectives  39.4 us (28%)
  Pallas kernels  30.4 us (21%)
  waiting for transfers between devices  24.5 us (17%)
  matrix products  2.1 us (1%)
  local copies, waits for them, and re-layouts  1.48 us (1%)
    all_to_all x2, blocking collectives, exchange(): return lax.all_to_all(x, axis, split_axis=0, concat_axis=0, tiled=True)  39.4 us
    all_to_all x3, starting transfers between devices, exchange(): return lax.all_to_all(x, axis, split_axis=0, concat_axis=0, tiled=True)  31.6 us
    pallas_call x8, Pallas kernels, run(): pl.pallas_call(kernel, out_shape=outs, in_specs=[pl.BlockSpec(memory_spac...  30.4 us
    all_to_all x3, waiting for transfers between devices, exchange(): return lax.all_to_all(x, axis, split_axis=0, concat_axis=0, tiled=True)  19.3 us
    ppermute x1, waiting for transfers between devices, shards(): lax.ppermute(start, ('dp', 'expert'), [(a * n_exp + b, b * n_exp + a if b...  4.58 us
    ppermute x1, starting transfers between devices, shards(): other_sums = lax.ppermute(sums, 'expert', swap)  3.59 us
    ppermute x1, starting transfers between devices, shards(): other = lax.ppermute(recv, 'expert', swap)  3.54 us
  transfers between devices with their start and end apart: 7, of which 4 were waited for; matrix products, arithmetic and copies ran while one was open for 2% of the time, Pallas kernels for 8%

profile of v5, /device:TPU:1, one launch (start us, length us, event | category | flops | bytes accessed | tf_op | source)
XLA Modules:
  0.0 142.5 jit_solution(6537991274016115232)
XLA Ops:
  0.6 2.1 %shard_map.104 = (bf16[16,2,8,768]{3,2,1,0:T(8,128)(2,1)}, f32[8,1280]{1,0:T(8,128)}, bf16[128,128]{1,0:T(8,128)(2,1)}) custom-call(s32[1,128]{1,0:T(1,128)} %bitcast.19, s32[1,128]{1,0:T(1,128)} %refs_1_.1, bf16[128,1280]{1,0:T(8,128)(2,1)} %refs_2_.2), custom_call_target="tpu_custom_call" | custom-call | tf_op jit(solution)/shard_map/pallas_call | solution.py:439
  2.8 17.7 %all-to-all-start = ((bf16[32,8,768]{2,1,0:T(8,128)(2,1)}), bf16[32,8,768]{2,1,0:T(8,128)(2,1)S(1)}, u32[]{:S(2)}, u32[]{:S(2)}) async-start(bf16[32,8,768]{2,1,0:T(8,128)(2,1)} %bitcast.12), calls=%async_computation | async-start | bytes 786432 | tf_op jit(solution)/shard_map/all_to_all | solution.py:21
  20.5 1.9 %collective-permute-start = (bf16[8,1280]{1,0:T(8,128)(2,1)}, bf16[8,1280]{1,0:T(8,128)(2,1)}, u32[]{:S(2)}, u32[]{:S(2)}) collective-permute-start(bf16[8,1280]{1,0:T(8,128)(2,1)} %param.15), channel_id=1, source_target_pairs={{0,0},{1,32},{2,64},{3,96},{4,128},{5,160},{6,192},{7,224},{8,256}... | collective-permute-start | bytes 61448 | tf_op jit(solution)/shard_map/ppermute | solution.py:479
  22.4 4.6 %collective-permute-done.refs_5_ = bf16[8,1280]{1,0:T(8,128)(2,1)} collective-permute-done((bf16[8,1280]{1,0:T(8,128)(2,1)}, bf16[8,1280]{1,0:T(8,128)(2,1)}, u32[]{:S(2)}, u32[]{:S(2)}) %collective-permute-start) | collective-permute-done | bytes 20512 | tf_op jit(solution)/shard_map/ppermute | solution.py:479
  27.0 7.4 %all-to-all-done.refs_1_ = bf16[32,8,768]{2,1,0:T(8,128)(2,1)S(1)} async-done(((bf16[32,8,768]{2,1,0:T(8,128)(2,1)}), bf16[32,8,768]{2,1,0:T(8,128)(2,1)S(1)}, u32[]{:S(2)}, u32[]{:S(2)}) %all-to-all-start) | async-done | bytes 393248 | tf_op jit(solution)/shard_map/all_to_all | solution.py:21
  34.4 0.0 copy-start
  34.4 0.7 copy-done
  35.1 3.5 %collective-permute-start.1 = (bf16[32,8,768]{2,1,0:T(8,128)(2,1)S(1)}, bf16[32,8,768]{2,1,0:T(8,128)(2,1)S(1)}, u32[]{:S(2)}, u32[]{:S(2)}) collective-permute-start(bf16[32,8,768]{2,1,0:T(8,128)(2,1)S(1)} %all-to-all-done.refs_1_), channel_id=1, source_target_pairs={{0,1},{1,0},{2,3},{3,2},{4,5},{5,4},{6,7},{7,6},{8,9},{9,8},{10,11... | collective-permute-start | bytes 1179656 | tf_op jit(solution)/shard_map/ppermute | solution.py:485
  38.7 0.7 pad_add_fusion.refs_0_
  39.4 0.6 collective-permute-done.1.refs_2_
  40.0 0.0 copy-start.1
  40.0 0.7 copy-done.1
  40.7 7.2 %shard_map.105 = (f32[256,1280]{1,0:T(8,128)}, bf16[256,1280]{1,0:T(8,128)(2,1)}, f32[256,128]{1,0:T(8,128)}, f32[8,128]{1,0:T(8,128)}, bf16[16,2,8,768]{3,2,1,0:T(8,128)(2,1)}) custom-call(s32[4]{0:T(128)} %pad_add_fusion.refs_0_, bf16[32,8,768]{2,1,0:T(8,128)(2,1)} %copy-done, bf16[32,8,768]{2,1,0:T(8,128)(2,1)} %copy-done.1, bf16[16,1280]{1,0:T(8,128)(2,1)} %bitcast.14, ...), custom_call_target="tpu_custom_call" | custom-call | tf_op jit(solution)/shard_map/pallas_call | solution.py:439
  47.9 26.7 %all_to_all.25.refs_0_.refs_3_ = bf16[32,8,768]{2,1,0:T(8,128)(2,1)} all-to-all(bf16[32,8,768]{2,1,0:T(8,128)(2,1)} %bitcast.13), channel_id=1, replica_groups=mesh['dp'=32,'expert'=32] {'expert'}, dimensions={0} | all-to-all | bytes 786432 | tf_op jit(solution)/shard_map/all_to_all | solution.py:21
  74.7 3.6 %collective-permute-start.2 = (bf16[32,8,768]{2,1,0:T(8,128)(2,1)}, bf16[32,8,768]{2,1,0:T(8,128)(2,1)}, u32[]{:S(2)}, u32[]{:S(2)}) collective-permute-start(bf16[32,8,768]{2,1,0:T(8,128)(2,1)} %all_to_all.25.refs_0_.refs_3_), channel_id=1, source_target_pairs={{0,1},{1,0},{2,3},{3,2},{4,5},{5,4},{6,7},{7,6},{8,9},{9,8},{10,11... | collective-permute-start | bytes 1179656 | tf_op jit(solution)/shard_map/ppermute | solution.py:507
  78.3 1.7 %shard_map.106 = bf16[32,8,128]{2,1,0:T(8,128)(2,1)} custom-call(bf16[32,8,768]{2,1,0:T(8,128)(2,1)} %all_to_all.25.refs_0_.refs_3_), custom_call_target="tpu_custom_call" | custom-call | tf_op jit(solution)/shard_map/pallas_call | solution.py:439
  79.9 12.6 %all_to_all.26.refs_1_ = bf16[32,8,128]{2,1,0:T(8,128)(2,1)} all-to-all(bf16[32,8,128]{2,1,0:T(8,128)(2,1)} %shard_map.106), channel_id=1, replica_groups=mesh['dp'=32,'expert'=32] {'expert'}, dimensions={0} | all-to-all | bytes 131072 | tf_op jit(solution)/shard_map/all_to_all | solution.py:21
  92.6 0.0 collective-permute-done.2.refs_4_
  92.6 4.4 %shard_map.107 = (f32[8,1280]{1,0:T(8,128)}, f32[32,8,128]{2,1,0:T(8,128)}) custom-call(s32[4]{0:T(128)} %pad_add_fusion.refs_0_, bf16[32,8,128]{2,1,0:T(8,128)(2,1)} %all_to_all.26.refs_1_, f32[8,128]{1,0:T(8,128)} %get-tuple-element.24.refs_2_, bf16[32,8,768]{2,1,0:T(8,128)(2,1)} %all_to_all.25.refs_0_.refs_3_, ...), custom_call_target="tpu_custom_call" | custom-call | tf_op jit(solution)/shard_map/pallas_call | solution.py:439
  97.0 9.5 %all-to-all-start.3 = ((f32[32,8,128]{2,1,0:T(8,128)}), f32[32,8,128]{2,1,0:T(8,128)}, u32[]{:S(2)}, u32[]{:S(2)}) async-start(f32[32,8,128]{2,1,0:T(8,128)} %get-tuple-element.32), calls=%async_computation.3 | async-start | bytes 262144 | tf_op jit(solution)/shard_map/all_to_all | solution.py:21
  106.5 6.4 %shard_map.108 = (bf16[256,1280]{1,0:T(8,128)(2,1)}, f32[256,640]{1,0:T(8,128)}, f32[256,128]{1,0:T(8,128)}) custom-call(s32[4]{0:T(128)} %pad_add_fusion.refs_0_, f32[8,1280]{1,0:T(8,128)} %get-tuple-element.25.refs_1_, f32[256,128]{1,0:T(8,128)} %get-tuple-element.26.refs_2_, bf16[1280,1280]{1,0:T(8,128)(2,1)} %refs_3_.1, ...), custom_call_target="tpu_custom_call" | custom-call | tf_op jit(solution)/shard_map/pallas_call | solution.py:439
  112.9 2.6 %collective-permute-start.3 = (f32[256,640]{1,0:T(8,128)}, f32[256,640]{1,0:T(8,128)}, u32[]{:S(2)}, u32[]{:S(2)}) collective-permute-start(f32[256,640]{1,0:T(8,128)} %get-tuple-element.31), channel_id=1, source_target_pairs={{0,1},{1,0},{2,3},{3,2},{4,5},{5,4},{6,7},{7,6},{8,9},{9,8},{10,11... | collective-permute-start | bytes 1966088 | tf_op jit(solution)/shard_map/ppermute | solution.py:523
  115.5 4.0 %shard_map.109.refs_0_ = f32[256,640]{1,0:T(8,128)} custom-call(s32[4]{0:T(128)} %pad_add_fusion.refs_0_, bf16[256,1280]{1,0:T(8,128)(2,1)} %get-tuple-element.29.refs_1_, bf16[1280,1280]{1,0:T(8,128)(2,1)} %refs_2_.3, f32[256,128]{1,0:T(8,128)} %get-tuple-element.30.refs_3_, bf16[16,1280]{1,0:T(8,128)(2,1)} %bitcast.16), custom_call_target="tpu_custom_call" | custom-call | flops 10000000000 | tf_op jit(solution)/shard_map/pallas_call | solution.py:439
  119.5 0.0 all-to-all-done.3.refs_2_
  119.5 0.0 collective-permute-done.3.refs_1_
  119.5 2.3 %shard_map.110 = bf16[32,8,768]{2,1,0:T(8,128)(2,1)} custom-call(f32[256,640]{1,0:T(8,128)} %shard_map.109.refs_0_, f32[256,640]{1,0:T(8,128)} %collective-permute-done.3.refs_1_, f32[32,8,128]{2,1,0:T(8,128)} %all-to-all-done.3.refs_2_), custom_call_target="tpu_custom_call" | custom-call | tf_op jit(solution)/shard_map/pallas_call | solution.py:439
  121.8 4.4 %all-to-all-start.4 = ((bf16[32,8,768]{2,1,0:T(8,128)(2,1)}), bf16[32,8,768]{2,1,0:T(8,128)(2,1)}, u32[]{:S(2)}, u32[]{:S(2)}) async-start(bf16[32,8,768]{2,1,0:T(8,128)(2,1)} %shard_map.110), calls=%async_computation.4 | async-start | bytes 786432 | tf_op jit(solution)/shard_map/all_to_all | solution.py:21
  126.2 2.1 %fusion.refs_2_ = f32[128,1280]{1,0:T(8,128)} fusion(f32[8,1280]{1,0:T(8,128)} %get-tuple-element.25.refs_1_, s32[128]{0:T(128)} %bitcast.17), kind=kOutput, calls=%fused_computation.1 | convolution fusion | flops 15729664 | bytes 696832 | tf_op jit(solution)/shard_map/dot_general | solution.py:539
  128.3 11.9 %all-to-all-done.4 = bf16[32,8,768]{2,1,0:T(8,128)(2,1)} async-done(((bf16[32,8,768]{2,1,0:T(8,128)(2,1)}), bf16[32,8,768]{2,1,0:T(8,128)(2,1)}, u32[]{:S(2)}, u32[]{:S(2)}) %all-to-all-start.4) | async-done | bytes 393248 | tf_op jit(solution)/shard_map/all_to_all | solution.py:21
  140.2 2.3 %shard_map.111 = (f32[128,1280]{1,0:T(8,128)}, f32[8,1280]{1,0:T(8,128)}) custom-call(bf16[16,2,8,768]{3,2,1,0:T(8,128)(2,1)} %bitcast.9.refs_0_, bf16[128,128]{1,0:T(8,128)(2,1)} %get-tuple-element.33.refs_1_, f32[128,1280]{1,0:T(8,128)} %fusion.refs_2_), custom_call_target="tpu_custom_call" | custom-call | tf_op jit(solution)/shard_map/pallas_call | solution.py:439
Async XLA Ops:
  2.8 31.6 %all-to-all-start = ((bf16[32,8,768]{2,1,0:T(8,128)(2,1)}), bf16[32,8,768]{2,1,0:T(8,128)(2,1)S(1)}, u32[]{:S(2)}, u32[]{:S(2)}) async-start(bf16[32,8,768]{2,1,0:T(8,128)(2,1)} %bitcast.12), calls=%async_computation | async-start | bytes 786432 | tf_op jit(solution)/shard_map/all_to_all | solution.py:21
  20.5 6.5 %collective-permute-start = (bf16[8,1280]{1,0:T(8,128)(2,1)}, bf16[8,1280]{1,0:T(8,128)(2,1)}, u32[]{:S(2)}, u32[]{:S(2)}) collective-permute-start(bf16[8,1280]{1,0:T(8,128)(2,1)} %param.15), channel_id=1, source_target_pairs={{0,0},{1,32},{2,64},{3,96},{4,128},{5,160},{6,192},{7,224},{8,256}... | collective-permute-start | bytes 61448 | tf_op jit(solution)/shard_map/ppermute | solution.py:479
  34.4 0.7 copy-start
  35.1 4.9 %collective-permute-start.1 = (bf16[32,8,768]{2,1,0:T(8,128)(2,1)S(1)}, bf16[32,8,768]{2,1,0:T(8,128)(2,1)S(1)}, u32[]{:S(2)}, u32[]{:S(2)}) collective-permute-start(bf16[32,8,768]{2,1,0:T(8,128)(2,1)S(1)} %all-to-all-done.refs_1_), channel_id=1, source_target_pairs={{0,1},{1,0},{2,3},{3,2},{4,5},{5,4},{6,7},{7,6},{8,9},{9,8},{10,11... | collective-permute-start | bytes 1179656 | tf_op jit(solution)/shard_map/ppermute | solution.py:485
  40.0 0.7 copy-start.1
  74.7 17.9 %collective-permute-start.2 = (bf16[32,8,768]{2,1,0:T(8,128)(2,1)}, bf16[32,8,768]{2,1,0:T(8,128)(2,1)}, u32[]{:S(2)}, u32[]{:S(2)}) collective-permute-start(bf16[32,8,768]{2,1,0:T(8,128)(2,1)} %all_to_all.25.refs_0_.refs_3_), channel_id=1, source_target_pairs={{0,1},{1,0},{2,3},{3,2},{4,5},{5,4},{6,7},{7,6},{8,9},{9,8},{10,11... | collective-permute-start | bytes 1179656 | tf_op jit(solution)/shard_map/ppermute | solution.py:507
  97.0 22.5 %all-to-all-start.3 = ((f32[32,8,128]{2,1,0:T(8,128)}), f32[32,8,128]{2,1,0:T(8,128)}, u32[]{:S(2)}, u32[]{:S(2)}) async-start(f32[32,8,128]{2,1,0:T(8,128)} %get-tuple-element.32), calls=%async_computation.3 | async-start | bytes 262144 | tf_op jit(solution)/shard_map/all_to_all | solution.py:21
  112.9 6.6 %collective-permute-start.3 = (f32[256,640]{1,0:T(8,128)}, f32[256,640]{1,0:T(8,128)}, u32[]{:S(2)}, u32[]{:S(2)}) collective-permute-start(f32[256,640]{1,0:T(8,128)} %get-tuple-element.31), channel_id=1, source_target_pairs={{0,1},{1,0},{2,3},{3,2},{4,5},{5,4},{6,7},{7,6},{8,9},{9,8},{10,11... | collective-permute-start | bytes 1966088 | tf_op jit(solution)/shard_map/ppermute | solution.py:523
  121.8 18.4 %all-to-all-start.4 = ((bf16[32,8,768]{2,1,0:T(8,128)(2,1)}), bf16[32,8,768]{2,1,0:T(8,128)(2,1)}, u32[]{:S(2)}, u32[]{:S(2)}) async-start(bf16[32,8,768]{2,1,0:T(8,128)(2,1)} %shard_map.110), calls=%async_computation.4 | async-start | bytes 786432 | tf_op jit(solution)/shard_map/all_to_all | solution.py:21

commit v6 on v5

--- a/solution.py
+++ b/solution.py
@@ -142,8 +142,15 @@
     return jnp.where(lane < strip, value + (mid + low), 0.0)
 
 
+def first_kernel(at_ref, recv, up, out):
+    n_exp, capacity, half = recv.ref.shape
+    own = recv.ready()[...].astype(f32).reshape(n_exp * capacity, half).astype(bf16)
+    out.send(nn(own, up.ready()[...]))
+
+
 def forward_kernel(
-    n_clips, strip, at_ref, recv, other, router, up, block, down, base, slope, hidden_out, aux_out, counts, pay_ref,
+    n_clips, strip, at_ref, recv, other, router, up, partial, block, down, base,
+    slope, hidden_out, aux_out, counts, pay_ref,
 ):
     n_exp, capacity, wide = recv.ref.shape
     half = wide - LANES
@@ -181,10 +188,7 @@
         )
     )
     weights = (clip * gate).T[:n_clips].astype(bf16)
-    up_ref = up.ready()
-    preact = nn(own, up_ref[pl.ds(own_at, half), :]) + nn(
-        other_rows, up_ref[pl.ds(other_at, half), :]
-    )
+    preact = nn(other_rows, up.ready()[...]) + partial.ready()[...]
     root = 0.7978845608028654
     square = preact * preact
     tanh = jnp.tanh(root * (preact + 0.044715 * (square * preact)))
@@ -483,6 +487,16 @@
     )
     recv, block = lax.optimization_barrier((recv, block))
     other = lax.ppermute(recv, "expert", swap)
+    (partial,) = run(
+        first_kernel,
+        [sds((rows, hid), f32)],
+        [at, recv, w_up],
+        views={
+            1: ((n_exp, capacity, half), lambda ref, _: ref.at[:, :, pl.ds(0, half)]),
+            2: up_rows(0),
+        },
+        flops=2 * rows * half * hid,
+    )
     gelu_slope, hidden, aux, counts, pay = run(
         functools.partial(forward_kernel, n_clips, strip),
         [
@@ -492,8 +506,9 @@
             sds((n_clips, LANES), f32),
             sds((n_exp // 2, 2, caps_dp, half + LANES), bf16),
         ],
-        [at, recv, other, router_t, w_up, block, w_down, base],
+        [at, recv, other, router_t, w_up, partial, block, w_down, base],
         kept=(4,),
+        views={4: up_rows(1)},
     )
     sums = exchange(pay.reshape(n_exp, caps_dp, half + LANES), "expert")
     (total,) = run(

time: 143 us -> 144 us (level)
  Pallas kernels: 30.4 us -> 33.7 us
  local copies, waits for them, and re-layouts: 1.48 us -> 0 us
    pallas_call x8 -> x9, Pallas kernels: 30.4 us -> 33.7 us  [run(): pl.pallas_call(kernel, out_shape=outs, in_specs=[pl.BlockSpec(memory_spac...]
    unnamed x4 -> x0, local copies, waits for them, and re-layouts: 1.48 us -> none
  transfers between devices with their start and end apart: 7 -> 7, of which waited for: 4 -> 3; matrix products, arithmetic and copies ran while one was open for 2% -> 2% of each run, Pallas kernels for 8% -> 11%
where the time goes in v6:
time: 144 us; the launch traced here: 143 us
  starting transfers between devices  43.4 us (30%)
  blocking collectives  39 us (27%)
  Pallas kernels  33.7 us (23%)
  waiting for transfers between devices  23.9 us (17%)
  matrix products  2.1 us (1%)
    all_to_all x2, blocking collectives, exchange(): return lax.all_to_all(x, axis, split_axis=0, concat_axis=0, tiled=True)  39 us
    pallas_call x9, Pallas kernels, run(): pl.pallas_call(kernel, out_shape=outs, in_specs=[pl.BlockSpec(memory_spac...  33.7 us
    all_to_all x3, starting transfers between devices, exchange(): return lax.all_to_all(x, axis, split_axis=0, concat_axis=0, tiled=True)  31.6 us
    all_to_all x3, waiting for transfers between devices, exchange(): return lax.all_to_all(x, axis, split_axis=0, concat_axis=0, tiled=True)  19.2 us
    ppermute x1, waiting for transfers between devices, shards(): lax.ppermute(start, ('dp', 'expert'), [(a * n_exp + b, b * n_exp + a if b...  4.68 us
    ppermute x1, starting transfers between devices, shards(): other = lax.ppermute(recv, 'expert', swap)  3.66 us
    ppermute x1, starting transfers between devices, shards(): other_sums = lax.ppermute(sums, 'expert', swap)  3.59 us
  transfers between devices with their start and end apart: 7, of which 3 were waited for; matrix products, arithmetic and copies ran while one was open for 2% of the time, Pallas kernels for 11%

profile of v6, /device:TPU:1, one launch (start us, length us, event | category | flops | bytes accessed | tf_op | source)
XLA Modules:
  0.0 143.5 jit_solution(16289765310824663536)
XLA Ops:
  0.6 2.1 %shard_map.104 = (bf16[16,2,8,768]{3,2,1,0:T(8,128)(2,1)}, f32[8,1280]{1,0:T(8,128)}, bf16[128,128]{1,0:T(8,128)(2,1)}) custom-call(s32[1,128]{1,0:T(1,128)} %bitcast.19, s32[1,128]{1,0:T(1,128)} %refs_1_.1, bf16[128,1280]{1,0:T(8,128)(2,1)} %refs_2_.3), custom_call_target="tpu_custom_call" | custom-call | tf_op jit(solution)/shard_map/pallas_call | solution.py:443
  2.8 18.3 %all-to-all-start = ((bf16[32,8,768]{2,1,0:T(8,128)(2,1)}), bf16[32,8,768]{2,1,0:T(8,128)(2,1)}, u32[]{:S(2)}, u32[]{:S(2)}) async-start(bf16[32,8,768]{2,1,0:T(8,128)(2,1)} %bitcast.12), calls=%async_computation | async-start | bytes 786432 | tf_op jit(solution)/shard_map/all_to_all | solution.py:21
  21.1 1.9 %collective-permute-start = (bf16[8,1280]{1,0:T(8,128)(2,1)}, bf16[8,1280]{1,0:T(8,128)(2,1)}, u32[]{:S(2)}, u32[]{:S(2)}) collective-permute-start(bf16[8,1280]{1,0:T(8,128)(2,1)} %param.15), channel_id=1, source_target_pairs={{0,0},{1,32},{2,64},{3,96},{4,128},{5,160},{6,192},{7,224},{8,256}... | collective-permute-start | bytes 61448 | tf_op jit(solution)/shard_map/ppermute | solution.py:483
  23.1 4.7 %collective-permute-done.refs_6_ = bf16[8,1280]{1,0:T(8,128)(2,1)} collective-permute-done((bf16[8,1280]{1,0:T(8,128)(2,1)}, bf16[8,1280]{1,0:T(8,128)(2,1)}, u32[]{:S(2)}, u32[]{:S(2)}) %collective-permute-start) | collective-permute-done | bytes 20512 | tf_op jit(solution)/shard_map/ppermute | solution.py:483
  27.7 7.3 %all-to-all-done.refs_1_ = bf16[32,8,768]{2,1,0:T(8,128)(2,1)} async-done(((bf16[32,8,768]{2,1,0:T(8,128)(2,1)}), bf16[32,8,768]{2,1,0:T(8,128)(2,1)}, u32[]{:S(2)}, u32[]{:S(2)}) %all-to-all-start) | async-done | bytes 393248 | tf_op jit(solution)/shard_map/all_to_all | solution.py:21
  35.1 3.7 %collective-permute-start.1 = (bf16[32,8,768]{2,1,0:T(8,128)(2,1)}, bf16[32,8,768]{2,1,0:T(8,128)(2,1)}, u32[]{:S(2)}, u32[]{:S(2)}) collective-permute-start(bf16[32,8,768]{2,1,0:T(8,128)(2,1)} %all-to-all-done.refs_1_), channel_id=1, source_target_pairs={{0,1},{1,0},{2,3},{3,2},{4,5},{5,4},{6,7},{7,6},{8,9},{9,8},{10,11... | collective-permute-start | bytes 1179656 | tf_op jit(solution)/shard_map/ppermute | solution.py:489
  38.8 0.6 pad_add_fusion.refs_0_
  39.4 4.0 %shard_map.105.refs_5_ = f32[256,1280]{1,0:T(8,128)} custom-call(s32[4]{0:T(128)} %pad_add_fusion.refs_0_, bf16[32,8,768]{2,1,0:T(8,128)(2,1)} %all-to-all-done.refs_1_, bf16[1280,1280]{1,0:T(8,128)(2,1)} %refs_2_.5), custom_call_target="tpu_custom_call" | custom-call | flops 419430400 | tf_op jit(solution)/shard_map/pallas_call | solution.py:443
  43.3 0.0 collective-permute-done.1.refs_2_
  43.3 6.6 %shard_map.106 = (f32[256,1280]{1,0:T(8,128)}, bf16[256,1280]{1,0:T(8,128)(2,1)}, f32[256,128]{1,0:T(8,128)}, f32[8,128]{1,0:T(8,128)}, bf16[16,2,8,768]{3,2,1,0:T(8,128)(2,1)}) custom-call(s32[4]{0:T(128)} %pad_add_fusion.refs_0_, bf16[32,8,768]{2,1,0:T(8,128)(2,1)} %all-to-all-done.refs_1_, bf16[32,8,768]{2,1,0:T(8,128)(2,1)} %collective-permute-done.1.refs_2_, ...), custom_call_target="tpu_custom_call" | custom-call | tf_op jit(solution)/shard_map/pallas_call | solution.py:443
  49.9 26.4 %all_to_all.25.refs_0_.refs_3_ = bf16[32,8,768]{2,1,0:T(8,128)(2,1)} all-to-all(bf16[32,8,768]{2,1,0:T(8,128)(2,1)} %bitcast.13), channel_id=1, replica_groups=mesh['dp'=32,'expert'=32] {'expert'}, dimensions={0} | all-to-all | bytes 786432 | tf_op jit(solution)/shard_map/all_to_all | solution.py:21
  76.3 3.6 %collective-permute-start.2 = (bf16[32,8,768]{2,1,0:T(8,128)(2,1)}, bf16[32,8,768]{2,1,0:T(8,128)(2,1)}, u32[]{:S(2)}, u32[]{:S(2)}) collective-permute-start(bf16[32,8,768]{2,1,0:T(8,128)(2,1)} %all_to_all.25.refs_0_.refs_3_), channel_id=1, source_target_pairs={{0,1},{1,0},{2,3},{3,2},{4,5},{5,4},{6,7},{7,6},{8,9},{9,8},{10,11... | collective-permute-start | bytes 1179656 | tf_op jit(solution)/shard_map/ppermute | solution.py:522
  79.9 1.7 %shard_map.107 = bf16[32,8,128]{2,1,0:T(8,128)(2,1)} custom-call(bf16[32,8,768]{2,1,0:T(8,128)(2,1)} %all_to_all.25.refs_0_.refs_3_), custom_call_target="tpu_custom_call" | custom-call | tf_op jit(solution)/shard_map/pallas_call | solution.py:443
  81.5 12.6 %all_to_all.26.refs_1_ = bf16[32,8,128]{2,1,0:T(8,128)(2,1)} all-to-all(bf16[32,8,128]{2,1,0:T(8,128)(2,1)} %shard_map.107), channel_id=1, replica_groups=mesh['dp'=32,'expert'=32] {'expert'}, dimensions={0} | all-to-all | bytes 131072 | tf_op jit(solution)/shard_map/all_to_all | solution.py:21
  94.2 0.0 collective-permute-done.2.refs_4_
  94.2 4.4 %shard_map.108 = (f32[8,1280]{1,0:T(8,128)}, f32[32,8,128]{2,1,0:T(8,128)}) custom-call(s32[4]{0:T(128)} %pad_add_fusion.refs_0_, bf16[32,8,128]{2,1,0:T(8,128)(2,1)} %all_to_all.26.refs_1_, f32[8,128]{1,0:T(8,128)} %get-tuple-element.24.refs_2_, bf16[32,8,768]{2,1,0:T(8,128)(2,1)} %all_to_all.25.refs_0_.refs_3_, ...), custom_call_target="tpu_custom_call" | custom-call | tf_op jit(solution)/shard_map/pallas_call | solution.py:443
  98.6 8.8 %all-to-all-start.3 = ((f32[32,8,128]{2,1,0:T(8,128)}), f32[32,8,128]{2,1,0:T(8,128)}, u32[]{:S(2)}, u32[]{:S(2)}) async-start(f32[32,8,128]{2,1,0:T(8,128)} %get-tuple-element.32), calls=%async_computation.3 | async-start | bytes 262144 | tf_op jit(solution)/shard_map/all_to_all | solution.py:21
  107.4 6.4 %shard_map.109 = (bf16[256,1280]{1,0:T(8,128)(2,1)}, f32[256,640]{1,0:T(8,128)}, f32[256,128]{1,0:T(8,128)}) custom-call(s32[4]{0:T(128)} %pad_add_fusion.refs_0_, f32[8,1280]{1,0:T(8,128)} %get-tuple-element.25.refs_1_, f32[256,128]{1,0:T(8,128)} %get-tuple-element.26.refs_2_, bf16[1280,1280]{1,0:T(8,128)(2,1)} %refs_3_.1, ...), custom_call_target="tpu_custom_call" | custom-call | tf_op jit(solution)/shard_map/pallas_call | solution.py:443
  113.8 2.6 %collective-permute-start.3 = (f32[256,640]{1,0:T(8,128)}, f32[256,640]{1,0:T(8,128)}, u32[]{:S(2)}, u32[]{:S(2)}) collective-permute-start(f32[256,640]{1,0:T(8,128)} %get-tuple-element.31), channel_id=1, source_target_pairs={{0,1},{1,0},{2,3},{3,2},{4,5},{5,4},{6,7},{7,6},{8,9},{9,8},{10,11... | collective-permute-start | bytes 1966088 | tf_op jit(solution)/shard_map/ppermute | solution.py:538
  116.4 4.0 %shard_map.110.refs_0_ = f32[256,640]{1,0:T(8,128)} custom-call(s32[4]{0:T(128)} %pad_add_fusion.refs_0_, bf16[256,1280]{1,0:T(8,128)(2,1)} %get-tuple-element.29.refs_1_, bf16[1280,1280]{1,0:T(8,128)(2,1)} %refs_2_.5, f32[256,128]{1,0:T(8,128)} %get-tuple-element.30.refs_3_, bf16[16,1280]{1,0:T(8,128)(2,1)} %bitcast.16), custom_call_target="tpu_custom_call" | custom-call | flops 10000000000 | tf_op jit(solution)/shard_map/pallas_call | solution.py:443
  120.4 0.0 all-to-all-done.3.refs_2_
  120.4 0.0 collective-permute-done.3.refs_1_
  120.4 2.3 %shard_map.111 = bf16[32,8,768]{2,1,0:T(8,128)(2,1)} custom-call(f32[256,640]{1,0:T(8,128)} %shard_map.110.refs_0_, f32[256,640]{1,0:T(8,128)} %collective-permute-done.3.refs_1_, f32[32,8,128]{2,1,0:T(8,128)} %all-to-all-done.3.refs_2_), custom_call_target="tpu_custom_call" | custom-call | tf_op jit(solution)/shard_map/pallas_call | solution.py:443
  122.7 4.5 %all-to-all-start.4 = ((bf16[32,8,768]{2,1,0:T(8,128)(2,1)}), bf16[32,8,768]{2,1,0:T(8,128)(2,1)}, u32[]{:S(2)}, u32[]{:S(2)}) async-start(bf16[32,8,768]{2,1,0:T(8,128)(2,1)} %shard_map.111), calls=%async_computation.4 | async-start | bytes 786432 | tf_op jit(solution)/shard_map/all_to_all | solution.py:21
  127.2 2.1 %fusion.refs_2_ = f32[128,1280]{1,0:T(8,128)} fusion(f32[8,1280]{1,0:T(8,128)} %get-tuple-element.25.refs_1_, s32[128]{0:T(128)} %bitcast.17), kind=kOutput, calls=%fused_computation.1 | convolution fusion | flops 15729664 | bytes 696832 | tf_op jit(solution)/shard_map/dot_general | solution.py:554
  129.3 11.9 %all-to-all-done.4 = bf16[32,8,768]{2,1,0:T(8,128)(2,1)} async-done(((bf16[32,8,768]{2,1,0:T(8,128)(2,1)}), bf16[32,8,768]{2,1,0:T(8,128)(2,1)}, u32[]{:S(2)}, u32[]{:S(2)}) %all-to-all-start.4) | async-done | bytes 393248 | tf_op jit(solution)/shard_map/all_to_all | solution.py:21
  141.1 2.3 %shard_map.112 = (f32[128,1280]{1,0:T(8,128)}, f32[8,1280]{1,0:T(8,128)}) custom-call(bf16[16,2,8,768]{3,2,1,0:T(8,128)(2,1)} %bitcast.9.refs_0_, bf16[128,128]{1,0:T(8,128)(2,1)} %get-tuple-element.33.refs_1_, f32[128,1280]{1,0:T(8,128)} %fusion.refs_2_), custom_call_target="tpu_custom_call" | custom-call | tf_op jit(solution)/shard_map/pallas_call | solution.py:443
Async XLA Ops:
  2.8 32.3 %all-to-all-start = ((bf16[32,8,768]{2,1,0:T(8,128)(2,1)}), bf16[32,8,768]{2,1,0:T(8,128)(2,1)}, u32[]{:S(2)}, u32[]{:S(2)}) async-start(bf16[32,8,768]{2,1,0:T(8,128)(2,1)} %bitcast.12), calls=%async_computation | async-start | bytes 786432 | tf_op jit(solution)/shard_map/all_to_all | solution.py:21
  21.1 6.6 %collective-permute-start = (bf16[8,1280]{1,0:T(8,128)(2,1)}, bf16[8,1280]{1,0:T(8,128)(2,1)}, u32[]{:S(2)}, u32[]{:S(2)}) collective-permute-start(bf16[8,1280]{1,0:T(8,128)(2,1)} %param.15), channel_id=1, source_target_pairs={{0,0},{1,32},{2,64},{3,96},{4,128},{5,160},{6,192},{7,224},{8,256}... | collective-permute-start | bytes 61448 | tf_op jit(solution)/shard_map/ppermute | solution.py:483
  35.1 8.3 %collective-permute-start.1 = (bf16[32,8,768]{2,1,0:T(8,128)(2,1)}, bf16[32,8,768]{2,1,0:T(8,128)(2,1)}, u32[]{:S(2)}, u32[]{:S(2)}) collective-permute-start(bf16[32,8,768]{2,1,0:T(8,128)(2,1)} %all-to-all-done.refs_1_), channel_id=1, source_target_pairs={{0,1},{1,0},{2,3},{3,2},{4,5},{5,4},{6,7},{7,6},{8,9},{9,8},{10,11... | collective-permute-start | bytes 1179656 | tf_op jit(solution)/shard_map/ppermute | solution.py:489
  76.3 17.9 %collective-permute-start.2 = (bf16[32,8,768]{2,1,0:T(8,128)(2,1)}, bf16[32,8,768]{2,1,0:T(8,128)(2,1)}, u32[]{:S(2)}, u32[]{:S(2)}) collective-permute-start(bf16[32,8,768]{2,1,0:T(8,128)(2,1)} %all_to_all.25.refs_0_.refs_3_), channel_id=1, source_target_pairs={{0,1},{1,0},{2,3},{3,2},{4,5},{5,4},{6,7},{7,6},{8,9},{9,8},{10,11... | collective-permute-start | bytes 1179656 | tf_op jit(solution)/shard_map/ppermute | solution.py:522
  98.6 21.8 %all-to-all-start.3 = ((f32[32,8,128]{2,1,0:T(8,128)}), f32[32,8,128]{2,1,0:T(8,128)}, u32[]{:S(2)}, u32[]{:S(2)}) async-start(f32[32,8,128]{2,1,0:T(8,128)} %get-tuple-element.32), calls=%async_computation.3 | async-start | bytes 262144 | tf_op jit(solution)/shard_map/all_to_all | solution.py:21
  113.8 6.6 %collective-permute-start.3 = (f32[256,640]{1,0:T(8,128)}, f32[256,640]{1,0:T(8,128)}, u32[]{:S(2)}, u32[]{:S(2)}) collective-permute-start(f32[256,640]{1,0:T(8,128)} %get-tuple-element.31), channel_id=1, source_target_pairs={{0,1},{1,0},{2,3},{3,2},{4,5},{5,4},{6,7},{7,6},{8,9},{9,8},{10,11... | collective-permute-start | bytes 1966088 | tf_op jit(solution)/shard_map/ppermute | solution.py:538
  122.7 18.4 %all-to-all-start.4 = ((bf16[32,8,768]{2,1,0:T(8,128)(2,1)}), bf16[32,8,768]{2,1,0:T(8,128)(2,1)}, u32[]{:S(2)}, u32[]{:S(2)}) async-start(bf16[32,8,768]{2,1,0:T(8,128)(2,1)} %shard_map.111), calls=%async_computation.4 | async-start | bytes 786432 | tf_op jit(solution)/shard_map/all_to_all | solution.py:21

commit v7 on v5

--- a/solution.py
+++ b/solution.py
@@ -143,7 +143,8 @@
 
 
 def forward_kernel(
-    n_clips, strip, at_ref, recv, other, router, up, block, down, base, slope, hidden_out, aux_out, counts, pay_ref,
+    n_clips, strip, at_ref, recv, other, router, up0, down0, up1, down1, block, base,
+    slope, hidden_out, aux_out, counts, pay_ref,
 ):
     n_exp, capacity, wide = recv.ref.shape
     half = wide - LANES
@@ -181,25 +182,30 @@
         )
     )
     weights = (clip * gate).T[:n_clips].astype(bf16)
-    up_ref = up.ready()
-    preact = nn(own, up_ref[pl.ds(own_at, half), :]) + nn(
-        other_rows, up_ref[pl.ds(other_at, half), :]
-    )
     root = 0.7978845608028654
-    square = preact * preact
-    tanh = jnp.tanh(root * (preact + 0.044715 * (square * preact)))
-    hidden = (preact * (0.5 * (1.0 + tanh))).astype(bf16)
-    hidden_out.send(hidden)
-    slope.send(
-        0.5 * (1.0 + tanh)
-        + 0.5 * preact * (1.0 - tanh * tanh) * (root * (1.0 + (3 * 0.044715) * square))
-    )
+    produced = None
+    part = up0.ref.shape[1]
+    for c, (up, down) in enumerate(((up0, down0), (up1, down1))):
+        up_ref = up.ready()
+        preact = nn(own, up_ref[pl.ds(own_at, half), :]) + nn(
+            other_rows, up_ref[pl.ds(other_at, half), :]
+        )
+        square = preact * preact
+        tanh = jnp.tanh(root * (preact + 0.044715 * (square * preact)))
+        hidden = (preact * (0.5 * (1.0 + tanh))).astype(bf16)
+        hidden_out.ref[:, c * part : (c + 1) * part] = hidden
+        slope.ref[:, c * part : (c + 1) * part] = 0.5 * (1.0 + tanh) + 0.5 * preact * (
+            1.0 - tanh * tanh
+        ) * (root * (1.0 + (3 * 0.044715) * square))
+        more = nn(hidden, down.ready()[...])
+        produced = more if produced is None else produced + more
+    hidden_out.copy.start()
+    slope.copy.start()
     captions = block.ready()
     for h in range(2):
         pay_ref[:, h, :, :half] = jnp.broadcast_to(
             captions[:, h * half : (h + 1) * half][None], (n_exp // 2, captions.shape[0], half)
         )
-    produced = nn(hidden, down.ready()[...])
     high = produced.astype(bf16)
     low = (produced - high.astype(f32)).astype(bf16)
     pooled = base.ready()[...] + (nn(weights, high) + nn(weights, low))
@@ -492,8 +498,17 @@
             sds((n_clips, LANES), f32),
             sds((n_exp // 2, 2, caps_dp, half + LANES), bf16),
         ],
-        [at, recv, other, router_t, w_up, block, w_down, base],
+        [at, recv, other, router_t, w_up, w_down, w_up, w_down, block, base],
         kept=(4,),
+        views={
+            i: (
+                (width, hid // 2) if i % 2 == 0 else (hid // 2, width),
+                lambda ref, _, i=i: ref.at[:, pl.ds((i - 4) // 2 * (hid // 2), hid // 2)]
+                if i % 2 == 0
+                else ref.at[pl.ds((i - 4) // 2 * (hid // 2), hid // 2), :],
+            )
+            for i in (4, 5, 6, 7)
+        },
     )
     sums = exchange(pay.reshape(n_exp, caps_dp, half + LANES), "expert")
     (total,) = run(

time: 143 us -> 144 us (level)
  no operation moved by 1% of the time
where the time goes in v7:
time: 144 us; the launch traced here: 143 us
  starting transfers between devices  43.2 us (30%)
  blocking collectives  39.4 us (27%)
  Pallas kernels  30.9 us (21%)
  waiting for transfers between devices  24.5 us (17%)
  matrix products  2.1 us (1%)
  local copies, waits for them, and re-layouts  1.48 us (1%)
    all_to_all x2, blocking collectives, exchange(): return lax.all_to_all(x, axis, split_axis=0, concat_axis=0, tiled=True)  39.4 us
    all_to_all x3, starting transfers between devices, exchange(): return lax.all_to_all(x, axis, split_axis=0, concat_axis=0, tiled=True)  31.6 us
    pallas_call x8, Pallas kernels, run(): pl.pallas_call(kernel, out_shape=outs, in_specs=[pl.BlockSpec(memory_spac...  30.9 us
    all_to_all x3, waiting for transfers between devices, exchange(): return lax.all_to_all(x, axis, split_axis=0, concat_axis=0, tiled=True)  19.3 us
    ppermute x1, waiting for transfers between devices, shards(): lax.ppermute(start, ('dp', 'expert'), [(a * n_exp + b, b * n_exp + a if b...  4.58 us
    ppermute x1, starting transfers between devices, shards(): other_sums = lax.ppermute(sums, 'expert', swap)  3.59 us
    ppermute x1, starting transfers between devices, shards(): other = lax.ppermute(recv, 'expert', swap)  3.54 us
  transfers between devices with their start and end apart: 7, of which 4 were waited for; matrix products, arithmetic and copies ran while one was open for 2% of the time, Pallas kernels for 8%

profile of v7, /device:TPU:1, one launch (start us, length us, event | category | flops | bytes accessed | tf_op | source)
XLA Modules:
  0.0 143.0 jit_solution(17507156681655580898)
XLA Ops:
  0.6 2.1 %shard_map.104 = (bf16[16,2,8,768]{3,2,1,0:T(8,128)(2,1)}, f32[8,1280]{1,0:T(8,128)}, bf16[128,128]{1,0:T(8,128)(2,1)}) custom-call(s32[1,128]{1,0:T(1,128)} %bitcast.19, s32[1,128]{1,0:T(1,128)} %refs_1_.1, bf16[128,1280]{1,0:T(8,128)(2,1)} %refs_2_.2), custom_call_target="tpu_custom_call" | custom-call | tf_op jit(solution)/shard_map/pallas_call | solution.py:445
  2.8 17.7 %all-to-all-start = ((bf16[32,8,768]{2,1,0:T(8,128)(2,1)}), bf16[32,8,768]{2,1,0:T(8,128)(2,1)S(1)}, u32[]{:S(2)}, u32[]{:S(2)}) async-start(bf16[32,8,768]{2,1,0:T(8,128)(2,1)} %bitcast.12), calls=%async_computation | async-start | bytes 786432 | tf_op jit(solution)/shard_map/all_to_all | solution.py:21
  20.5 1.9 %collective-permute-start = (bf16[8,1280]{1,0:T(8,128)(2,1)}, bf16[8,1280]{1,0:T(8,128)(2,1)}, u32[]{:S(2)}, u32[]{:S(2)}) collective-permute-start(bf16[8,1280]{1,0:T(8,128)(2,1)} %param.15), channel_id=1, source_target_pairs={{0,0},{1,32},{2,64},{3,96},{4,128},{5,160},{6,192},{7,224},{8,256}... | collective-permute-start | bytes 61448 | tf_op jit(solution)/shard_map/ppermute | solution.py:485
  22.4 4.6 %collective-permute-done.refs_8_ = bf16[8,1280]{1,0:T(8,128)(2,1)} collective-permute-done((bf16[8,1280]{1,0:T(8,128)(2,1)}, bf16[8,1280]{1,0:T(8,128)(2,1)}, u32[]{:S(2)}, u32[]{:S(2)}) %collective-permute-start) | collective-permute-done | bytes 20512 | tf_op jit(solution)/shard_map/ppermute | solution.py:485
  27.0 7.4 %all-to-all-done.refs_1_ = bf16[32,8,768]{2,1,0:T(8,128)(2,1)S(1)} async-done(((bf16[32,8,768]{2,1,0:T(8,128)(2,1)}), bf16[32,8,768]{2,1,0:T(8,128)(2,1)S(1)}, u32[]{:S(2)}, u32[]{:S(2)}) %all-to-all-start) | async-done | bytes 393248 | tf_op jit(solution)/shard_map/all_to_all | solution.py:21
  34.4 0.0 copy-start
  34.4 0.7 copy-done
  35.1 3.5 %collective-permute-start.1 = (bf16[32,8,768]{2,1,0:T(8,128)(2,1)S(1)}, bf16[32,8,768]{2,1,0:T(8,128)(2,1)S(1)}, u32[]{:S(2)}, u32[]{:S(2)}) collective-permute-start(bf16[32,8,768]{2,1,0:T(8,128)(2,1)S(1)} %all-to-all-done.refs_1_), channel_id=1, source_target_pairs={{0,1},{1,0},{2,3},{3,2},{4,5},{5,4},{6,7},{7,6},{8,9},{9,8},{10,11... | collective-permute-start | bytes 1179656 | tf_op jit(solution)/shard_map/ppermute | solution.py:491
  38.7 0.7 pad_add_fusion.refs_0_
  39.4 0.6 collective-permute-done.1.refs_2_
  40.0 0.0 copy-start.1
  40.0 0.7 copy-done.1
  40.7 7.7 %shard_map.105 = (f32[256,1280]{1,0:T(8,128)}, bf16[256,1280]{1,0:T(8,128)(2,1)}, f32[256,128]{1,0:T(8,128)}, f32[8,128]{1,0:T(8,128)}, bf16[16,2,8,768]{3,2,1,0:T(8,128)(2,1)}) custom-call(s32[4]{0:T(128)} %pad_add_fusion.refs_0_, bf16[32,8,768]{2,1,0:T(8,128)(2,1)} %copy-done, bf16[32,8,768]{2,1,0:T(8,128)(2,1)} %copy-done.1, bf16[16,1280]{1,0:T(8,128)(2,1)} %bitcast.14, ...), custom_call_target="tpu_custom_call" | custom-call | tf_op jit(solution)/shard_map/pallas_call | solution.py:445
  48.4 26.7 %all_to_all.25.refs_0_.refs_3_ = bf16[32,8,768]{2,1,0:T(8,128)(2,1)} all-to-all(bf16[32,8,768]{2,1,0:T(8,128)(2,1)} %bitcast.13), channel_id=1, replica_groups=mesh['dp'=32,'expert'=32] {'expert'}, dimensions={0} | all-to-all | bytes 786432 | tf_op jit(solution)/shard_map/all_to_all | solution.py:21
  75.1 3.6 %collective-permute-start.2 = (bf16[32,8,768]{2,1,0:T(8,128)(2,1)}, bf16[32,8,768]{2,1,0:T(8,128)(2,1)}, u32[]{:S(2)}, u32[]{:S(2)}) collective-permute-start(bf16[32,8,768]{2,1,0:T(8,128)(2,1)} %all_to_all.25.refs_0_.refs_3_), channel_id=1, source_target_pairs={{0,1},{1,0},{2,3},{3,2},{4,5},{5,4},{6,7},{7,6},{8,9},{9,8},{10,11... | collective-permute-start | bytes 1179656 | tf_op jit(solution)/shard_map/ppermute | solution.py:522
  78.7 1.7 %shard_map.106 = bf16[32,8,128]{2,1,0:T(8,128)(2,1)} custom-call(bf16[32,8,768]{2,1,0:T(8,128)(2,1)} %all_to_all.25.refs_0_.refs_3_), custom_call_target="tpu_custom_call" | custom-call | tf_op jit(solution)/shard_map/pallas_call | solution.py:445
  80.4 12.6 %all_to_all.26.refs_1_ = bf16[32,8,128]{2,1,0:T(8,128)(2,1)} all-to-all(bf16[32,8,128]{2,1,0:T(8,128)(2,1)} %shard_map.106), channel_id=1, replica_groups=mesh['dp'=32,'expert'=32] {'expert'}, dimensions={0} | all-to-all | bytes 131072 | tf_op jit(solution)/shard_map/all_to_all | solution.py:21
  93.0 0.0 collective-permute-done.2.refs_4_
  93.0 4.4 %shard_map.107 = (f32[8,1280]{1,0:T(8,128)}, f32[32,8,128]{2,1,0:T(8,128)}) custom-call(s32[4]{0:T(128)} %pad_add_fusion.refs_0_, bf16[32,8,128]{2,1,0:T(8,128)(2,1)} %all_to_all.26.refs_1_, f32[8,128]{1,0:T(8,128)} %get-tuple-element.24.refs_2_, bf16[32,8,768]{2,1,0:T(8,128)(2,1)} %all_to_all.25.refs_0_.refs_3_, ...), custom_call_target="tpu_custom_call" | custom-call | tf_op jit(solution)/shard_map/pallas_call | solution.py:445
  97.5 9.5 %all-to-all-start.3 = ((f32[32,8,128]{2,1,0:T(8,128)}), f32[32,8,128]{2,1,0:T(8,128)}, u32[]{:S(2)}, u32[]{:S(2)}) async-start(f32[32,8,128]{2,1,0:T(8,128)} %get-tuple-element.32), calls=%async_computation.3 | async-start | bytes 262144 | tf_op jit(solution)/shard_map/all_to_all | solution.py:21
  106.9 6.4 %shard_map.108 = (bf16[256,1280]{1,0:T(8,128)(2,1)}, f32[256,640]{1,0:T(8,128)}, f32[256,128]{1,0:T(8,128)}) custom-call(s32[4]{0:T(128)} %pad_add_fusion.refs_0_, f32[8,1280]{1,0:T(8,128)} %get-tuple-element.25.refs_1_, f32[256,128]{1,0:T(8,128)} %get-tuple-element.26.refs_2_, bf16[1280,1280]{1,0:T(8,128)(2,1)} %refs_3_.1, ...), custom_call_target="tpu_custom_call" | custom-call | tf_op jit(solution)/shard_map/pallas_call | solution.py:445
  113.3 2.6 %collective-permute-start.3 = (f32[256,640]{1,0:T(8,128)}, f32[256,640]{1,0:T(8,128)}, u32[]{:S(2)}, u32[]{:S(2)}) collective-permute-start(f32[256,640]{1,0:T(8,128)} %get-tuple-element.31), channel_id=1, source_target_pairs={{0,1},{1,0},{2,3},{3,2},{4,5},{5,4},{6,7},{7,6},{8,9},{9,8},{10,11... | collective-permute-start | bytes 1966088 | tf_op jit(solution)/shard_map/ppermute | solution.py:538
  115.9 4.0 %shard_map.109.refs_0_ = f32[256,640]{1,0:T(8,128)} custom-call(s32[4]{0:T(128)} %pad_add_fusion.refs_0_, bf16[256,1280]{1,0:T(8,128)(2,1)} %get-tuple-element.29.refs_1_, bf16[1280,1280]{1,0:T(8,128)(2,1)} %refs_2_.3, f32[256,128]{1,0:T(8,128)} %get-tuple-element.30.refs_3_, bf16[16,1280]{1,0:T(8,128)(2,1)} %bitcast.16), custom_call_target="tpu_custom_call" | custom-call | flops 10000000000 | tf_op jit(solution)/shard_map/pallas_call | solution.py:445
  119.9 0.0 all-to-all-done.3.refs_2_
  120.0 0.0 collective-permute-done.3.refs_1_
  120.0 2.3 %shard_map.110 = bf16[32,8,768]{2,1,0:T(8,128)(2,1)} custom-call(f32[256,640]{1,0:T(8,128)} %shard_map.109.refs_0_, f32[256,640]{1,0:T(8,128)} %collective-permute-done.3.refs_1_, f32[32,8,128]{2,1,0:T(8,128)} %all-to-all-done.3.refs_2_), custom_call_target="tpu_custom_call" | custom-call | tf_op jit(solution)/shard_map/pallas_call | solution.py:445
  122.3 4.4 %all-to-all-start.4 = ((bf16[32,8,768]{2,1,0:T(8,128)(2,1)}), bf16[32,8,768]{2,1,0:T(8,128)(2,1)}, u32[]{:S(2)}, u32[]{:S(2)}) async-start(bf16[32,8,768]{2,1,0:T(8,128)(2,1)} %shard_map.110), calls=%async_computation.4 | async-start | bytes 786432 | tf_op jit(solution)/shard_map/all_to_all | solution.py:21
  126.7 2.1 %fusion.refs_2_ = f32[128,1280]{1,0:T(8,128)} fusion(f32[8,1280]{1,0:T(8,128)} %get-tuple-element.25.refs_1_, s32[128]{0:T(128)} %bitcast.17), kind=kOutput, calls=%fused_computation.1 | convolution fusion | flops 15729664 | bytes 696832 | tf_op jit(solution)/shard_map/dot_general | solution.py:554
  128.8 11.9 %all-to-all-done.4 = bf16[32,8,768]{2,1,0:T(8,128)(2,1)} async-done(((bf16[32,8,768]{2,1,0:T(8,128)(2,1)}), bf16[32,8,768]{2,1,0:T(8,128)(2,1)}, u32[]{:S(2)}, u32[]{:S(2)}) %all-to-all-start.4) | async-done | bytes 393248 | tf_op jit(solution)/shard_map/all_to_all | solution.py:21
  140.7 2.3 %shard_map.111 = (f32[128,1280]{1,0:T(8,128)}, f32[8,1280]{1,0:T(8,128)}) custom-call(bf16[16,2,8,768]{3,2,1,0:T(8,128)(2,1)} %bitcast.9.refs_0_, bf16[128,128]{1,0:T(8,128)(2,1)} %get-tuple-element.33.refs_1_, f32[128,1280]{1,0:T(8,128)} %fusion.refs_2_), custom_call_target="tpu_custom_call" | custom-call | tf_op jit(solution)/shard_map/pallas_call | solution.py:445
Async XLA Ops:
  2.8 31.6 %all-to-all-start = ((bf16[32,8,768]{2,1,0:T(8,128)(2,1)}), bf16[32,8,768]{2,1,0:T(8,128)(2,1)S(1)}, u32[]{:S(2)}, u32[]{:S(2)}) async-start(bf16[32,8,768]{2,1,0:T(8,128)(2,1)} %bitcast.12), calls=%async_computation | async-start | bytes 786432 | tf_op jit(solution)/shard_map/all_to_all | solution.py:21
  20.5 6.5 %collective-permute-start = (bf16[8,1280]{1,0:T(8,128)(2,1)}, bf16[8,1280]{1,0:T(8,128)(2,1)}, u32[]{:S(2)}, u32[]{:S(2)}) collective-permute-start(bf16[8,1280]{1,0:T(8,128)(2,1)} %param.15), channel_id=1, source_target_pairs={{0,0},{1,32},{2,64},{3,96},{4,128},{5,160},{6,192},{7,224},{8,256}... | collective-permute-start | bytes 61448 | tf_op jit(solution)/shard_map/ppermute | solution.py:485
  34.4 0.7 copy-start
  35.1 4.9 %collective-permute-start.1 = (bf16[32,8,768]{2,1,0:T(8,128)(2,1)S(1)}, bf16[32,8,768]{2,1,0:T(8,128)(2,1)S(1)}, u32[]{:S(2)}, u32[]{:S(2)}) collective-permute-start(bf16[32,8,768]{2,1,0:T(8,128)(2,1)S(1)} %all-to-all-done.refs_1_), channel_id=1, source_target_pairs={{0,1},{1,0},{2,3},{3,2},{4,5},{5,4},{6,7},{7,6},{8,9},{9,8},{10,11... | collective-permute-start | bytes 1179656 | tf_op jit(solution)/shard_map/ppermute | solution.py:491
  40.0 0.7 copy-start.1
  75.1 17.9 %collective-permute-start.2 = (bf16[32,8,768]{2,1,0:T(8,128)(2,1)}, bf16[32,8,768]{2,1,0:T(8,128)(2,1)}, u32[]{:S(2)}, u32[]{:S(2)}) collective-permute-start(bf16[32,8,768]{2,1,0:T(8,128)(2,1)} %all_to_all.25.refs_0_.refs_3_), channel_id=1, source_target_pairs={{0,1},{1,0},{2,3},{3,2},{4,5},{5,4},{6,7},{7,6},{8,9},{9,8},{10,11... | collective-permute-start | bytes 1179656 | tf_op jit(solution)/shard_map/ppermute | solution.py:522
  97.5 22.5 %all-to-all-start.3 = ((f32[32,8,128]{2,1,0:T(8,128)}), f32[32,8,128]{2,1,0:T(8,128)}, u32[]{:S(2)}, u32[]{:S(2)}) async-start(f32[32,8,128]{2,1,0:T(8,128)} %get-tuple-element.32), calls=%async_computation.3 | async-start | bytes 262144 | tf_op jit(solution)/shard_map/all_to_all | solution.py:21
  113.3 6.6 %collective-permute-start.3 = (f32[256,640]{1,0:T(8,128)}, f32[256,640]{1,0:T(8,128)}, u32[]{:S(2)}, u32[]{:S(2)}) collective-permute-start(f32[256,640]{1,0:T(8,128)} %get-tuple-element.31), channel_id=1, source_target_pairs={{0,1},{1,0},{2,3},{3,2},{4,5},{5,4},{6,7},{7,6},{8,9},{9,8},{10,11... | collective-permute-start | bytes 1966088 | tf_op jit(solution)/shard_map/ppermute | solution.py:538
  122.3 18.4 %all-to-all-start.4 = ((bf16[32,8,768]{2,1,0:T(8,128)(2,1)}), bf16[32,8,768]{2,1,0:T(8,128)(2,1)}, u32[]{:S(2)}, u32[]{:S(2)}) async-start(bf16[32,8,768]{2,1,0:T(8,128)(2,1)} %shard_map.110), calls=%async_computation.4 | async-start | bytes 786432 | tf_op jit(solution)/shard_map/all_to_all | solution.py:21
